TPU v7x, 128 devices: a whole 4x4x4 slice. The times are simulated.
128 devices in a mesh: shard: 2 (over y_hi), ctx: 16 (over y_lo, z, core), tp: 4 (over x).
Axes of the slice: x: 4, y: 4 (y_hi: 2, y_lo: 2; y = y_hi * 2 + y_lo), z: 4, core: 2. Of those that a mesh axis runs over, the one named last changes fastest.
Arguments:
- hidden: bfloat16 [4, 4096, 1536], P('shard', 'ctx'), may hold values from -6 to 6
- lengths: int32 [4], P('shard'), may hold values from 1024 to 4096, as said below
- cotangent: bfloat16 [4, 4096, 1536], P('shard', 'ctx'), may hold values from -11 to 11
- in_weight: float32 [3, 1536, 1536], P(None, ('shard', 'ctx'), 'tp'), may hold values from -0.15625 to 0.15625
- in_moment: float32 [3, 1536, 1536], P(None, ('shard', 'ctx'), 'tp'), may hold values from -224 to 224
- in_average: float32 [3, 1536, 1536], P(None, ('shard', 'ctx'), 'tp'), may hold values from -0.15625 to 0.15625
- out_weight: float32 [1536, 1536], P('tp', ('shard', 'ctx')), may hold values from -0.15625 to 0.15625
- out_moment: float32 [1536, 1536], P('tp', ('shard', 'ctx')), may hold values from -224 to 224
- out_average: float32 [1536, 1536], P('tp', ('shard', 'ctx')), may hold values from -0.15625 to 0.15625
- gate_up_weight: float32 [2, 1536, 6912], P(None, ('shard', 'ctx'), 'tp'), may hold values from -0.15625 to 0.15625
- gate_up_moment: float32 [2, 1536, 6912], P(None, ('shard', 'ctx'), 'tp'), may hold values from -224 to 224
- gate_up_average: float32 [2, 1536, 6912], P(None, ('shard', 'ctx'), 'tp'), may hold values from -0.15625 to 0.15625
- down_weight: float32 [6912, 1536], P('tp', ('shard', 'ctx')), may hold values from -0.109375 to 0.109375
- down_moment: float32 [6912, 1536], P('tp', ('shard', 'ctx')), may hold values from -224 to 224
- down_average: float32 [6912, 1536], P('tp', ('shard', 'ctx')), may hold values from -0.109375 to 0.109375
- norm_gains: float32 [2, 1536], replicated, may hold values from 0.5 to 1.5
- gain_moment: float32 [2, 1536], replicated, may hold values from -224 to 224
- gain_average: float32 [2, 1536], replicated, may hold values from 0.5 to 1.5
- conv_taps: float32 [3, 1536], P(None, 'tp'), may hold values from -3.5 to 3.5
- taps_moment: float32 [3, 1536], P(None, 'tp'), may hold values from -224 to 224
- taps_average: float32 [3, 1536], P(None, 'tp'), may hold values from -3.5 to 3.5
Outputs:
- block_output: bfloat16 [4, 4096, 1536], P('shard', 'ctx')
- input_grad: float32 [4, 4096, 1536], P('shard', 'ctx')
- in_moment_new: float32 [3, 1536, 1536], P(None, ('shard', 'ctx'), 'tp')
- in_weight_new: float32 [3, 1536, 1536], P(None, ('shard', 'ctx'), 'tp')
- in_average_new: float32 [3, 1536, 1536], P(None, ('shard', 'ctx'), 'tp')
- out_moment_new: float32 [1536, 1536], P('tp', ('shard', 'ctx'))
- out_weight_new: float32 [1536, 1536], P('tp', ('shard', 'ctx'))
- out_average_new: float32 [1536, 1536], P('tp', ('shard', 'ctx'))
- gate_up_moment_new: float32 [2, 1536, 6912], P(None, ('shard', 'ctx'), 'tp')
- gate_up_weight_new: float32 [2, 1536, 6912], P(None, ('shard', 'ctx'), 'tp')
- gate_up_average_new: float32 [2, 1536, 6912], P(None, ('shard', 'ctx'), 'tp')
- down_moment_new: float32 [6912, 1536], P('tp', ('shard', 'ctx'))
- down_weight_new: float32 [6912, 1536], P('tp', ('shard', 'ctx'))
- down_average_new: float32 [6912, 1536], P('tp', ('shard', 'ctx'))
- gain_moment_new: float32 [2, 1536], replicated
- gains_new: float32 [2, 1536], replicated
- gain_average_new: float32 [2, 1536], replicated
- taps_moment_new: float32 [3, 1536], P(None, 'tp')
- taps_new: float32 [3, 1536], P(None, 'tp')
- taps_average_new: float32 [3, 1536], P(None, 'tp')
Inputs may be any that keep to these rules, and one draw needn't show every extreme that they name: `lengths`: in each aligned group of 2 slots one slot is used to its end.
All inputs are finite; a program needn't handle non-finite values.
Results may differ from a plain program's by a relative error of at most 0.012.
Values may be sent and summed in bfloat16 or wider, within the bound.
A program may use at most 256 MiB of HBM per device.

v0:
```python
import jax
import jax.numpy as jnp
from jax import lax
from jax.sharding import PartitionSpec as P

epsilon = 1e-05
momentum = 0.9
average_decay = 0.9
matrix_rate = 0.0004
small_rate = 0.005


def rows_first(arrays, axis, dims):
    turned = [jnp.moveaxis(a, dim, 0) for a, dim in zip(arrays, dims)]
    both = jnp.concatenate([t.reshape(len(t), -1) for t in turned], axis=1)
    whole, at, outs = (lax.all_gather(both, axis, axis=0, tiled=True), 0, [])
    for t, dim in zip(turned, dims):
        piece = whole[:, at : at + t[0].size].reshape(-1, *t.shape[1:])
        outs.append(jnp.moveaxis(piece, 0, dim))
        at += t[0].size
    return tuple(outs)


def from_behind(value, axis, steps):
    count = lax.axis_size(axis)
    leading, last = (max(0, -steps), min(count, count - steps))
    return lax.ppermute(value, axis, [(source, source + steps) for source in range(leading, last)])


def from_everyone(array, axis):
    copies = jnp.broadcast_to(array, (lax.axis_size(axis), *array.shape))
    return lax.all_to_all(copies, axis, split_axis=0, concat_axis=0, tiled=True)


def taken_together(array, axis):
    everything = from_everyone(array, axis)
    return jnp.sum(everything, axis=0)


def together(arrays, axis):
    flat, at, outs = (jnp.concatenate([a.reshape(-1) for a in arrays]), 0, [])
    total = taken_together(flat, axis)
    for a in arrays:
        outs.append(total[at : at + a.size].reshape(a.shape))
        at += a.size
    return tuple(outs)


def normalize(values):
    inverse = lax.rsqrt(jnp.mean(values * values, axis=-1, keepdims=True) + epsilon)
    return (values * inverse, inverse)


def norm_back(grad_normed, normed, inverse, gain_row):
    scaled = grad_normed * gain_row
    return inverse * (scaled - normed * jnp.mean(scaled * normed, axis=-1, keepdims=True))


def contract_rows(left_side, right_side):
    return lax.dot_general(
        left_side, right_side, (((0,), (0,)), ((), ())), preferred_element_type=jnp.float32
    )


def contract_cols(left_side, right_side):
    return lax.dot_general(
        left_side, right_side, (((1,), (1,)), ((), ())), preferred_element_type=jnp.float32
    )


def nesterov(weight, moment, average, gradient, step_rate):
    moment_new = momentum * moment + gradient
    weight_new = weight - step_rate * (gradient + momentum * moment_new)
    average_new = average_decay * average + (1.0 - average_decay) * weight_new
    return (moment_new, weight_new, average_new)


def on_device(
    hidden,
    lengths,
    cotangent,
    in_weight,
    in_moment,
    in_average,
    out_weight,
    out_moment,
    out_average,
    gate_up_weight,
    gate_up_moment,
    gate_up_average,
    down_weight,
    down_moment,
    down_average,
    norm_gains,
    gain_moment,
    gain_average,
    conv_taps,
    taps_moment,
    taps_average,
):
    in_low = in_weight.astype(jnp.bfloat16)
    out_low = out_weight.astype(jnp.bfloat16)
    gate_up_low = gate_up_weight.astype(jnp.bfloat16)
    down_low = down_weight.astype(jnp.bfloat16)
    in_full, out_full, gate_up_full, down_full = rows_first(
        (in_low, out_low, gate_up_low, down_low), ("shard", "ctx"), (1, 1, 1, 1)
    )
    slot_count, seq_len, model_width = hidden.shape
    row_count = slot_count * seq_len
    stream = hidden.astype(jnp.float32).reshape(row_count, model_width)
    positions = lax.axis_index("ctx") * seq_len + jnp.arange(seq_len, dtype=jnp.int32)
    valid_rows = (positions[None, :] < lengths[:, None]).astype(jnp.float32).reshape(row_count, 1)
    normed_one, inverse_one = normalize(stream)
    input_low = (normed_one * norm_gains[0]).astype(jnp.bfloat16)
    projected = jnp.einsum("rd,kde->kre", input_low, in_full, preferred_element_type=jnp.float32)
    channels = projected.shape[2]
    product = (projected[0] * projected[2]).reshape(slot_count, seq_len, channels)
    previous = from_behind(product[:, seq_len - 2 :, :], "ctx", 1)
    extended = jnp.concatenate([previous, product], axis=1)
    convolved = (
        conv_taps[0] * extended[:, :seq_len]
        + conv_taps[1] * extended[:, 1 : seq_len + 1]
        + conv_taps[2] * extended[:, 2:]
    ).reshape(row_count, channels)
    gated_low = (projected[1] * convolved).astype(jnp.bfloat16)
    mixed_sum = lax.psum(jnp.dot(gated_low, out_full, preferred_element_type=jnp.float32), "tp")
    residual = stream + mixed_sum
    normed_two, inverse_two = normalize(residual)
    second_low = (normed_two * norm_gains[1]).astype(jnp.bfloat16)
    gate_up = jnp.einsum(
        "rd,kdf->krf", second_low, gate_up_full, preferred_element_type=jnp.float32
    )
    sigmoid_gate = jax.nn.sigmoid(gate_up[0])
    activated = gate_up[0] * sigmoid_gate
    inner_low = (activated * gate_up[1]).astype(jnp.bfloat16)
    branch = lax.psum(jnp.dot(inner_low, down_full, preferred_element_type=jnp.float32), "tp")
    block_output = (
        (residual + branch).astype(jnp.bfloat16).reshape(slot_count, seq_len, model_width)
    )
    grad_out = cotangent.astype(jnp.float32).reshape(row_count, model_width) * valid_rows
    grad_low = grad_out.astype(jnp.bfloat16)
    grad_inner = contract_cols(grad_low, down_full)
    down_grad = contract_rows(inner_low, grad_low)
    grad_gate = grad_inner * gate_up[1] * sigmoid_gate * (1.0 + gate_up[0] * (1.0 - sigmoid_gate))
    grad_up = grad_inner * activated
    grad_gate_up = jnp.stack([grad_gate, grad_up]).astype(jnp.bfloat16)
    gate_up_grad = jnp.einsum(
        "rd,krf->kdf", second_low, grad_gate_up, preferred_element_type=jnp.float32
    )
    grad_second = lax.psum(
        jnp.einsum("krf,kdf->rd", grad_gate_up, gate_up_full, preferred_element_type=jnp.float32),
        "tp",
    )
    gain_two = jnp.sum(grad_second * normed_two, axis=0)
    grad_residual = grad_out + norm_back(grad_second, normed_two, inverse_two, norm_gains[1])
    residual_low = grad_residual.astype(jnp.bfloat16)
    grad_gated = contract_cols(residual_low, out_full)
    out_grad = contract_rows(gated_low, residual_low)
    grad_cproj = grad_gated * convolved
    grad_conv = (grad_gated * projected[1]).reshape(slot_count, seq_len, channels)
    following = from_behind(grad_conv[:, :2, :], "ctx", -1)
    grad_extended = jnp.concatenate([grad_conv, following], axis=1)
    grad_product = (
        conv_taps[2] * grad_extended[:, :seq_len]
        + conv_taps[1] * grad_extended[:, 1 : seq_len + 1]
        + conv_taps[0] * grad_extended[:, 2:]
    ).reshape(row_count, channels)
    taps_grad = jnp.stack(
        [
            jnp.sum(grad_conv * extended[:, offset : offset + seq_len], axis=(0, 1))
            for offset in range(3)
        ]
    )
    grad_projected = jnp.stack(
        [grad_product * projected[2], grad_cproj, grad_product * projected[0]]
    ).astype(jnp.bfloat16)
    in_grad = jnp.einsum(
        "rd,kre->kde", input_low, grad_projected, preferred_element_type=jnp.float32
    )
    grad_first = lax.psum(
        jnp.einsum("kre,kde->rd", grad_projected, in_full, preferred_element_type=jnp.float32), "tp"
    )
    gain_one = jnp.sum(grad_first * normed_one, axis=0)
    input_grad = (
        grad_residual + norm_back(grad_first, normed_one, inverse_one, norm_gains[0])
    ).reshape(slot_count, seq_len, model_width)
    gain_total, taps_total = together(
        (jnp.stack([gain_one, gain_two]), taps_grad), ("shard", "ctx")
    )
    in_sum, out_sum, gate_up_sum, down_sum = (
        lax.psum_scatter(in_grad, ("shard", "ctx"), scatter_dimension=1, tiled=True),
        lax.psum_scatter(out_grad, ("shard", "ctx"), scatter_dimension=1, tiled=True),
        lax.psum_scatter(gate_up_grad, ("shard", "ctx"), scatter_dimension=1, tiled=True),
        lax.psum_scatter(down_grad, ("shard", "ctx"), scatter_dimension=1, tiled=True),
    )
    in_new = nesterov(in_weight, in_moment, in_average, in_sum, matrix_rate)
    out_new = nesterov(out_weight, out_moment, out_average, out_sum, matrix_rate)
    gate_up_new = nesterov(
        gate_up_weight, gate_up_moment, gate_up_average, gate_up_sum, matrix_rate
    )
    down_new = nesterov(down_weight, down_moment, down_average, down_sum, matrix_rate)
    gain_new = nesterov(norm_gains, gain_moment, gain_average, gain_total, small_rate)
    taps_new = nesterov(conv_taps, taps_moment, taps_average, taps_total, small_rate)
    return (
        block_output,
        input_grad,
        in_new[0],
        in_new[1],
        in_new[2],
        out_new[0],
        out_new[1],
        out_new[2],
        gate_up_new[0],
        gate_up_new[1],
        gate_up_new[2],
        down_new[0],
        down_new[1],
        down_new[2],
        gain_new[0],
        gain_new[1],
        gain_new[2],
        taps_new[0],
        taps_new[1],
        taps_new[2],
    )


def solution(mesh):
    placed = (
        P("shard", "ctx", None),
        P("shard"),
        P("shard", "ctx", None),
        P(None, ("shard", "ctx"), "tp"),
        P(None, ("shard", "ctx"), "tp"),
        P(None, ("shard", "ctx"), "tp"),
        P("tp", ("shard", "ctx")),
        P("tp", ("shard", "ctx")),
        P("tp", ("shard", "ctx")),
        P(None, ("shard", "ctx"), "tp"),
        P(None, ("shard", "ctx"), "tp"),
        P(None, ("shard", "ctx"), "tp"),
        P("tp", ("shard", "ctx")),
        P("tp", ("shard", "ctx")),
        P("tp", ("shard", "ctx")),
        P(),
        P(),
        P(),
        P(None, "tp"),
        P(None, "tp"),
        P(None, "tp"),
    )
    return jax.shard_map(
        on_device,
        mesh=mesh,
        in_specs=placed,
        out_specs=(
            P("shard", "ctx", None),
            P("shard", "ctx", None),
            P(None, ("shard", "ctx"), "tp"),
            P(None, ("shard", "ctx"), "tp"),
            P(None, ("shard", "ctx"), "tp"),
            P("tp", ("shard", "ctx")),
            P("tp", ("shard", "ctx")),
            P("tp", ("shard", "ctx")),
            P(None, ("shard", "ctx"), "tp"),
            P(None, ("shard", "ctx"), "tp"),
            P(None, ("shard", "ctx"), "tp"),
            P("tp", ("shard", "ctx")),
            P("tp", ("shard", "ctx")),
            P("tp", ("shard", "ctx")),
            P(),
            P(),
            P(),
            P(None, "tp"),
            P(None, "tp"),
            P(None, "tp"),
        ),
        check_vma=False,
    )
```

profile of v0, /device:TPU:0, one launch (start us, length us, event | category | flops | bytes accessed | tf_op | source)
XLA Modules:
  0.0 889.5 jit_solution(4571534511916546219)
XLA Ops:
  14.9 82.8 %all-gather.2.cloned.1.call-done = bf16[1536,6720]{1,0:T(8,128)(2,1)} async-done(((bf16[48,6720]{1,0:T(8,128)(2,1)}), bf16[1536,6720]{1,0:T(8,128)(2,1)}) %all-gather.2.cloned.1.call-update) | async-done | bytes 20643856 | tf_op jit(solution)/shard_map/all_gather | solution.py:16
  97.7 4.0 slice.112
  101.7 5.7 copy.148
  107.5 4.5 convolution_bitcast_fusion.5
  118.8 3.7 multiply_add_fusion.1
  123.7 4.1 fusion.34
  130.2 9.8 %slice.120 = bf16[1536,3456]{1,0:T(8,128)(2,1)} slice(bf16[1536,6720]{1,0:T(8,128)(2,1)} %all-gather.2.cloned.1.call-done), slice={[0:1536], [1536:4992]} | slice | bytes 21233664 | tf_op jit(solution)/shard_map/slice | solution.py:18
  140.1 14.5 %copy.149 = bf16[1536,3456]{0,1:T(8,128)(2,1)} copy(bf16[1536,3456]{1,0:T(8,128)(2,1)} %slice.120) | data formatting | bytes 21233664 | tf_op jit(solution)/shard_map/slice | solution.py:18
  154.6 55.2 %all-reduce.9.cloned.1.call-done = f32[512,1536]{1,0:T(8,128)} async-done(((f32[512,1536]{1,0:T(8,128)}), f32[512,1536]{1,0:T(8,128)}) %all-reduce.9.cloned.1.call-update) | async-done | bytes 3145744 | tf_op jit(solution)/shard_map/psum | solution.py:126
  209.8 2.8 multiply_reduce_fusion.2
  213.2 12.2 %convolution_bitcast_fusion.2 = f32[2,512,1728]{1,2,0:T(8,128)} fusion(bf16[2,1536,1728]{1,2,0:T(8,128)(2,1)} %bitcast.156, f32[512,1536]{1,0:T(8,128)S(1)} %get-tuple-element.156, f32[1536]{0:T(1024)S(1)} %get-tuple-element.126, f32[512]{0:T(512)S(1)} %add_rsqrt_fusion), kind=kOutput, calls=%fused_computation.6 | convolution fusion | flops 5438177280 | bytes 20848640 | tf_op jit(solution)/shard_map/rd,kdf->krf/dot_general | solution.py:130
  225.5 9.0 %fusion.28 = (bf16[1,512,1728]{1,2,0:T(8,128)(2,1)S(1)}, bf16[1,512,1728]{1,2,0:T(8,128)(2,1)S(1)}) fusion(f32[2,512,1728]{1,2,0:T(8,128)} %convolution_bitcast_fusion.2, bf16[512,1536]{1,0:T(8,128)(2,1)S(1)} %copy-done.14, bf16[1536,6720]{1,0:T(8,128)(2,1)} %all-gather.2.cloned.1.call-done), kind=kOutput, calls=%fused_computation.51 | convolution fusion | flops 2729410560 | bytes 17694720 | tf_op jit(solution)/shard_map/dot_general | solution.py:66
  236.3 7.6 convolution_bitcast_fusion.3
  244.2 75.4 %all-reduce.11.cloned.1.call-done = f32[512,1536]{1,0:T(8,128)} async-done(((f32[512,1536]{1,0:T(8,128)}), f32[512,1536]{1,0:T(8,128)}) %all-reduce.11.cloned.1.call-update) | async-done | bytes 3145744 | tf_op jit(solution)/shard_map/psum | solution.py:150
  319.7 3.4 multiply_reduce_fusion
  328.4 9.5 %fusion.2 = f32[512,1536]{1,0:T(8,128)} fusion(bf16[1536,6720]{1,0:T(8,128)(2,1)} %all-gather.2.cloned.1.call-done, f32[2,512,1728]{1,2,0:T(8,128)} %convolution_bitcast_fusion.2), kind=kOutput, calls=%fused_computation.3 | convolution fusion | flops 2723217408 | bytes 15728640 | tf_op jit(solution)/shard_map/dot_general | solution.py:136
  338.0 3.9 fusion.39
  349.5 16.1 %multiply_reduce_fusion.4 = (f32[384]{0:T(512)}, f32[384]{0:T(512)}, f32[2,256,384]{1,0,2:T(2,128)}) fusion(f32[2,256,384]{1,0,2:T(2,128)S(1)} %copy-done.8, f32[2,256,384]{1,0,2:T(2,128)S(1)} %copy-done.7, f32[2,2,384]{1,0,2:T(2,128)S(1)} %copy-done.18, f32[2,258,384]{1,0,2:T(2,128)S(1)} %constant_dynamic-update-slice_fusion, f32[384]{0:T(512)S(1)} %copy-done.37, ...), kind=kLoop, calls=%fused_computation.73 | loop fusion | flops 2161920 | bytes 3945984 | tf_op jit(solution)/shard_map/reduce_sum | solution.py:170
  365.6 2.6 reshape.179
  371.0 5.9 convolution_bitcast_fusion.4
  378.9 9.2 %fusion.26 = f32[1728,1536]{0,1:T(8,128)} fusion(bf16[512,1536]{1,0:T(8,128)(2,1)S(1)} %bitcast.165, f32[2,512,1728]{1,2,0:T(8,128)} %convolution_bitcast_fusion.2), kind=kOutput, calls=%fused_computation.49 | convolution fusion | flops 2723217408 | bytes 19267584 | tf_op jit(solution)/shard_map/dot_general | solution.py:60
  388.2 12.3 %convolution_bitcast_fusion = f32[2,1536,1728]{1,2,0:T(8,128)} fusion(bf16[1,512,1728]{1,2,0:T(8,128)(2,1)} %copy-done.53, bf16[1,512,1728]{1,2,0:T(8,128)(2,1)} %copy-done.52, f32[512,1536]{1,0:T(8,128)S(1)} %get-tuple-element.156, f32[1536]{0:T(1024)S(1)} %get-tuple-element.126, f32[512]{0:T(512)} %copy-done.34), kind=kOutput, calls=%fused_computation | convolution fusion | flops 5439946752 | bytes 27926528 | tf_op jit(solution)/shard_map/rd,krf->kdf/dot_general | solution.py:147
  400.5 32.9 %copy.157 = f32[2,1536,1728]{2,0,1:T(2,128)} copy(f32[2,1536,1728]{1,2,0:T(8,128)} %convolution_bitcast_fusion) | data formatting | bytes 42467328 | tf_op jit(solution)/shard_map/rd,krf->kdf/transpose | solution.py:147
  433.4 6.5 convolution_bitcast_fusion.1
  440.0 10.9 %copy.154 = f32[3,1536,384]{2,0,1:T(4,128)} copy(f32[3,1536,384]{1,2,0:T(8,128)} %convolution_bitcast_fusion.1) | data formatting | bytes 14155776 | tf_op jit(solution)/shard_map/rd,kre->kde/transpose | solution.py:177
  454.5 82.0 %all-reduce.15.cloned.1.call-done = (f32[512,1536]{1,0:T(8,128)}, f32[512,1536]{1,0:T(8,128)}) async-done(((f32[512,1536]{1,0:T(8,128)}, f32[512,1536]{1,0:T(8,128)}), (f32[512,1536]{1,0:T(8,128)}, f32[512,1536]{1,0:T(8,128)})) %all-reduce.15.cloned.1.call-update) | async-done | bytes 6291472 | tf_op jit(solution)/shard_map/psum | solution.py:136
  536.5 3.2 fusion.21
  540.9 7.4 all-to-all-start
  548.3 7.8 fusion.20
  556.2 3.4 all-to-all-done
  563.1 77.1 %reduce-scatter.5.cloned.1.call-done = f32[1728,48]{0,1:T(8,128)} async-done(((f32[1728,1536]{0,1:T(8,128)}), f32[1728,48]{0,1:T(8,128)}) %reduce-scatter.5.cloned.1.call-update) | async-done | bytes 331792 | tf_op jit(solution)/shard_map/reduce_scatter | solution.py:194
  642.4 234.1 %all-reduce.13.cloned.1.call-done = (f32[3,1536,384]{2,0,1:T(4,128)}, f32[2,1536,1728]{2,0,1:T(2,128)}) async-done(((f32[3,1536,384]{2,0,1:T(4,128)}, f32[2,1536,1728]{2,0,1:T(2,128)}), (f32[3,1536,384]{2,0,1:T(4,128)}, f32[2,1536,1728]{2,0,1:T(2,128)})) %all-reduce.13.cloned.1.call-update) | async-done | bytes 28311568
  (193 shorter events, 53.6 us)
Async XLA Ops:
  7.2 90.5 %all-gather.2.cloned.1.call-start = ((), (), s32[]{:S(2)}) async-start(), calls=%async_computation.3 | async-start | bytes 21491712 | tf_op jit(solution)/shard_map/all_gather | solution.py:16
  12.8 197.0 %all-reduce.9.cloned.1.call-start = ((), (), s32[]{:S(2)}) async-start(), calls=%async_computation.4 | async-start | bytes 6291456 | tf_op jit(solution)/shard_map/psum | solution.py:126
  13.3 88.4 %copy-start.30 = (f32[1,2,2,128]{3,1,2,0:T(2,128)}, f32[1,2,2,128]{3,1,2,0:T(2,128)S(1)}, u32[]{:S(2)}) copy-start(f32[1,2,2,128]{3,1,2,0:T(2,128)S(1)} %copy.168) | copy-start | bytes 6148
  112.0 10.6 %copy-start.9 = (f32[3,512,384]{1,2,0:T(8,128)}, f32[3,512,384]{1,2,0:T(8,128)S(1)}, u32[]{:S(2)}) copy-start(f32[3,512,384]{1,2,0:T(8,128)S(1)} %convolution_bitcast_fusion.5) | copy-start | bytes 7077892
  115.3 3.5 collective-permute-start
  127.8 191.9 %all-reduce.11.cloned.1.call-start = ((), (), s32[]{:S(2)}) async-start(), calls=%async_computation.5 | async-start | bytes 6291456 | tf_op jit(solution)/shard_map/psum | solution.py:150
  128.7 11.4 %copy-start.42 = (f32[1,2,2,128]{3,1,2,0:T(2,128)}, f32[1,2,2,128]{3,1,2,0:T(2,128)S(1)}, u32[]{:S(2)}) copy-start(f32[1,2,2,128]{3,1,2,0:T(2,128)S(1)} %copy.170) | copy-start | bytes 6148
  213.2 12.2 %copy-start.14 = (bf16[512,1536]{1,0:T(8,128)(2,1)S(1)}, bf16[512,1536]{1,0:T(8,128)(2,1)}, u32[]{:S(2)}) copy-start(bf16[512,1536]{1,0:T(8,128)(2,1)} %fusion.23) | copy-start | bytes 4718596
  213.2 23.1 %slice-start = ((s8[10616832]{0:T(1024)(128)(4,1)}), s8[4194304]{0:T(1024)(128)(4,1)S(1)}, s32[]{:S(2)}) async-start(s8[10616832]{0:T(1024)(128)(4,1)} %bitcast.157), calls=%async_computation.10 | async-start | bytes 8388608
  213.2 23.1 %slice-start.1 = ((s8[10616832]{0:T(1024)(128)(4,1)}), s8[4194304]{0:T(1024)(128)(4,1)S(1)}, s32[]{:S(2)}) async-start(s8[10616832]{0:T(1024)(128)(4,1)} %bitcast.157), calls=%async_computation.11 | async-start | bytes 8388608
  225.5 10.8 %slice-start.2 = ((s8[10616832]{0:T(1024)(128)(4,1)}), s8[2228224]{0:T(1024)(128)(4,1)S(1)}, s32[]{:S(2)}) async-start(s8[10616832]{0:T(1024)(128)(4,1)} %bitcast.157), calls=%async_computation.12 | async-start | bytes 4456448
  244.0 208.9 %reduce-scatter.3.cloned.1.call-start = ((), (), s32[]{:S(2)}) async-start(), calls=%async_computation.6 | async-start | bytes 2433024 | tf_op jit(solution)/shard_map/reduce_scatter | solution.py:192
  328.4 208.2 %all-reduce.15.cloned.1.call-start = ((), (), s32[]{:S(2)}) async-start(), calls=%async_computation.9 | async-start | bytes 12582912 | tf_op jit(solution)/shard_map/psum | solution.py:136
  328.4 9.6 %copy-start.1 = (f32[512,1536]{1,0:T(8,128)S(1)}, f32[512,1536]{1,0:T(8,128)}, u32[]{:S(2)}) copy-start(f32[512,1536]{1,0:T(8,128)} %copy-done) | copy-start | bytes 9437188
  328.4 9.6 %copy-start.10 = (f32[1,512,384]{1,2,0:T(8,128)S(1)}, f32[1,512,384]{1,2,0:T(8,128)}, u32[]{:S(2)}) copy-start(f32[1,512,384]{1,2,0:T(8,128)} %slice_multiply_fusion.2) | copy-start | bytes 2359300
  328.4 9.6 %copy-start.12 = (f32[48,8,2,256]{3,1,2,0:T(8,128)S(1)}, f32[48,8,2,256]{3,1,2,0:T(8,128)}, u32[]{:S(2)}) copy-start(f32[48,8,2,256]{3,1,2,0:T(8,128)} %copy-done.11) | copy-start | bytes 2359300
  345.6 3.6 collective-permute-start.1
  376.9 263.3 %reduce-scatter.5.cloned.1.call-start = ((), (), s32[]{:S(2)}) async-start(), calls=%async_computation.7 | async-start | bytes 11354112 | tf_op jit(solution)/shard_map/reduce_scatter | solution.py:194
  388.2 488.3 %all-reduce.13.cloned.1.call-start = ((), (), s32[]{:S(2)}) async-start(), calls=%async_computation.8 | async-start | bytes 62914560
  450.9 85.6 %copy-start.31 = (f32[1,2,2,128]{3,1,2,0:T(2,128)S(1)}, f32[1,2,2,128]{3,1,2,0:T(2,128)}, u32[]{:S(2)}) copy-start(f32[1,2,2,128]{3,1,2,0:T(2,128)} %copy-done.30) | copy-start | bytes 6148
  540.9 18.7 %all-to-all-start = ((f32[32,1,4224]{2,1,0:T(1,128)}), f32[32,1,4224]{2,1,0:T(1,128)}, u32[]{:S(2)}, u32[]{:S(2)}) async-start(f32[32,1,4224]{2,1,0:T(1,128)} %broadcast_in_dim.2), calls=%async_computation.2 | async-start | bytes 1081344 | tf_op jit(solution)/shard_map/all_to_all | solution.py:32
  548.3 12.8 %copy-start.33 = (f32[3,384]{1,0:T(4,128)S(1)}, f32[3,384]{1,0:T(4,128)}, u32[]{:S(2)}) copy-start(f32[3,384]{1,0:T(4,128)} %param.39) | copy-start | bytes 13828
  548.3 12.8 %copy-start.49 = (f32[3,384]{1,0:T(4,128)S(1)}, f32[3,384]{1,0:T(4,128)}, u32[]{:S(2)}) copy-start(f32[3,384]{1,0:T(4,128)} %param.41) | copy-start | bytes 13828
  548.3 14.2 %copy-start.28 = (f32[2,1536]{1,0:T(2,128)S(1)}, f32[2,1536]{1,0:T(2,128)}, u32[]{:S(2)}) copy-start(f32[2,1536]{1,0:T(2,128)} %param.36) | copy-start | bytes 36868
  548.3 14.2 %copy-start.44 = (f32[2,1536]{1,0:T(2,128)S(1)}, f32[2,1536]{1,0:T(2,128)}, u32[]{:S(2)}) copy-start(f32[2,1536]{1,0:T(2,128)} %param.38) | copy-start | bytes 36868
  548.3 14.2 %copy-start.45 = (f32[2,1536]{1,0:T(2,128)S(1)}, f32[2,1536]{1,0:T(2,128)}, u32[]{:S(2)}) copy-start(f32[2,1536]{1,0:T(2,128)} %param.37) | copy-start | bytes 36868
  548.3 91.8 %copy-start.19 = (f32[1728,48]{0,1:T(8,128)S(1)}, f32[1728,48]{0,1:T(8,128)}, u32[]{:S(2)}) copy-start(f32[1728,48]{0,1:T(8,128)} %param.33) | copy-start | bytes 995332
  556.1 322.5 %copy-start.20 = (f32[3,48,384]{2,1,0:T(8,128)S(1)}, f32[3,48,384]{2,1,0:T(8,128)}, u32[]{:S(2)}) copy-start(f32[3,48,384]{2,1,0:T(8,128)} %param.24) | copy-start | bytes 663556
  556.1 322.5 %copy-start.23 = (f32[3,48,384]{2,1,0:T(8,128)S(1)}, f32[3,48,384]{2,1,0:T(8,128)}, u32[]{:S(2)}) copy-start(f32[3,48,384]{2,1,0:T(8,128)} %param.26) | copy-start | bytes 663556
  556.1 322.5 %copy-start.24 = (f32[3,48,384]{2,1,0:T(8,128)S(1)}, f32[3,48,384]{2,1,0:T(8,128)}, u32[]{:S(2)}) copy-start(f32[3,48,384]{2,1,0:T(8,128)} %param.25) | copy-start | bytes 663556
  561.0 318.6 %copy-start.13 = (f32[2,48,1728]{2,1,0:T(8,128)S(1)}, f32[2,48,1728]{2,1,0:T(8,128)}, u32[]{:S(2)}) copy-start(f32[2,48,1728]{2,1,0:T(8,128)} %param.30) | copy-start | bytes 1990660
  561.0 318.6 %copy-start.21 = (f32[2,48,1728]{2,1,0:T(8,128)S(1)}, f32[2,48,1728]{2,1,0:T(8,128)}, u32[]{:S(2)}) copy-start(f32[2,48,1728]{2,1,0:T(8,128)} %param.32) | copy-start | bytes 1990660
  (35 other events, 117.3 us)
Sparse Core Ops, SparseCore 0:
  13.0 84.6 all-gather.1
  127.9 81.8 all-reduce.8
  244.1 75.5 all-reduce.10
  328.5 79.3 reduce-scatter.2
  410.2 126.2 all-reduce.14
  540.6 99.4 reduce-scatter.4
  644.1 232.3 all-reduce.12
where the time goes:
time: 898 us; the launch traced here: 889 us
  waiting for transfers between devices  612 us (68%)
  local copies, waits for them, and re-layouts  99 us (11%)
  matrix products  87.4 us (10%)
  other arithmetic  63 us (7%)
  between operations  16.1 us (2%)
  starting transfers between devices  11.8 us (1%)
    unnamed x8, waiting for transfers between devices  234 us
    all_gather x1, waiting for transfers between devices, rows_first(): whole, at, outs = (lax.all_gather(both, axis, axis=0, tiled=True), 0, [])  82.8 us
    psum x1, waiting for transfers between devices, on_device(): lax.psum(jnp.dot(inner_low, down_full, preferred_element_type=jnp.float32...  82 us
    reduce_scatter x1, waiting for transfers between devices, on_device(): lax.psum_scatter(down_grad, ('shard', 'ctx'), scatter_dimension=1, tiled=...  77.1 us
    psum x1, waiting for transfers between devices, on_device(): lax.psum(jnp.einsum('krf,kdf->rd', grad_gate_up, gate_up_full, preferred_...  75.4 us
    psum x1, waiting for transfers between devices, on_device(): lax.psum(jnp.dot(gated_low, out_full, preferred_element_type=jnp.float32)...  55.2 us
    slice x4, local copies, waits for them, and re-layouts, rows_first(): piece = whole[:, at:at + t[0].size].reshape(-1, *t.shape[1:])  34.1 us
    transpose x1, local copies, waits for them, and re-layouts, on_device(): jnp.einsum('rd,krf->kdf', second_low, grad_gate_up, preferred_element_typ...  32.9 us
  transfers between devices with their start and end apart: 10, of which 9 were waited for; matrix products, arithmetic and copies ran while one was open for 19% of the time, Pallas kernels for 0%

commit v1 on v0

--- a/solution.py
+++ b/solution.py
@@ -1,24 +1,287 @@
+import functools
+
 import jax
 import jax.numpy as jnp
 from jax import lax
+from jax.experimental import pallas as pl
+from jax.experimental.pallas import tpu as pltpu
 from jax.sharding import PartitionSpec as P
 
+MESH = pl.DeviceIdType.MESH
 epsilon = 1e-05
 momentum = 0.9
 average_decay = 0.9
 matrix_rate = 0.0004
 small_rate = 0.005
-
-
-def rows_first(arrays, axis, dims):
-    turned = [jnp.moveaxis(a, dim, 0) for a, dim in zip(arrays, dims)]
-    both = jnp.concatenate([t.reshape(len(t), -1) for t in turned], axis=1)
-    whole, at, outs = (lax.all_gather(both, axis, axis=0, tiled=True), 0, [])
-    for t, dim in zip(turned, dims):
-        piece = whole[:, at : at + t[0].size].reshape(-1, *t.shape[1:])
-        outs.append(jnp.moveaxis(piece, 0, dim))
-        at += t[0].size
-    return tuple(outs)
+WIDTH = 1536
+CHANNELS = 384
+HIDDEN = 1728
+PADDED = 1792
+ROWS = 512
+QUARTER = 128
+SLOT_ROWS = 256
+BLOCK = 48
+
+
+class Place:
+    def __init__(self):
+        self.shard = lax.axis_index("shard")
+        self.ctx = lax.axis_index("ctx")
+        self.tp = lax.axis_index("tp")
+        self.y = self.shard * 2 + lax.div(self.ctx, 8)
+        self.z = lax.rem(lax.div(self.ctx, 2), 4)
+        self.core = lax.rem(self.ctx, 2)
+        self.first = self.y * (1 - self.core) + self.z * self.core
+        self.second = self.z * (1 - self.core) + self.y * self.core
+
+    def turn(self, value, by):
+        return lax.rem(value + by + 4, 4)
+
+    def device(self, y, z, core):
+        return (lax.div(y, 2), lax.rem(y, 2) * 8 + z * 2 + core, self.tp)
+
+    def grid_device(self, first, second):
+        y = first * (1 - self.core) + second * self.core
+        z = second * (1 - self.core) + first * self.core
+        return self.device(y, z, self.core)
+
+    def block(self, first, second):
+        y = first * (1 - self.core) + second * self.core
+        z = second * (1 - self.core) + first * self.core
+        return y * 8 + z * 2 + self.core
+
+    def along_first(self, by):
+        return self.grid_device(self.turn(self.first, by), self.second)
+
+    def along_second(self, by):
+        return self.grid_device(self.first, self.turn(self.second, by))
+
+    def along_tp(self, by):
+        return (self.shard, self.ctx, self.turn(self.tp, by))
+
+    def along_ctx(self, by):
+        return (self.shard, lax.rem(self.ctx + by + 16, 16), self.tp)
+
+    def sibling(self):
+        return self.device(self.y, self.z, 1 - self.core)
+
+    def greet(self):
+        barrier = pltpu.get_barrier_semaphore()
+        friends = [self.sibling(), self.along_ctx(1), self.along_ctx(-1)]
+        for by in (1, 2, 3):
+            friends += [self.along_first(by), self.along_second(by), self.along_tp(by)]
+        for friend in friends:
+            pl.semaphore_signal(barrier, inc=1, device_id=friend, device_id_type=MESH)
+        pl.semaphore_wait(barrier, len(friends))
+
+
+def remote(source, target, sems, at, device):
+    return pltpu.make_async_remote_copy(
+        src_ref=source,
+        dst_ref=target,
+        send_sem=sems.at[0, at],
+        recv_sem=sems.at[1, at],
+        device_id=device,
+        device_id_type=MESH,
+    )
+
+
+class Gather:
+    SEMS = 31
+
+    def __init__(self, place, local, whole, sems):
+        self.place, self.local, self.whole, self.sems = place, local, whole, sems
+        self.sent = []
+
+    def send(self, source, block, at, device):
+        copy = remote(source, self.whole.at[:, block], self.sems, at, device)
+        copy.start()
+        self.sent.append(copy)
+
+    def arrived(self, block, at):
+        spot = self.whole.at[:, block]
+        remote(spot, spot, self.sems, at, self.place.sibling()).wait_recv()
+
+    def start(self):
+        p = self.place
+        mine = p.block(p.first, p.second)
+        for by in (1, 2, 3):
+            self.send(self.local, mine, by - 1, p.along_first(by))
+        for by in (1, 2, 3):
+            self.send(self.local, mine, 3 + by - 1, p.along_second(by))
+        self.send(self.local, mine, 15, p.sibling())
+
+    def forward_first(self):
+        p = self.place
+        for back in (1, 3, 2):
+            block = p.block(p.turn(p.first, -back), p.second)
+            self.arrived(block, back - 1)
+            for by in (1, 2, 3):
+                self.send(self.whole.at[:, block], block, 3 + back * 3 + by - 1, p.along_second(by))
+            self.send(self.whole.at[:, block], block, 15 + back * 4, p.sibling())
+
+    def forward_second(self):
+        p = self.place
+        for back in (0, 1, 3, 2):
+            for by in (1, 3, 2):
+                block = p.block(p.turn(p.first, -back), p.turn(p.second, -by))
+                self.arrived(block, 3 + back * 3 + by - 1)
+                self.send(self.whole.at[:, block], block, 15 + back * 4 + by, p.sibling())
+
+    def finish(self):
+        p = self.place
+        for back in range(4):
+            for by in range(4):
+                self.arrived(p.block(p.turn(p.first, -back), p.turn(p.second, -by)), 15 + back * 4 + by)
+        for copy in self.sent:
+            copy.wait_send()
+
+
+def dot(left, right):
+    return jnp.dot(left, right, preferred_element_type=jnp.float32)
+
+
+def dot_t(left, right):
+    return lax.dot_general(left, right, (((1,), (1,)), ((), ())), preferred_element_type=jnp.float32)
+
+
+def forward_kernel(
+    io_local,
+    gud_local,
+    x,
+    gains,
+    taps,
+    io_full,
+    gud_full,
+    second_low,
+    residual,
+    projected,
+    product,
+    convolved,
+    gated,
+    input_low,
+    x_send,
+    x_recv,
+    own_part,
+    io_sems,
+    gud_sems,
+    x_sems,
+    local_sems,
+):
+    place = Place()
+    place.greet()
+    mine = place.block(place.first, place.second)
+    keep = [
+        pltpu.make_async_copy(io_local, io_full.at[:, mine], local_sems.at[0]),
+        pltpu.make_async_copy(gud_local, gud_full.at[:, mine], local_sems.at[1]),
+    ]
+    for copy in keep:
+        copy.start()
+    io = Gather(place, io_local, io_full, io_sems)
+    gud = Gather(place, gud_local, gud_full, gud_sems)
+    io.start()
+
+    @pl.loop(0, ROWS, step=64)
+    def _(at):
+        values = x[pl.ds(at, 64), :].astype(jnp.float32)
+        inverse = lax.rsqrt(jnp.mean(values * values, axis=-1, keepdims=True) + epsilon)
+        input_low[pl.ds(at, 64), :] = (values * inverse * gains[0:1, :]).astype(jnp.bfloat16)
+
+    io.forward_first()
+    io.forward_second()
+    gud.start()
+    io.finish()
+    keep[0].wait()
+
+    for member in (0, 2):
+        projected[member] = dot(input_low[...], io_full[member].reshape(WIDTH, CHANNELS))
+    product[:, 8:, :] = (projected[0] * projected[2]).reshape(2, SLOT_ROWS, CHANNELS)
+    halo = remote(
+        product.at[:, pl.ds(SLOT_ROWS, 8)], product.at[:, pl.ds(0, 8)], x_sems, 6, place.along_ctx(1)
+    )
+    halo.start()
+    projected[1] = dot(input_low[...], io_full[1].reshape(WIDTH, CHANNELS))
+    halo.wait()
+    product[:, :8, :] = jnp.where(place.ctx > 0, product[:, :8, :], 0.0)
+    convolved[...] = (
+        taps[0:1, :] * product[:, 6 : 6 + SLOT_ROWS, :]
+        + taps[1:2, :] * product[:, 7 : 7 + SLOT_ROWS, :]
+        + taps[2:3, :] * product[:, 8 : 8 + SLOT_ROWS, :]
+    ).reshape(ROWS, CHANNELS)
+    gated[...] = (projected[1] * convolved[...]).astype(jnp.bfloat16)
+
+    sent = []
+    for by in (2, 1, 3, 0):
+        row = place.turn(place.tp, by) * QUARTER
+        part = dot_t(gated[pl.ds(row, QUARTER), :], io_full[3].reshape(WIDTH, CHANNELS))
+        if by == 0:
+            own_part[...] = part
+        else:
+            x_send[by - 1] = part.astype(jnp.bfloat16)
+            copy = remote(x_send.at[by - 1], x_recv.at[by - 1], x_sems, by - 1, place.along_tp(by))
+            copy.start()
+            sent.append(copy)
+    gud.forward_first()
+    for copy in sent:
+        copy.wait_recv()
+    own_rows = pl.ds(place.tp * QUARTER, QUARTER)
+    total = (
+        own_part[...]
+        + x_recv[0].astype(jnp.float32)
+        + x_recv[1].astype(jnp.float32)
+        + x_recv[2].astype(jnp.float32)
+    )
+    stream = x[own_rows, :].astype(jnp.float32) + total
+    residual[...] = stream
+    inverse = lax.rsqrt(jnp.mean(stream * stream, axis=-1, keepdims=True) + epsilon)
+    second_low[own_rows, :] = (stream * inverse * gains[1:2, :]).astype(jnp.bfloat16)
+    for by in (2, 1, 3):
+        spot = second_low.at[own_rows]
+        copy = remote(spot, spot, x_sems, 3 + by - 1, place.along_tp(by))
+        copy.start()
+        sent.append(copy)
+    gud.forward_second()
+    gud.finish()
+    keep[1].wait()
+    for copy in sent[3:]:
+        copy.wait_recv()
+    for copy in sent:
+        copy.wait_send()
+
+
+def forward(io_local, gud_local, x, gains, taps):
+    vmem = pl.BlockSpec(memory_space=pltpu.VMEM)
+    hbm = pl.BlockSpec(memory_space=pl.ANY)
+    f32, b16 = jnp.float32, jnp.bfloat16
+    return pl.pallas_call(
+        forward_kernel,
+        out_shape=(
+            jax.ShapeDtypeStruct((4, 32, BLOCK, CHANNELS), b16),
+            jax.ShapeDtypeStruct((3, 32, BLOCK, PADDED), b16),
+            jax.ShapeDtypeStruct((ROWS, WIDTH), b16),
+            jax.ShapeDtypeStruct((QUARTER, WIDTH), f32),
+            jax.ShapeDtypeStruct((3, ROWS, CHANNELS), f32),
+            jax.ShapeDtypeStruct((2, 8 + SLOT_ROWS, CHANNELS), f32),
+            jax.ShapeDtypeStruct((ROWS, CHANNELS), f32),
+            jax.ShapeDtypeStruct((ROWS, CHANNELS), b16),
+        ),
+        in_specs=[hbm, hbm, vmem, vmem, vmem],
+        out_specs=(vmem, hbm, vmem, vmem, vmem, vmem, vmem, vmem),
+        scratch_shapes=[
+            pltpu.VMEM((ROWS, WIDTH), b16),
+            pltpu.VMEM((3, QUARTER, WIDTH), b16),
+            pltpu.VMEM((3, QUARTER, WIDTH), b16),
+            pltpu.VMEM((QUARTER, WIDTH), f32),
+            pltpu.SemaphoreType.DMA((2, Gather.SEMS)),
+            pltpu.SemaphoreType.DMA((2, Gather.SEMS)),
+            pltpu.SemaphoreType.DMA((2, 7)),
+            pltpu.SemaphoreType.DMA((2,)),
+        ],
+        compiler_params=pltpu.CompilerParams(
+            collective_id=0, has_side_effects=True, vmem_limit_bytes=56 * 2**20
+        ),
+        name="forward",
+    )(io_local, gud_local, x, gains, taps)
 
 
 def from_behind(value, axis, steps):
@@ -98,35 +361,30 @@
     taps_moment,
     taps_average,
 ):
-    in_low = in_weight.astype(jnp.bfloat16)
-    out_low = out_weight.astype(jnp.bfloat16)
-    gate_up_low = gate_up_weight.astype(jnp.bfloat16)
-    down_low = down_weight.astype(jnp.bfloat16)
-    in_full, out_full, gate_up_full, down_full = rows_first(
-        (in_low, out_low, gate_up_low, down_low), ("shard", "ctx"), (1, 1, 1, 1)
-    )
+    b16 = jnp.bfloat16
+    io_local = jnp.concatenate([in_weight.astype(b16), out_weight.astype(b16).T[None]], axis=0)
+    gud_local = jnp.concatenate(
+        [gate_up_weight.astype(b16), down_weight.astype(b16).T[None]], axis=0
+    )
+    gud_local = jnp.pad(gud_local, ((0, 0), (0, 0), (0, PADDED - HIDDEN)))
     slot_count, seq_len, model_width = hidden.shape
     row_count = slot_count * seq_len
+    io_full, gud_full, second_low, residual_own, projected, extended, convolved, gated_low = forward(
+        io_local, gud_local, hidden.reshape(row_count, model_width), norm_gains, conv_taps
+    )
+    in_full = io_full[:3].reshape(3, WIDTH, CHANNELS)
+    out_full = io_full[3].reshape(WIDTH, CHANNELS).T
+    gate_up_full = gud_full[:2].reshape(2, WIDTH, PADDED)[:, :, :HIDDEN]
+    down_full = gud_full[2].reshape(WIDTH, PADDED)[:, :HIDDEN].T
+    channels = CHANNELS
     stream = hidden.astype(jnp.float32).reshape(row_count, model_width)
     positions = lax.axis_index("ctx") * seq_len + jnp.arange(seq_len, dtype=jnp.int32)
     valid_rows = (positions[None, :] < lengths[:, None]).astype(jnp.float32).reshape(row_count, 1)
     normed_one, inverse_one = normalize(stream)
     input_low = (normed_one * norm_gains[0]).astype(jnp.bfloat16)
-    projected = jnp.einsum("rd,kde->kre", input_low, in_full, preferred_element_type=jnp.float32)
-    channels = projected.shape[2]
-    product = (projected[0] * projected[2]).reshape(slot_count, seq_len, channels)
-    previous = from_behind(product[:, seq_len - 2 :, :], "ctx", 1)
-    extended = jnp.concatenate([previous, product], axis=1)
-    convolved = (
-        conv_taps[0] * extended[:, :seq_len]
-        + conv_taps[1] * extended[:, 1 : seq_len + 1]
-        + conv_taps[2] * extended[:, 2:]
-    ).reshape(row_count, channels)
-    gated_low = (projected[1] * convolved).astype(jnp.bfloat16)
-    mixed_sum = lax.psum(jnp.dot(gated_low, out_full, preferred_element_type=jnp.float32), "tp")
-    residual = stream + mixed_sum
+    extended = extended[:, 6:]
+    residual = lax.all_gather(residual_own, "tp", axis=0, tiled=True)
     normed_two, inverse_two = normalize(residual)
-    second_low = (normed_two * norm_gains[1]).astype(jnp.bfloat16)
     gate_up = jnp.einsum(
         "rd,kdf->krf", second_low, gate_up_full, preferred_element_type=jnp.float32
     )

time: 898 us -> 819 us (0.912)
  waiting for transfers between devices: 612 us -> 506 us
  Pallas kernels: 0 us -> 95.4 us
  local copies, waits for them, and re-layouts: 99 us -> 74.4 us
  other arithmetic: 63 us -> 39.1 us
  matrix products: 87.4 us -> 73.1 us
    pallas_call x0 -> x1, Pallas kernels: none -> 95.4 us  [forward(): pl.pallas_call(forward_kernel, out_shape=(jax.ShapeDtypeStruct((4, 32, BL...]
    all_gather x1, waiting for transfers between devices: 82.8 us -> 0.01 us  [on_device(): residual = lax.all_gather(residual_own, 'tp', axis=0, tiled=True)]
    reduce_scatter x1, waiting for transfers between devices: 0.02 us -> 61.5 us  [on_device(): lax.psum_scatter(out_grad, ('shard', 'ctx'), scatter_dimension=1, tiled=T...]
    psum x1 -> x0, waiting for transfers between devices: 55.2 us -> none  [on_device(): lax.psum(jnp.dot(gated_low, out_full, preferred_element_type=jnp.float32)...]
    psum x1, waiting for transfers between devices: 75.4 us -> 58.7 us  [on_device(): lax.psum(jnp.einsum('krf,kdf->rd', grad_gate_up, gate_up_full, preferred_...]
    reduce_sum x1 -> x0, other arithmetic: 16.1 us -> none  [on_device(): jnp.sum(grad_conv * extended[:, offset:offset + seq_len], axis=(0, 1))]
    psum x1, waiting for transfers between devices: 82 us -> 67.3 us  [on_device(): lax.psum(jnp.dot(inner_low, down_full, preferred_element_type=jnp.float32...]
    slice x7 -> x6, local copies, waits for them, and re-layouts: 34.7 us -> 22.5 us  [the longest x1 9.82 us: on_device(): gate_up_full = gud_full[:2].reshape(2, WIDTH, PADDED)[:, :, :HIDDEN]]
  transfers between devices with their start and end apart: 10 -> 8, of which waited for: 9 -> 7; matrix products, arithmetic and copies ran while one was open for 19% -> 20% of each run, Pallas kernels for 0% -> 0%
where the time goes in v1:
time: 819 us; the launch traced here: 812 us
  waiting for transfers between devices  506 us (62%)
  Pallas kernels  95.4 us (12%)
  local copies, waits for them, and re-layouts  74.4 us (9%)
  matrix products  73.1 us (9%)
  other arithmetic  39.1 us (5%)
  between operations  15.7 us (2%)
    unnamed x7, waiting for transfers between devices  234 us
    pallas_call x1, Pallas kernels, forward(): pl.pallas_call(forward_kernel, out_shape=(jax.ShapeDtypeStruct((4, 32, BL...  95.4 us
    reduce_scatter x1, waiting for transfers between devices, on_device(): lax.psum_scatter(down_grad, ('shard', 'ctx'), scatter_dimension=1, tiled=...  79.2 us
    psum x1, waiting for transfers between devices, on_device(): lax.psum(jnp.dot(inner_low, down_full, preferred_element_type=jnp.float32...  67.3 us
    reduce_scatter x1, waiting for transfers between devices, on_device(): lax.psum_scatter(out_grad, ('shard', 'ctx'), scatter_dimension=1, tiled=T...  61.5 us
    psum x1, waiting for transfers between devices, on_device(): lax.psum(jnp.einsum('krf,kdf->rd', grad_gate_up, gate_up_full, preferred_...  58.7 us
    transpose x1, local copies, waits for them, and re-layouts, on_device(): jnp.einsum('rd,krf->kdf', second_low, grad_gate_up, preferred_element_typ...  32.6 us
  transfers between devices with their start and end apart: 8, of which 7 were waited for; matrix products, arithmetic and copies ran while one was open for 20% of the time, Pallas kernels for 0%

profile of v1, /device:TPU:0, one launch (start us, length us, event | category | flops | bytes accessed | tf_op | source)
XLA Modules:
  0.0 811.5 jit_solution(3442599423900609923)
XLA Ops:
  12.7 95.4 %forward.1 = (bf16[4,32,48,384]{3,2,1,0:T(8,128)(2,1)}, bf16[3,32,48,1792]{3,2,1,0:T(8,128)(2,1)}, bf16[512,1536]{1,0:T(8,128)(2,1)}, f32[128,1536]{1,0:T(8,128)...) custom-call(bf16[4,48,384]{2,1,0:T(8,128)(2,1)} %pad_maximum_fusion.7.io_loca, ...), custom_call_target="tpu_custom_call" | custom-call | tf_op jit(solution)/shard_map/forward/pallas_call | solution.py:256
  108.4 5.3 slice.94
  113.7 9.8 %slice.90 = bf16[2,32,48,1792]{3,2,1,0:T(8,128)(2,1)} slice(bf16[3,32,48,1792]{3,2,1,0:T(8,128)(2,1)} %get-tuple-element.29), slice={[0:2], [0:32], [0:48], [0:1792]} | slice | bytes 22020096 | tf_op jit(solution)/shard_map/slice | solution.py:377
  123.9 11.5 %fusion.8 = f32[2,512,1728]{1,2,0:T(8,128)} fusion(bf16[2,1536,1792]{2,1,0:T(8,128)(2,1)} %bitcast.126, bf16[512,1536]{1,0:T(8,128)(2,1)} %get-tuple-element.30), kind=kOutput, calls=%fused_computation.10 | convolution fusion | flops 5435817984 | bytes 19660800 | tf_op jit(solution)/shard_map/rd,kdf->krf/dot_general | solution.py:388
  135.4 7.9 fusion.27
  143.3 9.7 %fusion.19 = f32[512,1536]{1,0:T(8,128)} fusion(bf16[2,1536,1792]{2,1,0:T(8,128)(2,1)S(1)} %bitcast.129, bf16[1,512,1728]{1,2,0:T(8,128)(2,1)} %get-tuple-element.152, bf16[1,512,1728]{1,2,0:T(8,128)(2,1)} %get-tuple-element.151), kind=kOutput, calls=%fused_computation.27 | convolution fusion | flops 5437587456 | bytes 17694720 | tf_op jit(solution)/shard_map/krf,kdf->rd/dot_general | solution.py:409
  153.3 2.4 slice.98
  155.8 4.4 slice.107
  161.1 7.9 fusion.6
  169.1 2.3 multiply_reduce_fusion.5
  171.4 58.7 %all-reduce.9.cloned.1.call-done = f32[512,1536]{1,0:T(8,128)} async-done(((f32[512,1536]{1,0:T(8,128)}), f32[512,1536]{1,0:T(8,128)}) %all-reduce.9.cloned.1.call-update) | async-done | bytes 3145744 | tf_op jit(solution)/shard_map/psum | solution.py:408
  230.1 3.4 multiply_reduce_fusion
  236.3 1.7 multiply_reduce_fusion.8
  242.4 3.9 convolution_bitcast_fusion.2
  247.3 4.3 fusion.40
  251.7 1.7 multiply_convert_fusion.2
  253.4 9.1 %fusion.25 = f32[1728,1536]{0,1:T(8,128)} fusion(bf16[512,1536]{1,0:T(8,128)(2,1)S(1)} %bitcast.141, f32[2,512,1728]{1,2,0:T(8,128)} %fusion.8), kind=kOutput, calls=%fused_computation.44 | convolution fusion | flops 2723217408 | bytes 19267584 | tf_op jit(solution)/shard_map/dot_general | solution.py:323
  262.8 1.8 multiply_reduce_fusion.3
  264.6 12.1 %convolution_bitcast_fusion = f32[2,1536,1728]{1,2,0:T(8,128)} fusion(bf16[1,512,1728]{1,2,0:T(8,128)(2,1)} %get-tuple-element.152, bf16[1,512,1728]{1,2,0:T(8,128)(2,1)} %get-tuple-element.151, bf16[512,1536]{1,0:T(8,128)(2,1)} %get-tuple-element.30), kind=kOutput, calls=%fused_computation | convolution fusion | flops 5437587456 | bytes 26345472 | tf_op jit(solution)/shard_map/rd,krf->kdf/dot_general | solution.py:405
  276.8 32.6 %copy.109 = f32[2,1536,1728]{2,0,1:T(2,128)} copy(f32[2,1536,1728]{1,2,0:T(8,128)} %convolution_bitcast_fusion) | data formatting | bytes 42467328 | tf_op jit(solution)/shard_map/rd,krf->kdf/transpose | solution.py:405
  309.4 67.3 %all-reduce.13.cloned.1.call-done = (f32[512,1536]{1,0:T(8,128)}, f32[512,1536]{1,0:T(8,128)}) async-done(((f32[512,1536]{1,0:T(8,128)}, f32[512,1536]{1,0:T(8,128)}), (f32[512,1536]{1,0:T(8,128)}, f32[512,1536]{1,0:T(8,128)})) %all-reduce.13.cloned.1.call-update) | async-done | bytes 6291472 | tf_op jit(solution)/shard_map/psum | solution.py:394
  376.7 3.5 multiply_reduce_fusion.1
  380.1 4.9 convolution_bitcast_fusion.1
  385.1 10.9 %copy.106 = f32[3,1536,384]{2,0,1:T(4,128)} copy(f32[3,1536,384]{1,2,0:T(8,128)} %convolution_bitcast_fusion.1) | data formatting | bytes 14155776 | tf_op jit(solution)/shard_map/rd,kre->kde/transpose | solution.py:435
  398.0 61.5 %reduce-scatter.3.cloned.1.call-done = f32[384,48]{0,1:T(8,128)} async-done(((f32[384,1536]{0,1:T(8,128)}), f32[384,48]{0,1:T(8,128)}) %reduce-scatter.3.cloned.1.call-update) | async-done | bytes 73744 | tf_op jit(solution)/shard_map/reduce_scatter | solution.py:450
  462.2 5.3 all-to-all-start
  467.6 7.4 multiply_add_fusion
  475.0 3.9 all-to-all-done
  483.1 79.2 %reduce-scatter.5.cloned.1.call-done = f32[1728,48]{0,1:T(8,128)} async-done(((f32[1728,1536]{0,1:T(8,128)}), f32[1728,48]{0,1:T(8,128)}) %reduce-scatter.5.cloned.1.call-update) | async-done | bytes 331792 | tf_op jit(solution)/shard_map/reduce_scatter | solution.py:452
  562.3 2.2 multiply_add_fusion.4
  564.6 233.9 %all-reduce.11.cloned.1.call-done = (f32[3,1536,384]{2,0,1:T(4,128)}, f32[2,1536,1728]{2,0,1:T(2,128)}) async-done(((f32[3,1536,384]{2,0,1:T(4,128)}, f32[2,1536,1728]{2,0,1:T(2,128)}), (f32[3,1536,384]{2,0,1:T(4,128)}, f32[2,1536,1728]{2,0,1:T(2,128)})) %all-reduce.11.cloned.1.call-update) | async-done | bytes 28311568
  801.6 2.6 multiply_add_fusion.2
  (144 shorter events, 27.2 us)
Async XLA Ops:
  7.2 161.9 %all-gather.2.cloned.1.call-start = ((), (), s32[]{:S(2)}) async-start(), calls=%async_computation.3 | async-start | bytes 3932160 | tf_op jit(solution)/shard_map/all_gather | solution.py:386
  108.2 122.0 %all-reduce.9.cloned.1.call-start = ((), (), s32[]{:S(2)}) async-start(), calls=%async_computation.4 | async-start | bytes 6291456 | tf_op jit(solution)/shard_map/psum | solution.py:408
  113.6 9.8 %copy-start.33 = (s32[2]{0:T(128)S(1)}, s32[2]{0:T(128)}, u32[]{:S(2)}) copy-start(s32[2]{0:T(128)} %param.22) | copy-start | bytes 28
  113.7 9.9 %copy-start.2 = (bf16[2,256,1536]{2,1,0:T(8,128)(2,1)S(1)}, bf16[2,256,1536]{2,1,0:T(8,128)(2,1)}, u32[]{:S(2)}) copy-start(bf16[2,256,1536]{2,1,0:T(8,128)(2,1)} %param.23) | copy-start | bytes 4718596
  123.6 11.9 %slice-start.3 = ((s8[5505024]{0:T(1024)(128)(4,1)}), s8[4194304]{0:T(1024)(128)(4,1)S(1)}, s32[]{:S(2)}) async-start(s8[5505024]{0:T(1024)(128)(4,1)} %bitcast.131), calls=%async_computation.12 | async-start | bytes 8388608
  123.9 11.5 %slice-start.4 = ((s8[5505024]{0:T(1024)(128)(4,1)}), s8[1310720]{0:T(1024)(128)(4,1)S(1)}, s32[]{:S(2)}) async-start(s8[5505024]{0:T(1024)(128)(4,1)} %bitcast.131), calls=%async_computation.13 | async-start | bytes 2621440
  123.9 19.4 %slice-start = ((s8[11010048]{0:T(1024)(128)(4,1)}), s8[4194304]{0:T(1024)(128)(4,1)S(1)}, s32[]{:S(2)}) async-start(s8[11010048]{0:T(1024)(128)(4,1)} %bitcast.127), calls=%async_computation.9 | async-start | bytes 8388608
  123.9 19.4 %slice-start.1 = ((s8[11010048]{0:T(1024)(128)(4,1)}), s8[4194304]{0:T(1024)(128)(4,1)S(1)}, s32[]{:S(2)}) async-start(s8[11010048]{0:T(1024)(128)(4,1)} %bitcast.127), calls=%async_computation.10 | async-start | bytes 8388608
  135.4 7.9 slice-start.2
  153.1 223.6 %all-reduce.13.cloned.1.call-start = ((), (), s32[]{:S(2)}) async-start(), calls=%async_computation.8 | async-start | bytes 12582912 | tf_op jit(solution)/shard_map/psum | solution.py:394
  155.7 4.4 copy-start.28
  155.7 4.4 copy-start.24
  155.8 5.4 copy-start.35
  169.1 61.1 %copy-start = (f32[512,1536]{1,0:T(8,128)S(1)}, f32[512,1536]{1,0:T(8,128)}, u32[]{:S(2)}) copy-start(f32[512,1536]{1,0:T(8,128)} %all-gather.2.cloned.1.call-done) | copy-start | bytes 9437188
  238.0 3.1 collective-permute-start
  246.3 213.1 %reduce-scatter.3.cloned.1.call-start = ((), (), s32[]{:S(2)}) async-start(), calls=%async_computation.5 | async-start | bytes 2433024 | tf_op jit(solution)/shard_map/reduce_scatter | solution.py:450
  251.6 310.7 %reduce-scatter.5.cloned.1.call-start = ((), (), s32[]{:S(2)}) async-start(), calls=%async_computation.6 | async-start | bytes 11354112 | tf_op jit(solution)/shard_map/reduce_scatter | solution.py:452
  262.5 536.0 %all-reduce.11.cloned.1.call-start = ((), (), s32[]{:S(2)}) async-start(), calls=%async_computation.7 | async-start | bytes 62914560
  276.8 99.9 %copy-start.25 = (f32[1536]{0:T(1024)S(1)}, f32[1536]{0:T(1024)}, u32[]{:S(2)}) copy-start(f32[1536]{0:T(1024)} %get-tuple-element.123) | copy-start | bytes 18436
  376.6 3.5 copy-start.16
  376.6 3.5 copy-start.18
  376.6 3.5 copy-start.20
  396.0 63.4 %copy-start.21 = (f32[384,48]{0,1:T(8,128)S(1)}, f32[384,48]{0,1:T(8,128)}, u32[]{:S(2)}) copy-start(f32[384,48]{0,1:T(8,128)} %param.27) | copy-start | bytes 221188
  396.0 63.4 %copy-start.26 = (f32[384,48]{0,1:T(8,128)S(1)}, f32[384,48]{0,1:T(8,128)}, u32[]{:S(2)}) copy-start(f32[384,48]{0,1:T(8,128)} %param.29) | copy-start | bytes 221188
  396.0 63.4 %copy-start.27 = (f32[384,48]{0,1:T(8,128)S(1)}, f32[384,48]{0,1:T(8,128)}, u32[]{:S(2)}) copy-start(f32[384,48]{0,1:T(8,128)} %param.28) | copy-start | bytes 221188
  462.2 16.7 %all-to-all-start = ((f32[32,1,4224]{2,1,0:T(1,128)}), f32[32,1,4224]{2,1,0:T(1,128)}, u32[]{:S(2)}, u32[]{:S(2)}) async-start(f32[32,1,4224]{2,1,0:T(1,128)} %broadcast_in_dim.8), calls=%async_computation.2 | async-start | bytes 1081344 | tf_op jit(solution)/shard_map/all_to_all | solution.py:295
  467.5 94.8 %copy-start.9 = (f32[1728,48]{0,1:T(8,128)S(1)}, f32[1728,48]{0,1:T(8,128)}, u32[]{:S(2)}) copy-start(f32[1728,48]{0,1:T(8,128)} %param.33) | copy-start | bytes 995332
  475.0 325.7 %copy-start.10 = (f32[3,48,384]{2,1,0:T(8,128)S(1)}, f32[3,48,384]{2,1,0:T(8,128)}, u32[]{:S(2)}) copy-start(f32[3,48,384]{2,1,0:T(8,128)} %param.24) | copy-start | bytes 663556
  475.0 325.7 %copy-start.22 = (f32[3,48,384]{2,1,0:T(8,128)S(1)}, f32[3,48,384]{2,1,0:T(8,128)}, u32[]{:S(2)}) copy-start(f32[3,48,384]{2,1,0:T(8,128)} %param.26) | copy-start | bytes 663556
  475.0 325.7 %copy-start.23 = (f32[3,48,384]{2,1,0:T(8,128)S(1)}, f32[3,48,384]{2,1,0:T(8,128)}, u32[]{:S(2)}) copy-start(f32[3,48,384]{2,1,0:T(8,128)} %param.25) | copy-start | bytes 663556
  480.3 321.4 %copy-start.7 = (f32[2,48,1728]{2,1,0:T(8,128)S(1)}, f32[2,48,1728]{2,1,0:T(8,128)}, u32[]{:S(2)}) copy-start(f32[2,48,1728]{2,1,0:T(8,128)} %param.30) | copy-start | bytes 1990660
  480.3 321.4 %copy-start.14 = (f32[2,48,1728]{2,1,0:T(8,128)S(1)}, f32[2,48,1728]{2,1,0:T(8,128)}, u32[]{:S(2)}) copy-start(f32[2,48,1728]{2,1,0:T(8,128)} %param.32) | copy-start | bytes 1990660
  (17 other events, 35.5 us)
Sparse Core Ops, SparseCore 0:
  108.3 40.5 all-gather.1
  153.2 76.8 all-reduce.8
  246.5 130.1 all-reduce.12
  380.1 79.3 reduce-scatter.2
  463.6 98.6 reduce-scatter.4
  566.1 232.3 all-reduce.10

commit v2 on v1

v2 whole, which is shorter than its diff:
```python
import functools

import jax
import jax.numpy as jnp
from jax import lax
from jax.experimental import pallas as pl
from jax.experimental.pallas import tpu as pltpu
from jax.sharding import PartitionSpec as P

MESH = pl.DeviceIdType.MESH
epsilon = 1e-05
momentum = 0.9
average_decay = 0.9
matrix_rate = 0.0004
small_rate = 0.005
WIDTH = 1536
CHANNELS = 384
HIDDEN = 1728
TILE = 256
PADDED = 1792
ROWS = 512
QUARTER = 128
SLOT_ROWS = 256
BLOCK = 48


class Place:
    def __init__(self):
        self.shard = lax.axis_index("shard")
        self.ctx = lax.axis_index("ctx")
        self.tp = lax.axis_index("tp")
        self.y = self.shard * 2 + lax.div(self.ctx, 8)
        self.z = lax.rem(lax.div(self.ctx, 2), 4)
        self.core = lax.rem(self.ctx, 2)
        self.first = self.y * (1 - self.core) + self.z * self.core
        self.second = self.z * (1 - self.core) + self.y * self.core

    def turn(self, value, by):
        return lax.rem(value + by + 4, 4)

    def device(self, y, z, core):
        return (lax.div(y, 2), lax.rem(y, 2) * 8 + z * 2 + core, self.tp)

    def grid_device(self, first, second):
        y = first * (1 - self.core) + second * self.core
        z = second * (1 - self.core) + first * self.core
        return self.device(y, z, self.core)

    def block(self, first, second):
        y = first * (1 - self.core) + second * self.core
        z = second * (1 - self.core) + first * self.core
        return y * 8 + z * 2 + self.core

    def along_first(self, by):
        return self.grid_device(self.turn(self.first, by), self.second)

    def along_second(self, by):
        return self.grid_device(self.first, self.turn(self.second, by))

    def along_tp(self, by):
        return (self.shard, self.ctx, self.turn(self.tp, by))

    def along_ctx(self, by):
        return (self.shard, lax.rem(self.ctx + by + 16, 16), self.tp)

    def sibling(self):
        return self.device(self.y, self.z, 1 - self.core)

    def greet(self):
        barrier = pltpu.get_barrier_semaphore()
        friends = [self.sibling(), self.along_ctx(1), self.along_ctx(-1)]
        for by in (1, 2, 3):
            friends += [self.along_first(by), self.along_second(by), self.along_tp(by)]
        for friend in friends:
            pl.semaphore_signal(barrier, inc=1, device_id=friend, device_id_type=MESH)
        pl.semaphore_wait(barrier, len(friends))


def remote(source, target, sems, at, device):
    return pltpu.make_async_remote_copy(
        src_ref=source,
        dst_ref=target,
        send_sem=sems.at[0, at],
        recv_sem=sems.at[1, at],
        device_id=device,
        device_id_type=MESH,
    )


class Gather:
    SEMS = 31

    def __init__(self, place, local, whole, sems):
        self.place, self.local, self.whole, self.sems = place, local, whole, sems
        self.sent = []

    def part(self, block):
        return self.whole.at[:, block] if self.whole.ndim == 4 else self.whole.at[block]

    def send(self, source, block, at, device):
        copy = remote(source, self.part(block), self.sems, at, device)
        copy.start()
        self.sent.append(copy)

    def arrived(self, block, at):
        spot = self.part(block)
        remote(spot, spot, self.sems, at, self.place.sibling()).wait_recv()

    def start(self):
        p = self.place
        mine = p.block(p.first, p.second)
        for by in (1, 2, 3):
            self.send(self.local, mine, by - 1, p.along_first(by))
        for by in (1, 2, 3):
            self.send(self.local, mine, 3 + by - 1, p.along_second(by))
        self.send(self.local, mine, 15, p.sibling())

    def forward_first(self):
        p = self.place
        for back in (1, 3, 2):
            block = p.block(p.turn(p.first, -back), p.second)
            self.arrived(block, back - 1)
            for by in (1, 2, 3):
                self.send(self.part(block), block, 3 + back * 3 + by - 1, p.along_second(by))
            self.send(self.part(block), block, 15 + back * 4, p.sibling())

    def forward_second(self):
        p = self.place
        for back in (0, 1, 3, 2):
            for by in (1, 3, 2):
                block = p.block(p.turn(p.first, -back), p.turn(p.second, -by))
                self.arrived(block, 3 + back * 3 + by - 1)
                self.send(self.part(block), block, 15 + back * 4 + by, p.sibling())

    def finish(self):
        p = self.place
        for back in range(4):
            for by in range(4):
                self.arrived(p.block(p.turn(p.first, -back), p.turn(p.second, -by)), 15 + back * 4 + by)
        for copy in self.sent:
            copy.wait_send()


class Scatter:
    SEMS = 7

    def __init__(self, place, partial, width, recv, out, stage, sems, local_sems):
        self.place, self.width, self.out = place, width, out
        self.sib_recv, self.second_recv, self.first_recv = recv
        self.stage, self.sems, self.local_sems = stage, sems, local_sems
        columns = pl.ds(0, width)
        self.blocks = partial.reshape(16, 2, BLOCK, PADDED).at[:, :, :, columns]
        self.grid = partial.reshape(4, 4, 2, BLOCK, PADDED).at[:, :, :, :, columns]
        self.sent = []

    def mine(self, first, second):
        return lax.div(self.place.block(first, second), 2)

    def to_sibling(self):
        p = self.place
        copy = remote(self.blocks.at[:, 1 - p.core], self.sib_recv, self.sems, 0, p.sibling())
        copy.start()
        self.sent.append(copy)

    def fetch(self, source, count):
        target = self.stage.at[pl.ds(0, count), :, pl.ds(0, self.width)]
        copy = pltpu.make_async_copy(source, target, self.local_sems.at[0])
        copy.start()
        copy.wait()

    def along_second(self):
        p = self.place
        self.sent[0].wait_recv()
        self.fetch(self.sib_recv, 16)

        @pl.loop(0, 16)
        def _(at):
            both = self.blocks[at, p.core].astype(jnp.float32)
            both = both + self.stage[at, :, : self.width].astype(jnp.float32)
            self.blocks[at, p.core] = both.astype(jnp.bfloat16)

        for by in (1, 3, 2):
            there = p.turn(p.second, by)
            spot = self.second_recv.at[pl.ds((by - 1) * 4, 4)]
            flat = remote(self.grid.at[:, there, 0], spot, self.sems, by, p.along_second(by))
            tall = remote(self.grid.at[there, :, 1], spot, self.sems, by, p.along_second(by))

            @pl.when(p.core == 0)
            def _():
                flat.start()

            @pl.when(p.core == 1)
            def _():
                tall.start()

            self.sent.append(flat)

    def along_first(self):
        p = self.place
        for copy in self.sent[1:4]:
            copy.wait_recv()
        self.fetch(self.second_recv, 12)

        @pl.loop(0, 4)
        def _(first):
            at = self.mine(first, p.second)
            total = self.blocks[at, p.core].astype(jnp.float32)
            for by in range(3):
                total = total + self.stage[by * 4 + first, :, : self.width].astype(jnp.float32)
            self.blocks[at, p.core] = total.astype(jnp.bfloat16)

        for by in (1, 3, 2):
            source = self.blocks.at[self.mine(p.turn(p.first, by), p.second), p.core]
            copy = remote(
                source, self.first_recv.at[by - 1], self.sems, 3 + by, p.along_first(by)
            )
            copy.start()
            self.sent.append(copy)

    def finish(self):
        p = self.place
        for copy in self.sent[4:7]:
            copy.wait_recv()
        total = self.blocks[self.mine(p.first, p.second), p.core].astype(jnp.float32)
        for by in range(3):
            total = total + self.first_recv[by].astype(jnp.float32)
        self.out[...] = total

    def drain(self):
        for copy in self.sent:
            copy.wait_send()


class TpSum:
    def __init__(self, place, send, recv, own, sems):
        self.place, self.send, self.recv, self.own, self.sems = place, send, recv, own, sems
        self.sent = []

    def give(self, values, column, width, slot):
        p = self.place
        columns = pl.ds(column, width)
        self.send[:, columns] = values.astype(jnp.bfloat16)
        for by in (2, 1, 3):
            rows = pl.ds(pl.multiple_of(p.turn(p.tp, by) * QUARTER, QUARTER), QUARTER)
            copy = remote(
                self.send.at[rows, columns],
                self.recv.at[by - 1, :, columns],
                self.sems,
                slot * 3 + by - 1,
                p.along_tp(by),
            )
            copy.start()
            self.sent.append(copy)

    def take(self):
        p = self.place
        for copy in self.sent:
            copy.wait_recv()
        rows = pl.ds(pl.multiple_of(p.tp * QUARTER, QUARTER), QUARTER)
        total = self.send[rows, :].astype(jnp.float32)
        for by in range(3):
            total = total + self.recv[by].astype(jnp.float32)
        return total

    def drain(self):
        for copy in self.sent:
            copy.wait_send()


class TpSpread:
    def __init__(self, place, source, whole, sems):
        self.place, self.source, self.whole, self.sems = place, source, whole, sems
        self.sent = []

    def start(self):
        p = self.place
        rows = pl.ds(pl.multiple_of(p.tp * QUARTER, QUARTER), QUARTER)
        for by in (2, 1, 3):
            copy = remote(self.source, self.whole.at[rows], self.sems, by - 1, p.along_tp(by))
            copy.start()
            self.sent.append(copy)

    def finish(self):
        for copy in self.sent:
            copy.wait_recv()

    def drain(self):
        for copy in self.sent:
            copy.wait_send()


def dot(left, right):
    return jnp.dot(left, right, preferred_element_type=jnp.float32)


def dot_t(left, right):
    return lax.dot_general(
        left, right, (((1,), (1,)), ((), ())), preferred_element_type=jnp.float32
    )


def turned(source, target):
    @pl.loop(0, WIDTH // TILE)
    def _(at):
        at = pl.multiple_of(at * TILE, TILE)
        target[pl.ds(at, TILE), :] = source[:, pl.ds(at, TILE)].T


def own_rows_of(place):
    return pl.ds(pl.multiple_of(place.tp * QUARTER, QUARTER), QUARTER)


def forward_kernel(
    io_local,
    gud_local,
    x,
    gains,
    taps,
    io_full,
    gud_full,
    second_low,
    residual,
    projected,
    product,
    convolved,
    gated,
    input_low,
    x_send,
    x_recv,
    io_sems,
    gud_sems,
    sum_sems,
    spread_sems,
    halo_sems,
    local_sems,
):
    place = Place()
    place.greet()
    mine = place.block(place.first, place.second)
    keep = [
        pltpu.make_async_copy(io_local, io_full.at[mine], local_sems.at[0]),
        pltpu.make_async_copy(gud_local, gud_full.at[:, mine], local_sems.at[1]),
    ]
    for copy in keep:
        copy.start()
    io = Gather(place, io_local, io_full, io_sems)
    gud = Gather(place, gud_local, gud_full, gud_sems)
    io.start()

    @pl.loop(0, ROWS, step=64)
    def _(at):
        values = x[pl.ds(at, 64), :].astype(jnp.float32)
        inverse = lax.rsqrt(jnp.mean(values * values, axis=-1, keepdims=True) + epsilon)
        input_low[pl.ds(at, 64), :] = (values * inverse * gains[0:1, :]).astype(jnp.bfloat16)

    io.forward_first()
    io.forward_second()
    gud.start()
    io.finish()
    keep[0].wait()

    def weight(member):
        return io_full.reshape(WIDTH, 4 * CHANNELS)[:, member * CHANNELS : (member + 1) * CHANNELS]

    for member in (0, 2):
        projected[member] = dot(input_low[...], weight(member))
    product[:, 8:, :] = (projected[0] * projected[2]).reshape(2, SLOT_ROWS, CHANNELS)
    halo = remote(
        product.at[:, pl.ds(SLOT_ROWS, 8)],
        product.at[:, pl.ds(0, 8)],
        halo_sems,
        0,
        place.along_ctx(1),
    )
    halo.start()
    projected[1] = dot(input_low[...], weight(1))
    halo.wait()
    product[:, :8, :] = jnp.where(place.ctx > 0, product[:, :8, :], 0.0)
    convolved[...] = (
        taps[0:1, :] * product[:, 6 : 6 + SLOT_ROWS, :]
        + taps[1:2, :] * product[:, 7 : 7 + SLOT_ROWS, :]
        + taps[2:3, :] * product[:, 8 : 8 + SLOT_ROWS, :]
    ).reshape(ROWS, CHANNELS)
    gated[...] = (projected[1] * convolved[...]).astype(jnp.bfloat16)

    mixed = TpSum(place, x_send, x_recv, None, sum_sems)
    whole = io_full.reshape(WIDTH, 4 * CHANNELS)
    for slot in range(3):
        part = dot_t(gated[...], whole[slot * 512 : (slot + 1) * 512, 3 * CHANNELS :])
        mixed.give(part, slot * 512, 512, slot)
    gud.forward_first()
    own_rows = own_rows_of(place)
    stream = x[own_rows, :].astype(jnp.float32) + mixed.take()
    residual[...] = stream
    inverse = lax.rsqrt(jnp.mean(stream * stream, axis=-1, keepdims=True) + epsilon)
    second_low[own_rows, :] = (stream * inverse * gains[1:2, :]).astype(jnp.bfloat16)
    spread = TpSpread(place, second_low.at[own_rows], second_low, spread_sems)
    spread.start()
    gud.forward_second()
    gud.finish()
    keep[1].wait()
    spread.finish()
    spread.drain()
    mixed.drain()


def forward(io_local, gud_local, x, gains, taps):
    vmem = pl.BlockSpec(memory_space=pltpu.VMEM)
    hbm = pl.BlockSpec(memory_space=pl.ANY)
    f32, b16 = jnp.float32, jnp.bfloat16
    return pl.pallas_call(
        forward_kernel,
        out_shape=(
            jax.ShapeDtypeStruct((32, BLOCK, 4 * CHANNELS), b16),
            jax.ShapeDtypeStruct((3, 32, BLOCK, PADDED), b16),
            jax.ShapeDtypeStruct((ROWS, WIDTH), b16),
            jax.ShapeDtypeStruct((QUARTER, WIDTH), f32),
            jax.ShapeDtypeStruct((3, ROWS, CHANNELS), f32),
            jax.ShapeDtypeStruct((2, 8 + SLOT_ROWS, CHANNELS), f32),
            jax.ShapeDtypeStruct((ROWS, CHANNELS), f32),
            jax.ShapeDtypeStruct((ROWS, CHANNELS), b16),
            jax.ShapeDtypeStruct((ROWS, WIDTH), b16),
        ),
        in_specs=[hbm, hbm, vmem, vmem, vmem],
        out_specs=(vmem, hbm, vmem, vmem, vmem, vmem, vmem, vmem, vmem),
        scratch_shapes=[
            pltpu.VMEM((ROWS, WIDTH), b16),
            pltpu.VMEM((3, QUARTER, WIDTH), b16),
            pltpu.SemaphoreType.DMA((2, Gather.SEMS)),
            pltpu.SemaphoreType.DMA((2, Gather.SEMS)),
            pltpu.SemaphoreType.DMA((2, 9)),
            pltpu.SemaphoreType.DMA((2, 3)),
            pltpu.SemaphoreType.DMA((2, 1)),
            pltpu.SemaphoreType.DMA((2,)),
        ],
        compiler_params=pltpu.CompilerParams(
            collective_id=0, has_side_effects=True, vmem_limit_bytes=56 * 2**20
        ),
        name="forward",
    )(io_local, gud_local, x, gains, taps)


def backward_kernel(
    io_full,
    gud_full,
    input_low,
    x,
    cotangent,
    second_low,
    residual,
    projected,
    product,
    convolved,
    gated,
    valid,
    gains,
    taps,
    block_out,
    input_out,
    sib_hbm,
    second_hbm,
    io_sib_hbm,
    io_second_hbm,
    io_grad,
    gud_grad,
    small,
    weights,
    io,
    big,
    grad_proj,
    grad_low,
    x_own,
    turn_a,
    turn_b,
    send_a,
    send_b,
    recv_a,
    recv_b,
    recv_c,
    low_full,
    grad_own,
    block_own,
    input_own,
    conv_grad,
    stage,
    first_recv,
    io_first_recv,
    small_recv,
    weight_sems,
    scatter_sems,
    sum_sems,
    spread_sems,
    halo_sems,
    small_sems,
    local_sems,
):
    f32, b16 = jnp.float32, jnp.bfloat16
    place = Place()
    own_rows = own_rows_of(place)
    tiles = PADDED // TILE
    flat_in = gud_full.reshape(3, WIDTH, PADDED)

    def tile_copy(at):
        columns = pl.ds(pl.multiple_of(at * TILE, TILE), TILE)
        return pltpu.make_async_copy(
            flat_in.at[:, :, columns], weights.at[:, :, columns], weight_sems.at[at]
        )

    io_copy = pltpu.make_async_copy(
        io_full.reshape(WIDTH, 4 * CHANNELS), io, local_sems.at[1]
    )
    low_copy = pltpu.make_async_copy(cotangent, grad_low, local_sems.at[3])
    x_copy = pltpu.make_async_copy(x.at[own_rows], x_own, local_sems.at[4])
    low_copy.start()
    for at in range(tiles):
        tile_copy(at).start()
    io_copy.start()
    x_copy.start()
    place.greet()
    low_copy.wait()
    grad_low[...] = (grad_low[...].astype(f32) * valid[...]).astype(b16)

    @pl.loop(0, tiles)
    def _(at):
        tile_copy(at).wait()
        columns = pl.ds(pl.multiple_of(at * TILE, TILE), TILE)
        gate = dot(second_low[...], weights[0, :, columns])
        up = dot(second_low[...], weights[1, :, columns])
        grad_inner = dot(grad_low[...], weights[2, :, columns])
        sigmoid = jax.nn.sigmoid(gate)
        active = gate * sigmoid
        big[0:ROWS, columns] = (active * up).astype(b16)
        big[ROWS : 2 * ROWS, columns] = (
            grad_inner * up * sigmoid * (1.0 + gate * (1.0 - sigmoid))
        ).astype(b16)
        big[2 * ROWS :, columns] = (grad_inner * active).astype(b16)

    branch = TpSum(place, send_a, recv_a, None, sum_sems.at[0])
    for slot in range(3):
        part = dot_t(big[0:ROWS, :], weights[2, slot * 512 : (slot + 1) * 512, :])
        branch.give(part, slot * 512, 512, slot)
    second = TpSum(place, send_b, recv_b, None, sum_sems.at[1])
    for slot in range(3):
        rows = slice(slot * 512, (slot + 1) * 512)
        part = dot_t(big[ROWS : 2 * ROWS, :], weights[0, rows, :])
        part = part + dot_t(big[2 * ROWS :, :], weights[1, rows, :])
        second.give(part, slot * 512, 512, slot)

    def gradient(left, at, member):
        @pl.loop(0, tiles)
        def _(tile):
            columns = pl.ds(pl.multiple_of(tile * TILE, TILE), TILE)
            weights[at, :, columns] = dot(
                left[...], big[member * ROWS : (member + 1) * ROWS, columns]
            ).astype(b16)

    def piece(at):
        return Scatter(
            place,
            weights.at[at],
            PADDED,
            (sib_hbm.at[at], second_hbm.at[at], first_recv.at[at]),
            gud_grad.at[at],
            stage,
            scatter_sems.at[at],
            local_sems,
        )

    gate_piece, up_piece, down_piece = piece(0), piece(1), piece(2)
    turned(grad_low, turn_a)
    gradient(turn_a, 2, 0)
    down_piece.to_sibling()
    turned(second_low, turn_b)
    gradient(turn_b, 0, 1)
    gate_piece.to_sibling()
    down_piece.along_second()
    gradient(turn_b, 1, 2)
    up_piece.to_sibling()
    gate_piece.along_second()

    stream = residual[...]
    block_own[...] = (stream + branch.take()).astype(b16)
    branch.drain()

    def norm_of(values):
        inverse = lax.rsqrt(jnp.mean(values * values, axis=-1, keepdims=True) + epsilon)
        return values * inverse, inverse

    normed, inverse = norm_of(stream)
    grad_second = second.take()
    small[...] = jnp.zeros_like(small)
    small[1:2, :] = jnp.sum(grad_second * normed, axis=0, keepdims=True)
    scaled = grad_second * gains[1:2, :]
    grad_stream = grad_low[own_rows, :].astype(f32) + inverse * (
        scaled - normed * jnp.mean(scaled * normed, axis=-1, keepdims=True)
    )
    grad_own[...] = grad_stream
    low_full[own_rows, :] = grad_stream.astype(b16)
    low_spread = TpSpread(place, low_full.at[own_rows], low_full, spread_sems.at[0])
    low_spread.start()
    block_keep = pltpu.make_async_copy(block_own, block_out.at[own_rows], local_sems.at[2])
    block_keep.start()
    block_spread = TpSpread(place, block_own, block_out, spread_sems.at[1])
    block_spread.start()
    up_piece.along_second()
    second.drain()
    input_copy = pltpu.make_async_copy(input_low, send_b, local_sems.at[5])
    input_copy.start()
    down_piece.along_first()
    gate_piece.along_first()
    low_spread.finish()
    io_copy.wait()

    grad_gated = dot(low_full[...], io[:, 3 * CHANNELS :])
    conv_grad[:, :SLOT_ROWS, :] = (grad_gated * projected[1]).reshape(2, SLOT_ROWS, CHANNELS)
    halo = remote(
        conv_grad.at[:, pl.ds(0, 8)],
        conv_grad.at[:, pl.ds(SLOT_ROWS, 8)],
        halo_sems,
        0,
        place.along_ctx(-1),
    )
    halo.start()
    grad_proj[:, CHANNELS : 2 * CHANNELS] = (grad_gated * convolved[...]).astype(b16)
    own_columns = pl.ds(pl.multiple_of(place.tp * CHANNELS, QUARTER), CHANNELS)
    for tap in range(3):
        small[2 + tap : 3 + tap, own_columns] = jnp.sum(
            conv_grad[:, :SLOT_ROWS, :] * product[:, 6 + tap : 6 + tap + SLOT_ROWS, :], axis=(0, 1)
        ).reshape(1, CHANNELS)
    halo.wait()
    conv_grad[:, SLOT_ROWS:, :] = jnp.where(place.ctx < 15, conv_grad[:, SLOT_ROWS:, :], 0.0)
    grad_product = (
        taps[2:3, :] * conv_grad[:, 0:SLOT_ROWS, :]
        + taps[1:2, :] * conv_grad[:, 1 : 1 + SLOT_ROWS, :]
        + taps[0:1, :] * conv_grad[:, 2 : 2 + SLOT_ROWS, :]
    ).reshape(ROWS, CHANNELS)
    grad_proj[:, 0:CHANNELS] = (grad_product * projected[2]).astype(b16)
    grad_proj[:, 2 * CHANNELS : 3 * CHANNELS] = (grad_product * projected[0]).astype(b16)
    first = TpSum(place, send_a, recv_c, None, sum_sems.at[2])
    for slot in range(3):
        part = dot_t(
            grad_proj[...], io[slot * 512 : (slot + 1) * 512, : 3 * CHANNELS]
        )
        first.give(part, slot * 512, 512, slot)

    input_copy.wait()
    turned(send_b, turn_a)
    turned(low_full, turn_b)
    for member in range(3):
        columns = slice(member * CHANNELS, (member + 1) * CHANNELS)
        big[:, columns] = dot(turn_a[...], grad_proj[:, columns]).astype(b16)
    big[:, 3 * CHANNELS : 4 * CHANNELS] = dot(turn_b[...], gated[...]).astype(b16)
    io_piece = Scatter(
        place,
        big,
        4 * CHANNELS,
        (io_sib_hbm, io_second_hbm, io_first_recv),
        io_grad,
        stage,
        scatter_sems.at[3],
        local_sems,
    )
    io_piece.to_sibling()
    up_piece.along_first()
    io_piece.along_second()

    x_copy.wait()
    normed, inverse = norm_of(x_own[...].astype(f32))
    grad_first = first.take()
    small[0:1, :] = jnp.sum(grad_first * normed, axis=0, keepdims=True)
    scaled = grad_first * gains[0:1, :]
    input_own[...] = (
        grad_own[...]
        + inverse * (scaled - normed * jnp.mean(scaled * normed, axis=-1, keepdims=True))
    ).astype(b16)
    input_keep = pltpu.make_async_copy(input_own, input_out.at[own_rows], local_sems.at[6])
    input_keep.start()
    input_spread = TpSpread(place, input_own, input_out, spread_sems.at[2])
    input_spread.start()

    def exchange(start, devices):
        copies = [
            remote(small, small_recv.at[start + at], small_sems, start + at, device)
            for at, device in enumerate(devices)
        ]
        for copy in copies:
            copy.start()
        for copy in copies:
            copy.wait()
        total = small[...]
        for at in range(len(devices)):
            total = total + small_recv[start + at]
        small[...] = total

    exchange(0, [place.sibling()])
    io_piece.along_first()
    exchange(1, [place.along_tp(by) for by in (1, 2, 3)])
    down_piece.finish()
    gate_piece.finish()
    exchange(4, [place.along_first(by) for by in (1, 2, 3)])
    up_piece.finish()
    exchange(7, [place.along_second(by) for by in (1, 2, 3)])
    io_piece.finish()
    block_keep.wait()
    input_keep.wait()
    block_spread.finish()
    input_spread.finish()
    for part in (low_spread, block_spread, input_spread, first):
        part.drain()
    for part in (down_piece, gate_piece, up_piece, io_piece):
        part.drain()


def backward(*given):
    vmem = pl.BlockSpec(memory_space=pltpu.VMEM)
    hbm = pl.BlockSpec(memory_space=pl.ANY)
    f32, b16 = jnp.float32, jnp.bfloat16
    dma = pltpu.SemaphoreType.DMA
    return pl.pallas_call(
        backward_kernel,
        out_shape=(
            jax.ShapeDtypeStruct((ROWS, WIDTH), b16),
            jax.ShapeDtypeStruct((ROWS, WIDTH), b16),
            jax.ShapeDtypeStruct((3, 16, BLOCK, PADDED), b16),
            jax.ShapeDtypeStruct((3, 12, BLOCK, PADDED), b16),
            jax.ShapeDtypeStruct((16, BLOCK, 4 * CHANNELS), b16),
            jax.ShapeDtypeStruct((12, BLOCK, 4 * CHANNELS), b16),
            jax.ShapeDtypeStruct((BLOCK, 4 * CHANNELS), f32),
            jax.ShapeDtypeStruct((3, BLOCK, PADDED), f32),
            jax.ShapeDtypeStruct((8, WIDTH), f32),
        ),
        in_specs=[hbm] * 5 + [vmem] * 9,
        out_specs=(hbm,) * 6 + (vmem,) * 3,
        scratch_shapes=[
            pltpu.VMEM((3, WIDTH, PADDED), b16),
            pltpu.VMEM((WIDTH, 4 * CHANNELS), b16),
            pltpu.VMEM((WIDTH, PADDED), b16),
            pltpu.VMEM((ROWS, 3 * CHANNELS), b16),
            pltpu.VMEM((ROWS, WIDTH), b16),
            pltpu.VMEM((QUARTER, WIDTH), b16),
            pltpu.VMEM((WIDTH, ROWS), b16),
            pltpu.VMEM((WIDTH, ROWS), b16),
            pltpu.VMEM((ROWS, WIDTH), b16),
            pltpu.VMEM((ROWS, WIDTH), b16),
            pltpu.VMEM((3, QUARTER, WIDTH), b16),
            pltpu.VMEM((3, QUARTER, WIDTH), b16),
            pltpu.VMEM((3, QUARTER, WIDTH), b16),
            pltpu.VMEM((ROWS, WIDTH), b16),
            pltpu.VMEM((QUARTER, WIDTH), f32),
            pltpu.VMEM((QUARTER, WIDTH), b16),
            pltpu.VMEM((QUARTER, WIDTH), b16),
            pltpu.VMEM((2, SLOT_ROWS + 8, CHANNELS), f32),
            pltpu.VMEM((16, BLOCK, PADDED), b16),
            pltpu.VMEM((3, 3, BLOCK, PADDED), b16),
            pltpu.VMEM((3, BLOCK, 4 * CHANNELS), b16),
            pltpu.VMEM((10, 8, WIDTH), f32),
            dma((PADDED // TILE,)),
            dma((4, 2, Scatter.SEMS)),
            dma((3, 2, 9)),
            dma((3, 2, 3)),
            dma((2, 1)),
            dma((2, 10)),
            dma((7,)),
        ],
        compiler_params=pltpu.CompilerParams(
            collective_id=1, has_side_effects=True, vmem_limit_bytes=62 * 2**20
        ),
        name="backward",
    )(*given)


def nesterov(weight, moment, average, gradient, step_rate):
    moment_new = momentum * moment + gradient
    weight_new = weight - step_rate * (gradient + momentum * moment_new)
    average_new = average_decay * average + (1.0 - average_decay) * weight_new
    return (moment_new, weight_new, average_new)


def on_device(
    hidden,
    lengths,
    cotangent,
    in_weight,
    in_moment,
    in_average,
    out_weight,
    out_moment,
    out_average,
    gate_up_weight,
    gate_up_moment,
    gate_up_average,
    down_weight,
    down_moment,
    down_average,
    norm_gains,
    gain_moment,
    gain_average,
    conv_taps,
    taps_moment,
    taps_average,
):
    b16 = jnp.bfloat16
    io_local = jnp.concatenate(
        [in_weight[0], in_weight[1], in_weight[2], out_weight.T], axis=1
    ).astype(b16)
    gud_local = jnp.pad(
        jnp.concatenate([gate_up_weight, down_weight.T[None]], axis=0).astype(b16),
        ((0, 0), (0, 0), (0, PADDED - HIDDEN)),
    )
    slot_count, seq_len, model_width = hidden.shape
    row_count = slot_count * seq_len
    x = hidden.reshape(row_count, model_width)
    positions = lax.axis_index("ctx") * seq_len + jnp.arange(seq_len, dtype=jnp.int32)
    valid_rows = (positions[None, :] < lengths[:, None]).astype(jnp.float32).reshape(row_count, 1)
    (
        io_full,
        gud_full,
        second_low,
        residual,
        projected,
        product,
        convolved,
        gated,
        input_low,
    ) = forward(io_local, gud_local, x, norm_gains, conv_taps)
    block_output, input_low_grad, _, _, _, _, io_sum, gud_sum, small = backward(
        io_full,
        gud_full,
        input_low,
        x,
        cotangent.reshape(row_count, model_width),
        second_low,
        residual,
        projected,
        product,
        convolved,
        gated,
        valid_rows,
        norm_gains,
        conv_taps,
    )
    block_output = block_output.reshape(slot_count, seq_len, model_width)
    input_grad = input_low_grad.astype(jnp.float32).reshape(slot_count, seq_len, model_width)
    in_sum = jnp.moveaxis(io_sum[:, : 3 * CHANNELS].reshape(BLOCK, 3, CHANNELS), 1, 0)
    out_sum = io_sum[:, 3 * CHANNELS :].T
    gate_up_sum = gud_sum[:2, :, :HIDDEN]
    down_sum = gud_sum[2, :, :HIDDEN].T
    gain_total = small[:2]
    taps_total = lax.dynamic_slice_in_dim(
        small[2:5], lax.axis_index("tp") * CHANNELS, CHANNELS, axis=1
    )
    in_new = nesterov(in_weight, in_moment, in_average, in_sum, matrix_rate)
    out_new = nesterov(out_weight, out_moment, out_average, out_sum, matrix_rate)
    gate_up_new = nesterov(
        gate_up_weight, gate_up_moment, gate_up_average, gate_up_sum, matrix_rate
    )
    down_new = nesterov(down_weight, down_moment, down_average, down_sum, matrix_rate)
    gain_new = nesterov(norm_gains, gain_moment, gain_average, gain_total, small_rate)
    taps_new = nesterov(conv_taps, taps_moment, taps_average, taps_total, small_rate)
    return (
        block_output,
        input_grad,
        in_new[0],
        in_new[1],
        in_new[2],
        out_new[0],
        out_new[1],
        out_new[2],
        gate_up_new[0],
        gate_up_new[1],
        gate_up_new[2],
        down_new[0],
        down_new[1],
        down_new[2],
        gain_new[0],
        gain_new[1],
        gain_new[2],
        taps_new[0],
        taps_new[1],
        taps_new[2],
    )


def solution(mesh):
    placed = (
        P("shard", "ctx", None),
        P("shard"),
        P("shard", "ctx", None),
        P(None, ("shard", "ctx"), "tp"),
        P(None, ("shard", "ctx"), "tp"),
        P(None, ("shard", "ctx"), "tp"),
        P("tp", ("shard", "ctx")),
        P("tp", ("shard", "ctx")),
        P("tp", ("shard", "ctx")),
        P(None, ("shard", "ctx"), "tp"),
        P(None, ("shard", "ctx"), "tp"),
        P(None, ("shard", "ctx"), "tp"),
        P("tp", ("shard", "ctx")),
        P("tp", ("shard", "ctx")),
        P("tp", ("shard", "ctx")),
        P(),
        P(),
        P(),
        P(None, "tp"),
        P(None, "tp"),
        P(None, "tp"),
    )
    return jax.shard_map(
        on_device,
        mesh=mesh,
        in_specs=placed,
        out_specs=(
            P("shard", "ctx", None),
            P("shard", "ctx", None),
            P(None, ("shard", "ctx"), "tp"),
            P(None, ("shard", "ctx"), "tp"),
            P(None, ("shard", "ctx"), "tp"),
            P("tp", ("shard", "ctx")),
            P("tp", ("shard", "ctx")),
            P("tp", ("shard", "ctx")),
            P(None, ("shard", "ctx"), "tp"),
            P(None, ("shard", "ctx"), "tp"),
            P(None, ("shard", "ctx"), "tp"),
            P("tp", ("shard", "ctx")),
            P("tp", ("shard", "ctx")),
            P("tp", ("shard", "ctx")),
            P(),
            P(),
            P(),
            P(None, "tp"),
            P(None, "tp"),
            P(None, "tp"),
        ),
        check_vma=False,
    )
```

time: 819 us -> 267 us (0.33)
  waiting for transfers between devices: 506 us -> 0 us
  Pallas kernels: 95.4 us -> 247 us
  matrix products: 73.1 us -> 0 us
  local copies, waits for them, and re-layouts: 74.4 us -> 4.56 us
  other arithmetic: 39.1 us -> 14.4 us
  between operations: 15.7 us -> 0.93 us
    unnamed x7 -> x0, waiting for transfers between devices: 234 us -> none
    pallas_call x1 -> x2, Pallas kernels: 95.4 us -> 247 us  [the longest x1 152 us: backward(): pl.pallas_call(backward_kernel, out_shape=(jax.ShapeDtypeStruct((ROWS, WI...]
    reduce_scatter x2 -> x0, waiting for transfers between devices: 141 us -> none  [the longest x1 79.2 us: on_device(): lax.psum_scatter(down_grad, ('shard', 'ctx'), scatter_dimension=1, tiled=...]
    psum x2 -> x0, waiting for transfers between devices: 126 us -> none  [the longest x1 67.3 us: on_device(): lax.psum(jnp.dot(inner_low, down_full, preferred_element_type=jnp.float32...]
    dot_general x10 -> x0, matrix products: 73.1 us -> none  [the longest x2 13.4 us: contract_rows(): lax.dot_general(left_side, right_side, (((0,), (0,)), ((), ())), preferre...]
    transpose x2 -> x0, local copies, waits for them, and re-layouts: 43.5 us -> none  [the longest x1 32.6 us: on_device(): jnp.einsum('rd,krf->kdf', second_low, grad_gate_up, preferred_element_typ...]
    slice x10 -> x2, local copies, waits for them, and re-layouts: 22.5 us -> 1.9 us  [the longest x1 0.95 us: on_device(): io_sum[:, :3 * CHANNELS].reshape(BLOCK, 3, CHANNELS)]
    reduce_sum x5 -> x0, other arithmetic: 12.3 us -> none  [the longest x2 4.11 us: normalize(): jnp.mean(values * values, axis=-1, keepdims=True) + epsilon]
  transfers between devices with their start and end apart: 8 -> 0, of which waited for: 7 -> 0; matrix products, arithmetic and copies ran while one was open for 20% -> 0% of each run, Pallas kernels for 0% -> 0%
where the time goes in v2:
time: 267 us
  Pallas kernels  247 us (93%)
  other arithmetic  14.4 us (5%)
  local copies, waits for them, and re-layouts  4.56 us (2%)
    pallas_call x1, Pallas kernels, backward(): pl.pallas_call(backward_kernel, out_shape=(jax.ShapeDtypeStruct((ROWS, WI...  152 us
    pallas_call x1, Pallas kernels, forward(): pl.pallas_call(forward_kernel, out_shape=(jax.ShapeDtypeStruct((32, BLOCK...  95.4 us
    add x6, other arithmetic, nesterov(): average_new = average_decay * average + (1.0 - average_decay) * weight_new  7.12 us

profile of v2, /device:TPU:0, one launch (start us, length us, event | category | flops | bytes accessed | tf_op | source)
XLA Modules:
  0.0 266.8 jit_solution(4046640799847702909)
XLA Ops:
  0.7 0.8 fusion.11
  1.5 0.9 convert_bitcast_fusion.1
  2.4 0.9 convert.25
  3.3 0.7 pad_maximum_fusion.io_local
  4.0 1.0 convert_bitcast_fusion
  5.0 0.9 copy.53
  5.9 0.8 fusion.2.gud_local
  6.8 95.4 %forward.1 = (bf16[32,48,1536]{2,1,0:T(8,128)(2,1)}, bf16[3,32,48,1792]{3,2,1,0:T(8,128)(2,1)}, bf16[512,1536]{1,0:T(8,128)(2,1)}, f32[128,1536]{1,0:T(8,128)}, ...) custom-call(bf16[48,1536]{1,0:T(8,128)(2,1)} %pad_maximum_fusion.io_, ...), custom_call_target="tpu_custom_call" | custom-call | tf_op jit(solution)/shard_map/forward/pallas_call | solution.py:411
  102.2 0.0 copy-start.13
  102.2 0.0 copy-start.17
  102.2 0.0 copy-start.18
  102.2 0.0 copy-start.16
  102.2 0.0 copy-start.19
  102.2 0.0 copy-start.20
  102.3 0.0 copy-start.10
  102.3 0.0 copy-start.14
  102.3 0.0 copy-start.15
  102.3 0.0 copy-start.12
  102.3 151.5 %backward.1 = (bf16[512,1536]{1,0:T(8,128)(2,1)}, bf16[512,1536]{1,0:T(8,128)(2,1)}, bf16[3,16,48,1792]{3,2,1,0:T(8,128)(2,1)}, bf16[3,12,48,1792]{3,2,1,0:T(8,1...) custom-call(bf16[32,48,1536]{2,1,0:T(8,128)(2,1)} %get-tuple-element, ...), custom_call_target="tpu_custom_call" | custom-call | tf_op jit(solution)/shard_map/backward/pallas_call | solution.py:719
  253.8 0.0 copy-start.3
  253.9 0.9 slice.38
  254.9 1.4 multiply_add_fusion.5
  256.3 0.6 multiply_add_fusion.7
  256.9 0.9 slice.33
  257.9 1.6 multiply_add_fusion.4
  259.5 0.0 copy-start.7
  259.5 0.9 multiply_add_fusion.3
  260.5 1.1 multiply_add_fusion.2
  261.5 1.5 multiply_add_fusion
  263.0 0.5 copy-done.2
  263.6 2.1 convert.29
  265.6 1.1 copy.59
  (33 shorter events, 0.1 us)
Async XLA Ops:
  0.7 5.2 %copy-start = (f32[2,48,1728]{2,1,0:T(8,128)S(1)}, f32[2,48,1728]{2,1,0:T(8,128)}, u32[]{:S(2)}) copy-start(f32[2,48,1728]{2,1,0:T(8,128)} %param.30) | copy-start | bytes 1990660
  102.2 152.7 %copy-start.13 = (f32[2,1536]{1,0:T(2,128)S(1)}, f32[2,1536]{1,0:T(2,128)}, u32[]{:S(2)}) copy-start(f32[2,1536]{1,0:T(2,128)} %gains.3) | copy-start | bytes 36868
  102.2 152.6 %copy-start.17 = (f32[2,1536]{1,0:T(2,128)S(1)}, f32[2,1536]{1,0:T(2,128)}, u32[]{:S(2)}) copy-start(f32[2,1536]{1,0:T(2,128)} %param.38) | copy-start | bytes 36868
  102.2 152.6 %copy-start.18 = (f32[2,1536]{1,0:T(2,128)S(1)}, f32[2,1536]{1,0:T(2,128)}, u32[]{:S(2)}) copy-start(f32[2,1536]{1,0:T(2,128)} %param.37) | copy-start | bytes 36868
  102.2 154.1 %copy-start.16 = (f32[3,384]{1,0:T(4,128)S(1)}, f32[3,384]{1,0:T(4,128)}, u32[]{:S(2)}) copy-start(f32[3,384]{1,0:T(4,128)} %taps.3) | copy-start | bytes 13828
  102.2 154.1 %copy-start.19 = (f32[3,384]{1,0:T(4,128)S(1)}, f32[3,384]{1,0:T(4,128)}, u32[]{:S(2)}) copy-start(f32[3,384]{1,0:T(4,128)} %param.41) | copy-start | bytes 13828
  102.2 154.1 %copy-start.20 = (f32[3,384]{1,0:T(4,128)S(1)}, f32[3,384]{1,0:T(4,128)}, u32[]{:S(2)}) copy-start(f32[3,384]{1,0:T(4,128)} %param.40) | copy-start | bytes 13828
  102.3 155.6 %copy-start.10 = (f32[384,48]{0,1:T(8,128)S(1)}, f32[384,48]{0,1:T(8,128)}, u32[]{:S(2)}) copy-start(f32[384,48]{0,1:T(8,128)} %param.27) | copy-start | bytes 221188
  102.3 155.6 %copy-start.14 = (f32[384,48]{0,1:T(8,128)S(1)}, f32[384,48]{0,1:T(8,128)}, u32[]{:S(2)}) copy-start(f32[384,48]{0,1:T(8,128)} %param.29) | copy-start | bytes 221188
  102.3 155.6 %copy-start.15 = (f32[384,48]{0,1:T(8,128)S(1)}, f32[384,48]{0,1:T(8,128)}, u32[]{:S(2)}) copy-start(f32[384,48]{0,1:T(8,128)} %param.28) | copy-start | bytes 221188
  102.3 157.2 %copy-start.5 = (f32[3,48,384]{2,1,0:T(8,128)S(1)}, f32[3,48,384]{2,1,0:T(8,128)}, u32[]{:S(2)}) copy-start(f32[3,48,384]{2,1,0:T(8,128)} %param.24) | copy-start | bytes 663556
  102.3 157.2 %copy-start.11 = (f32[3,48,384]{2,1,0:T(8,128)S(1)}, f32[3,48,384]{2,1,0:T(8,128)}, u32[]{:S(2)}) copy-start(f32[3,48,384]{2,1,0:T(8,128)} %param.26) | copy-start | bytes 663556
  102.3 157.2 %copy-start.12 = (f32[3,48,384]{2,1,0:T(8,128)S(1)}, f32[3,48,384]{2,1,0:T(8,128)}, u32[]{:S(2)}) copy-start(f32[3,48,384]{2,1,0:T(8,128)} %param.25) | copy-start | bytes 663556
  253.8 6.6 %copy-start.3 = (f32[1728,48]{0,1:T(8,128)S(1)}, f32[1728,48]{0,1:T(8,128)}, u32[]{:S(2)}) copy-start(f32[1728,48]{0,1:T(8,128)} %param.33) | copy-start | bytes 995332
  253.9 6.6 %copy-start.4 = (f32[3,48,1792]{2,1,0:T(8,128)S(1)}, f32[3,48,1792]{2,1,0:T(8,128)}, u32[]{:S(2)}) copy-start(f32[3,48,1792]{2,1,0:T(8,128)} %get-tuple-element.46) | copy-start | bytes 3096580
  253.9 6.6 %copy-start.8 = (f32[1728,48]{0,1:T(8,128)S(1)}, f32[1728,48]{0,1:T(8,128)}, u32[]{:S(2)}) copy-start(f32[1728,48]{0,1:T(8,128)} %param.35) | copy-start | bytes 995332
  253.9 6.6 %copy-start.9 = (f32[1728,48]{0,1:T(8,128)S(1)}, f32[1728,48]{0,1:T(8,128)}, u32[]{:S(2)}) copy-start(f32[1728,48]{0,1:T(8,128)} %param.34) | copy-start | bytes 995332
  259.5 2.0 copy-start.6
  259.5 2.0 copy-start.7
  261.5 2.0 copy-start.2
  263.6 2.1 copy-start.1

commit v3 on v2

v3 whole, which is shorter than its diff:
```python
import functools

import jax
import jax.numpy as jnp
from jax import lax
from jax.experimental import pallas as pl
from jax.experimental.pallas import tpu as pltpu
from jax.sharding import PartitionSpec as P

MESH = pl.DeviceIdType.MESH
epsilon = 1e-05
momentum = 0.9
average_decay = 0.9
matrix_rate = 0.0004
small_rate = 0.005
WIDTH = 1536
CHANNELS = 384
HIDDEN = 1728
TILE = 256
EDGE = 16
WIDE = 4 * CHANNELS
PADDED = 1792
ROWS = 512
QUARTER = 128
SLOT_ROWS = 256
BLOCK = 48
HALF = QUARTER // 2


class Place:
    def __init__(self):
        self.shard = lax.axis_index("shard")
        self.ctx = lax.axis_index("ctx")
        self.tp = lax.axis_index("tp")
        self.y = self.shard * 2 + lax.div(self.ctx, 8)
        self.z = lax.rem(lax.div(self.ctx, 2), 4)
        self.core = lax.rem(self.ctx, 2)
        self.first = self.y * (1 - self.core) + self.z * self.core
        self.second = self.z * (1 - self.core) + self.y * self.core

    def turn(self, value, by):
        return lax.rem(value + by + 4, 4)

    def device(self, y, z, core):
        return (lax.div(y, 2), lax.rem(y, 2) * 8 + z * 2 + core, self.tp)

    def grid_device(self, first, second):
        y = first * (1 - self.core) + second * self.core
        z = second * (1 - self.core) + first * self.core
        return self.device(y, z, self.core)

    def block(self, first, second):
        y = first * (1 - self.core) + second * self.core
        z = second * (1 - self.core) + first * self.core
        return y * 8 + z * 2 + self.core

    def along_first(self, by):
        return self.grid_device(self.turn(self.first, by), self.second)

    def along_second(self, by):
        return self.grid_device(self.first, self.turn(self.second, by))

    def along_tp(self, by):
        return (self.shard, self.ctx, self.turn(self.tp, by))

    def along_ctx(self, by, tp=None):
        return (self.shard, lax.rem(self.ctx + by + 16, 16), self.tp if tp is None else tp)

    def sibling(self):
        return self.device(self.y, self.z, 1 - self.core)

    def greet(self):
        barrier = pltpu.get_barrier_semaphore()
        friends = [self.sibling()]
        for tp in range(4):
            friends += [self.along_ctx(1, tp), self.along_ctx(-1, tp)]
        for by in (1, 2, 3):
            friends += [self.along_first(by), self.along_second(by), self.along_tp(by)]
        for friend in friends:
            pl.semaphore_signal(barrier, inc=1, device_id=friend, device_id_type=MESH)
        pl.semaphore_wait(barrier, len(friends))


def remote(source, target, sems, at, device):
    return pltpu.make_async_remote_copy(
        src_ref=source,
        dst_ref=target,
        send_sem=sems.at[0, at],
        recv_sem=sems.at[1, at],
        device_id=device,
        device_id_type=MESH,
    )


class Gather:
    SEMS = 36

    def __init__(self, place, local, whole, sems):
        self.place, self.local, self.whole, self.sems = place, local, whole, sems
        self.half = local.shape[-1] // 2
        self.sent = []

    def part(self, block, half=None):
        spot = self.whole.at[:, block] if self.whole.ndim == 4 else self.whole.at[block]
        if half is None:
            return spot
        columns = pl.ds(half * self.half, self.half)
        return spot.at[:, :, columns] if self.whole.ndim == 4 else spot.at[:, columns]

    def send(self, source, target, at, device):
        copy = remote(source, target, self.sems, at, device)
        copy.start()
        self.sent.append(copy)

    def arrived(self, spot, at):
        remote(spot, spot, self.sems, at, self.place.sibling()).wait_recv()

    def block(self, back, by):
        p = self.place
        return p.block(p.turn(p.first, -back), p.turn(p.second, -by))

    def to_second(self, source, back, by):
        spot = self.part(self.block(back, 0))
        self.send(source, spot, 4 + 4 * back, self.place.along_second(1))
        self.send(source, spot, 5 + 4 * back, self.place.along_second(-1))
        self.to_sibling(source, back, by)

    def to_sibling(self, source, back, by):
        spot = self.part(self.block(back, by))
        self.send(source, spot, 20 + 4 * back + by, self.place.sibling())

    def start(self):
        p = self.place
        spot = self.part(self.block(0, 0))
        self.send(self.local, spot, 0, p.along_first(1))
        self.send(self.local, spot, 1, p.along_first(-1))
        self.to_second(self.local, 0, 0)

    def first(self):
        p = self.place
        for back, at, half, by in ((1, 0, 0, 1), (3, 1, 1, -1)):
            block = self.block(back, 0)
            self.arrived(self.part(block), at)
            piece = self.part(block, half)
            self.send(piece, piece, 2 + half, p.along_first(by))
            self.to_second(self.part(block), back, 0)

    def first_far(self):
        block = self.block(2, 0)
        for half in range(2):
            self.arrived(self.part(block, half), 2 + half)
        self.to_second(self.part(block), 2, 0)

    def second(self, back):
        p = self.place
        for by, half, step in ((1, 0, 1), (3, 1, -1)):
            block = self.block(back, by)
            self.arrived(self.part(block), 4 + 4 * back + half)
            piece = self.part(block, half)
            self.send(piece, piece, 6 + 4 * back + half, p.along_second(step))
            self.to_sibling(self.part(block), back, by)

    def second_far(self, back):
        block = self.block(back, 2)
        for half in range(2):
            self.arrived(self.part(block, half), 6 + 4 * back + half)
        self.to_sibling(self.part(block), back, 2)

    def finish(self):
        for back in range(4):
            for by in range(4):
                self.arrived(self.part(self.block(back, by)), 20 + 4 * back + by)

    def drain(self):
        for copy in self.sent:
            copy.wait_send()


class Scatter:
    SEMS = 13

    def __init__(self, place, partial, width, recv, out, stage, sems, local_sems):
        self.place, self.width, self.out = place, width, out
        self.sib_recv, self.second_recv, self.first_recv = recv
        self.stage, self.sems, self.local_sems = stage, sems, local_sems
        columns = pl.ds(0, width)
        self.blocks = partial.reshape(16, 2, BLOCK, PADDED).at[:, :, :, columns]
        self.grid = partial.reshape(4, 4, 2, BLOCK, PADDED).at[:, :, :, :, columns]
        self.sent = []

    def mine(self, first, second):
        return lax.div(self.place.block(first, second), 2)

    def arrived(self, spot, at):
        remote(spot, spot, self.sems, at, self.place.sibling()).wait_recv()

    def move(self, source, target, at, device):
        copy = remote(source, target, self.sems, at, device)
        copy.start()
        self.sent.append(copy)

    def to_sibling(self):
        p = self.place
        self.move(self.blocks.at[:, 1 - p.core], self.sib_recv, 0, p.sibling())

    def fetch(self, source, count):
        target = self.stage.at[pl.ds(0, count), :, pl.ds(0, self.width)]
        copy = pltpu.make_async_copy(source, target, self.local_sems.at[0])
        copy.start()
        copy.wait()

    def add_to(self, at, parts):
        total = self.blocks[at, self.place.core].astype(jnp.float32)
        for part in parts:
            total = total + self.stage[part, :, : self.width].astype(jnp.float32)
        self.blocks[at, self.place.core] = total.astype(jnp.bfloat16)

    def pair(self, half, by, target, at, step):
        p = self.place
        there = p.turn(p.second, by)
        two = pl.ds(2 * half, 2)
        flat = remote(self.grid.at[two, there, 0], target, self.sems, at, p.along_second(step))
        tall = remote(self.grid.at[there, two, 1], target, self.sems, at, p.along_second(step))

        @pl.when(p.core == 0)
        def _():
            flat.start()

        @pl.when(p.core == 1)
        def _():
            tall.start()

        self.sent.append(flat)

    def second_start(self):
        p = self.place
        self.arrived(self.sib_recv, 0)
        self.fetch(self.sib_recv, 16)

        @pl.loop(0, 16)
        def _(at):
            self.add_to(at, [at])

        for half, step in ((0, 1), (1, -1)):
            self.pair(half, 2, self.second_recv.at[pl.ds(8 + 2 * half, 2)], 1 + half, step)
        for half, step in ((0, 1), (1, -1)):
            spot = self.second_recv.at[pl.ds(4 * half + 2 * (1 - half), 2)]
            self.pair(1 - half, step, spot, 3 + half, step)

    def second_relay(self):
        p = self.place
        for half in range(2):
            self.arrived(self.second_recv.at[pl.ds(8 + 2 * half, 2)], 1 + half)
        self.fetch(self.second_recv.at[pl.ds(8, 4)], 4)
        for half, step in ((0, 1), (1, -1)):

            @pl.loop(0, 2)
            def _(first):
                at = self.mine(2 * half + first, p.turn(p.second, step))
                self.add_to(at, [2 * half + first])

            spot = self.second_recv.at[pl.ds(4 * half + 2 * half, 2)]
            self.pair(half, step, spot, 5 + half, step)

    def first_start(self):
        p = self.place
        for at in (3, 4, 5, 6):
            self.arrived(self.second_recv.at[pl.ds(0, 2)], at)
        self.fetch(self.second_recv.at[pl.ds(0, 8)], 8)

        @pl.loop(0, 4)
        def _(first):
            self.add_to(self.mine(first, p.second), [first, 4 + first])

        for half, step in ((0, 1), (1, -1)):
            self.strip(half, 2, self.first_recv.at[2], 7 + half, step)
        for half, step in ((0, 1), (1, -1)):
            self.strip(1 - half, step, self.first_recv.at[half], 9 + half, step)

    def columns(self, half):
        return pl.ds(half * (self.width // 2), self.width // 2)

    def strip(self, half, by, target, at, step):
        p = self.place
        source = self.blocks.at[self.mine(p.turn(p.first, by), p.second), p.core]
        columns = self.columns(half)
        self.move(source.at[:, columns], target.at[:, columns], at, p.along_first(step))

    def first_relay(self):
        p = self.place
        for half, step in ((0, 1), (1, -1)):
            columns = self.columns(half)
            self.arrived(self.first_recv.at[2, :, columns], 7 + half)
            at = self.mine(p.turn(p.first, step), p.second)
            both = self.blocks[at, p.core, :, columns].astype(jnp.float32)
            both = both + self.first_recv[2, :, columns].astype(jnp.float32)
            self.blocks[at, p.core, :, columns] = both.astype(jnp.bfloat16)
            self.strip(half, step, self.first_recv.at[half], 11 + half, step)

    def finish(self):
        p = self.place
        for at in (9, 10, 11, 12):
            self.arrived(self.first_recv.at[0, :, self.columns(0)], at)
        total = self.blocks[self.mine(p.first, p.second), p.core].astype(jnp.float32)
        for by in range(2):
            total = total + self.first_recv[by].astype(jnp.float32)
        self.out[...] = total

    def drain(self):
        for copy in self.sent:
            copy.wait_send()


class TpSum:
    SEMS = 18

    def __init__(self, place, send, relay, final, sems):
        self.place, self.send, self.relay_in, self.final = place, send, relay, final
        self.sems = sems
        self.sent = []

    def rows(self, by, half):
        p = self.place
        start = p.turn(p.tp, by) * QUARTER + half * HALF
        return pl.ds(pl.multiple_of(start, HALF), HALF)

    def move(self, source, target, at, by):
        copy = remote(source, target, self.sems, at, self.place.along_tp(by))
        copy.start()
        self.sent.append(copy)

    def give(self, values, slot, width):
        columns = pl.ds(slot * width, width)
        if values is not None:
            self.send[:, columns] = values.astype(jnp.bfloat16)
        for half, by in ((0, 1), (1, -1)):
            self.move(
                self.send.at[self.rows(2, half), columns],
                self.relay_in.at[half, :, columns],
                slot * 6 + half,
                by,
            )
        for half, by in ((0, 1), (1, -1)):
            self.move(
                self.send.at[self.rows(by, 1 - half), columns],
                self.final.at[half, pl.ds((1 - half) * HALF, HALF), columns],
                slot * 6 + 2 + half,
                by,
            )

    def relay(self, slot, width):
        columns = pl.ds(slot * width, width)
        for half, by in ((0, 1), (1, -1)):
            spot = self.relay_in.at[half, :, columns]
            remote(
                spot, spot, self.sems, slot * 6 + half, self.place.along_tp(by)
            ).wait_recv()
            rows = self.rows(by, half)
            both = self.send[rows, columns].astype(jnp.float32) + spot[...].astype(jnp.float32)
            self.send[rows, columns] = both.astype(jnp.bfloat16)
            self.move(
                self.send.at[rows, columns],
                self.final.at[half, pl.ds(half * HALF, HALF), columns],
                slot * 6 + 4 + half,
                by,
            )

    def take(self, slots, width):
        p = self.place
        for slot in range(slots):
            for at in (2, 3, 4, 5):
                half = at % 2
                spot = self.final.at[half, pl.ds(0, HALF), pl.ds(slot * width, width)]
                remote(spot, spot, self.sems, slot * 6 + at, p.along_tp(1)).wait_recv()
        rows = pl.ds(pl.multiple_of(p.tp * QUARTER, QUARTER), QUARTER)
        total = self.send[rows, :].astype(jnp.float32)
        for half in range(2):
            total = total + self.final[half].astype(jnp.float32)
        return total

    def drain(self):
        for copy in self.sent:
            copy.wait_send()


class TpSpread:
    SEMS = 6

    def __init__(self, place, source, whole, sems):
        self.place, self.source, self.whole, self.sems = place, source, whole, sems
        self.sent = []

    def spot(self, by, half):
        p = self.place
        start = p.turn(p.tp, by) * QUARTER + half * HALF
        return self.whole.at[pl.ds(pl.multiple_of(start, HALF), HALF)]

    def move(self, source, target, at, by):
        copy = remote(source, target, self.sems, at, self.place.along_tp(by))
        copy.start()
        self.sent.append(copy)

    def start(self):
        for at, half, by in ((0, 0, 1), (1, 1, -1), (2, 1, 1), (3, 0, -1)):
            self.move(self.source.at[pl.ds(half * HALF, HALF)], self.spot(0, half), at, by)

    def arrived(self, at, by, half):
        spot = self.spot(by, half)
        remote(spot, spot, self.sems, at, self.place.along_tp(1)).wait_recv()

    def relay(self):
        for half, by in ((0, 1), (1, -1)):
            self.arrived(half, -by, half)
            spot = self.spot(-by, half)
            self.move(spot, spot, 4 + half, by)

    def finish(self):
        self.arrived(2, -1, 1)
        self.arrived(3, 1, 0)
        self.arrived(4, 2, 0)
        self.arrived(5, 2, 1)

    def drain(self):
        for copy in self.sent:
            copy.wait_send()


def dot(left, right):
    return jnp.dot(left, right, preferred_element_type=jnp.float32)


def dot_t(left, right):
    return lax.dot_general(
        left, right, (((1,), (1,)), ((), ())), preferred_element_type=jnp.float32
    )


def turned(source, target):
    @pl.loop(0, WIDTH // TILE)
    def _(at):
        at = pl.multiple_of(at * TILE, TILE)
        target[pl.ds(at, TILE), :] = source[pl.ds(0, ROWS), pl.ds(at, TILE)].T


def own_rows_of(place):
    return pl.ds(pl.multiple_of(place.tp * QUARTER, QUARTER), QUARTER)


def norm_of(values):
    inverse = lax.rsqrt(jnp.mean(values * values, axis=-1, keepdims=True) + epsilon)
    return values * inverse, inverse


def norm_back(grad, normed, inverse, gain):
    scaled = grad * gain
    return inverse * (scaled - normed * jnp.mean(scaled * normed, axis=-1, keepdims=True))


def kernel(
    x,
    cotangent,
    lengths,
    in_weight,
    out_weight,
    gate_up_weight,
    down_weight,
    gains,
    taps,
    block_out,
    input_out,
    sib_hbm,
    second_hbm,
    io_sib_hbm,
    io_second_hbm,
    io_grad,
    gud_grad,
    small,
    io_local,
    gud_local,
    io,
    weights,
    big,
    grad_proj,
    grad_low,
    x_own,
    edges,
    input_low,
    turn_a,
    turn_b,
    send_a,
    send_b,
    relays,
    finals,
    second_low,
    residual,
    projected,
    product,
    convolved,
    gated,
    grad_own,
    block_own,
    input_own,
    conv_grad,
    stage,
    first_recv,
    io_first_recv,
    small_recv,
    io_sems,
    down_sems,
    wide_sems,
    scatter_sems,
    sum_sems,
    spread_sems,
    edge_sems,
    small_sems,
    local_sems,
):
    f32, b16 = jnp.float32, jnp.bfloat16
    place = Place()
    own_rows = own_rows_of(place)
    tiles = PADDED // TILE
    mine = place.block(place.first, place.second)
    flat_io = io.reshape(WIDTH, WIDE)
    flat_weights = weights.reshape(3, WIDTH, PADDED)

    x_copy = pltpu.make_async_copy(x, send_b, local_sems.at[1])
    low_copy = pltpu.make_async_copy(cotangent, grad_low, local_sems.at[2])
    own_copy = pltpu.make_async_copy(x.at[own_rows], x_own, local_sems.at[3])
    for copy in (x_copy, low_copy, own_copy):
        copy.start()
    for member in range(3):
        io_local[:, member * CHANNELS : (member + 1) * CHANNELS] = in_weight[member].astype(b16)
    io_local[:, 3 * CHANNELS :] = out_weight[...].astype(b16)
    for member in range(2):
        gud_local[member, :, :HIDDEN] = gate_up_weight[member].astype(b16)
    gud_local[2, :, :HIDDEN] = down_weight[...].astype(b16)
    gud_local[:, :, HIDDEN:] = jnp.zeros((3, BLOCK, PADDED - HIDDEN), b16)
    io[mine] = io_local[...]
    weights[:, mine] = gud_local[...]
    place.greet()
    slots_x = x.reshape(2, SLOT_ROWS, WIDTH)
    edge_copies = [
        remote(slots_x.at[:, pl.ds(SLOT_ROWS - EDGE, EDGE)], edges.at[0], edge_sems, 0, place.along_ctx(1)),
        remote(slots_x.at[:, pl.ds(0, EDGE)], edges.at[1], edge_sems, 1, place.along_ctx(-1)),
    ]
    for copy in edge_copies:
        copy.start()
    io_gather = Gather(place, io_local, io, io_sems)
    down_gather = Gather(place, gud_local.at[2], weights.at[2], down_sems)
    wide_gather = Gather(place, gud_local.at[pl.ds(0, 2)], weights.at[pl.ds(0, 2)], wide_sems)
    io_gather.start()

    def normed_low(values):
        normed, _ = norm_of(values.astype(f32))
        return (normed * gains[0:1, :]).astype(b16)

    x_copy.wait()

    @pl.loop(0, ROWS, step=64)
    def _(at):
        input_low[pl.ds(at, 64), :] = normed_low(send_b[pl.ds(at, 64), :])

    io_gather.first()
    for copy in edge_copies:
        copy.wait()
    for side in range(2):
        rows = pl.ds(ROWS + side * 2 * EDGE, 2 * EDGE)
        input_low[rows, :] = normed_low(edges[side].reshape(2 * EDGE, WIDTH))
    io_gather.second(0)
    io_gather.first_far()
    low_copy.wait()
    positions = place.ctx * SLOT_ROWS + lax.broadcasted_iota(jnp.int32, (SLOT_ROWS, 1), 0)
    for slot in range(2):
        rows = slice(slot * SLOT_ROWS, (slot + 1) * SLOT_ROWS)
        kept = jnp.where(positions < lengths[slot], 1.0, 0.0)
        grad_low[rows, :] = (grad_low[rows, :].astype(f32) * kept).astype(b16)
    io_gather.second(1)
    io_gather.second(3)
    io_gather.second_far(0)
    io_gather.second(2)
    down_gather.start()
    for back in (1, 3, 2):
        io_gather.second_far(back)
    io_gather.finish()
    for member in range(3):
        projected[member] = dot(
            input_low[...], flat_io[:, member * CHANNELS : (member + 1) * CHANNELS]
        )
    down_gather.first()
    down_gather.second(0)
    wide_gather.start()
    product[:, 8:, :] = (projected[0, :ROWS] * projected[2, :ROWS]).reshape(
        2, SLOT_ROWS, CHANNELS
    )
    before = (
        projected[0, ROWS : ROWS + 2 * EDGE] * projected[2, ROWS : ROWS + 2 * EDGE]
    ).reshape(2, EDGE, CHANNELS)
    product[:, :8, :] = jnp.where(place.ctx > 0, before[:, EDGE - 8 :, :], 0.0)
    convolved[...] = (
        taps[0:1, :] * product[:, 6 : 6 + SLOT_ROWS, :]
        + taps[1:2, :] * product[:, 7 : 7 + SLOT_ROWS, :]
        + taps[2:3, :] * product[:, 8 : 8 + SLOT_ROWS, :]
    ).reshape(ROWS, CHANNELS)
    gated[...] = (projected[1, :ROWS] * convolved[...]).astype(b16)

    mixed = TpSum(place, send_a, relays.at[0], finals.at[0], sum_sems.at[0])
    for slot in range(3):
        part = dot_t(gated[...], flat_io[slot * 512 : (slot + 1) * 512, 3 * CHANNELS :])
        mixed.give(part, slot, 512)
    down_gather.first_far()
    mixed.relay(0, 512)
    down_gather.second(1)
    down_gather.second(3)
    down_gather.second_far(0)
    mixed.relay(1, 512)
    mixed.relay(2, 512)
    turned(grad_low, turn_a)
    wide_gather.first()
    wide_gather.second(0)
    own_copy.wait()
    stream = x_own[...].astype(f32) + mixed.take(3, 512)
    residual[...] = stream
    normed, _ = norm_of(stream)
    second_low[own_rows, :] = (normed * gains[1:2, :]).astype(b16)
    second_spread = TpSpread(place, second_low.at[own_rows], second_low, spread_sems.at[0])
    second_spread.start()
    wide_gather.first_far()
    down_gather.second(2)
    for back in (1, 3, 2):
        down_gather.second_far(back)
    wide_gather.second(1)
    wide_gather.second(3)
    second_spread.relay()
    wide_gather.second_far(0)
    down_gather.finish()

    @pl.loop(0, tiles)
    def _(at):
        columns = pl.ds(pl.multiple_of(at * TILE, TILE), TILE)
        big[0:ROWS, columns] = dot(grad_low[...], flat_weights[2, :, columns]).astype(b16)

    wide_gather.second(2)
    second_spread.finish()
    turned(second_low, turn_b)
    for back in (1, 3, 2):
        wide_gather.second_far(back)
    wide_gather.finish()
    for part in (io_gather, down_gather, wide_gather, mixed, second_spread):
        part.drain()

    @pl.loop(0, tiles)
    def _(at):
        columns = pl.ds(pl.multiple_of(at * TILE, TILE), TILE)
        gate = dot(second_low[0:ROWS, :], flat_weights[0, :, columns])
        up = dot(second_low[0:ROWS, :], flat_weights[1, :, columns])
        grad_inner = big[0:ROWS, columns].astype(f32)
        sigmoid = jax.nn.sigmoid(gate)
        active = gate * sigmoid
        big[0:ROWS, columns] = (active * up).astype(b16)
        big[ROWS : 2 * ROWS, columns] = (
            grad_inner * up * sigmoid * (1.0 + gate * (1.0 - sigmoid))
        ).astype(b16)
        big[2 * ROWS :, columns] = (grad_inner * active).astype(b16)

    def gradient(left, at, member):
        @pl.loop(0, tiles)
        def _(tile):
            columns = pl.ds(pl.multiple_of(tile * TILE, TILE), TILE)
            flat_weights[at, :, columns] = dot(
                left[...], big[member * ROWS : (member + 1) * ROWS, columns]
            ).astype(b16)

    def piece(at):
        return Scatter(
            place,
            flat_weights.at[at],
            PADDED,
            (sib_hbm.at[at], second_hbm.at[at], first_recv.at[at]),
            gud_grad.at[at],
            stage,
            scatter_sems.at[at],
            local_sems,
        )

    gate_piece, up_piece, down_piece = piece(0), piece(1), piece(2)
    second = TpSum(place, send_b, relays.at[1], finals.at[1], sum_sems.at[1])
    branch = TpSum(place, send_a, relays.at[2], finals.at[2], sum_sems.at[2])

    def give_second(slot):
        rows = slice(slot * 512, (slot + 1) * 512)
        part = dot_t(big[ROWS : 2 * ROWS, :], flat_weights[0, rows, :])
        part = part + dot_t(big[2 * ROWS :, :], flat_weights[1, rows, :])
        second.give(part, slot, 512)

    give_second(0)
    for slot in range(3):
        columns = slice(slot * 512, (slot + 1) * 512)
        send_a[:, columns] = dot_t(big[0:ROWS, :], flat_weights[2, columns, :]).astype(b16)
    give_second(1)
    second.relay(0, 512)
    give_second(2)
    gradient(turn_a, 2, 0)
    down_piece.to_sibling()
    second.relay(1, 512)
    second.relay(2, 512)
    gradient(turn_b, 0, 1)
    gate_piece.to_sibling()
    down_piece.second_start()
    normed, inverse = norm_of(residual[...])
    grad_second = second.take(3, 512)
    small[...] = jnp.zeros_like(small)
    small[1:2, :] = jnp.sum(grad_second * normed, axis=0, keepdims=True)
    grad_stream = grad_low[own_rows, :].astype(f32) + norm_back(
        grad_second, normed, inverse, gains[1:2, :]
    )
    grad_own[...] = grad_stream
    second_low[own_rows, :] = grad_stream.astype(b16)
    low_spread = TpSpread(place, second_low.at[own_rows], second_low, spread_sems.at[1])
    low_spread.start()
    even = lax.rem(place.tp, 2) == 0
    edge_source = second_low.at[pl.ds(pl.multiple_of(place.tp * QUARTER, QUARTER), EDGE)]
    edge_target = second_low.at[
        pl.ds(pl.multiple_of(ROWS + lax.div(place.tp, 2) * EDGE, EDGE), EDGE)
    ]
    for tp in range(4):

        @pl.when(even)
        def _():
            pltpu.make_async_remote_copy(
                src_ref=edge_source,
                dst_ref=edge_target,
                send_sem=edge_sems.at[0, 2 + tp],
                recv_sem=edge_sems.at[1, 2 + lax.div(place.tp, 2)],
                device_id=place.along_ctx(-1, tp),
                device_id_type=MESH,
            ).start()

    gradient(turn_b, 1, 2)
    up_piece.to_sibling()
    gate_piece.second_start()
    low_spread.relay()
    for slot in range(3):
        branch.give(None, slot, 512)
    down_piece.second_relay()
    up_piece.second_start()
    low_spread.finish()
    for slot in range(2):
        spot = second_low.at[pl.ds(ROWS + slot * EDGE, EDGE)]
        remote(spot, spot, edge_sems, 2 + slot, place.sibling()).wait_recv()
    for tp in range(4):

        @pl.when(even)
        def _():
            remote(edge_source, edge_target, edge_sems, 2 + tp, place.sibling()).wait_send()

    grad_gated = dot(second_low[...], flat_io[:, 3 * CHANNELS :])
    conv_grad[:, :SLOT_ROWS, :] = (grad_gated[:ROWS] * projected[1, :ROWS]).reshape(
        2, SLOT_ROWS, CHANNELS
    )
    after = (grad_gated[ROWS:] * projected[1, ROWS + 2 * EDGE :]).reshape(2, EDGE, CHANNELS)
    conv_grad[:, SLOT_ROWS:, :] = jnp.where(place.ctx < 15, after[:, :8, :], 0.0)
    grad_proj[:, CHANNELS : 2 * CHANNELS] = (grad_gated[:ROWS] * convolved[...]).astype(b16)
    grad_product = (
        taps[2:3, :] * conv_grad[:, 0:SLOT_ROWS, :]
        + taps[1:2, :] * conv_grad[:, 1 : 1 + SLOT_ROWS, :]
        + taps[0:1, :] * conv_grad[:, 2 : 2 + SLOT_ROWS, :]
    ).reshape(ROWS, CHANNELS)
    grad_proj[:, 0:CHANNELS] = (grad_product * projected[2, :ROWS]).astype(b16)
    grad_proj[:, 2 * CHANNELS :] = (grad_product * projected[0, :ROWS]).astype(b16)
    second.drain()
    first = TpSum(place, send_b, relays.at[0], finals.at[0], sum_sems.at[3])
    for slot in range(3):
        part = dot_t(grad_proj[...], flat_io[slot * 512 : (slot + 1) * 512, : 3 * CHANNELS])
        first.give(part, slot, 512)
    for slot in range(3):
        branch.relay(slot, 512)
    gate_piece.second_relay()
    turned(input_low, turn_a)
    turned(second_low, turn_b)
    big[:, : 3 * CHANNELS] = dot(turn_a[...], grad_proj[...]).astype(b16)
    big[:, 3 * CHANNELS : 4 * CHANNELS] = dot(turn_b[...], gated[...]).astype(b16)
    io_piece = Scatter(
        place,
        big,
        WIDE,
        (io_sib_hbm, io_second_hbm, io_first_recv),
        io_grad,
        stage,
        scatter_sems.at[3],
        local_sems,
    )
    io_piece.to_sibling()
    down_piece.first_start()
    first.relay(0, 512)
    block_own[...] = (residual[...] + branch.take(3, 512)).astype(b16)
    block_keep = pltpu.make_async_copy(block_own, block_out.at[own_rows], local_sems.at[4])
    block_keep.start()
    first.relay(1, 512)
    first.relay(2, 512)
    block_spread = TpSpread(place, block_own, block_out, spread_sems.at[2])
    block_spread.start()
    up_piece.second_relay()
    io_piece.second_start()
    own_columns = pl.ds(pl.multiple_of(place.tp * CHANNELS, QUARTER), CHANNELS)
    for tap in range(3):
        small[2 + tap : 3 + tap, own_columns] = jnp.sum(
            conv_grad[:, :SLOT_ROWS, :] * product[:, 6 + tap : 6 + tap + SLOT_ROWS, :], axis=(0, 1)
        ).reshape(1, CHANNELS)
    normed, inverse = norm_of(x_own[...].astype(f32))
    grad_first = first.take(3, 512)
    small[0:1, :] = jnp.sum(grad_first * normed, axis=0, keepdims=True)
    input_own[...] = (
        grad_own[...] + norm_back(grad_first, normed, inverse, gains[0:1, :])
    ).astype(b16)

    def exchange(start, devices):
        copies = [
            remote(small, small_recv.at[start + at], small_sems, start + at, device)
            for at, device in enumerate(devices)
        ]
        for copy in copies:
            copy.start()
        return copies

    def added(start, copies):
        for copy in copies:
            copy.wait()
        total = small[...]
        for at in range(len(copies)):
            total = total + small_recv[start + at]
        small[...] = total

    tp_copies = exchange(0, [place.along_tp(by) for by in (1, 2, 3)])
    input_keep = pltpu.make_async_copy(input_own, input_out.at[own_rows], local_sems.at[5])
    input_keep.start()
    input_spread = TpSpread(place, input_own, input_out, spread_sems.at[3])
    input_spread.start()
    gate_piece.first_start()
    added(0, tp_copies)
    sibling_copies = exchange(3, [place.sibling()])
    down_piece.first_relay()
    block_spread.relay()
    io_piece.second_relay()
    added(3, sibling_copies)
    first_copies = exchange(4, [place.along_first(by) for by in (1, 2, 3)])
    up_piece.first_start()
    gate_piece.first_relay()
    added(4, first_copies)
    second_copies = exchange(7, [place.along_second(by) for by in (1, 2, 3)])
    io_piece.first_start()
    input_spread.relay()
    up_piece.first_relay()
    down_piece.finish()
    gate_piece.finish()
    io_piece.first_relay()
    added(7, second_copies)
    up_piece.finish()
    io_piece.finish()
    block_keep.wait()
    input_keep.wait()
    block_spread.finish()
    input_spread.finish()
    for part in (low_spread, block_spread, input_spread, first, branch):
        part.drain()
    for part in (down_piece, gate_piece, up_piece, io_piece):
        part.drain()


def step(*given):
    vmem = pl.BlockSpec(memory_space=pltpu.VMEM)
    smem = pl.BlockSpec(memory_space=pltpu.SMEM)
    hbm = pl.BlockSpec(memory_space=pl.ANY)
    f32, b16 = jnp.float32, jnp.bfloat16
    dma = pltpu.SemaphoreType.DMA
    own16 = pltpu.VMEM((QUARTER, WIDTH), b16)
    own32 = pltpu.VMEM((QUARTER, WIDTH), f32)
    full = pltpu.VMEM((ROWS, WIDTH), b16)
    across = pltpu.VMEM((WIDTH, ROWS), b16)
    return pl.pallas_call(
        kernel,
        out_shape=(
            jax.ShapeDtypeStruct((ROWS, WIDTH), b16),
            jax.ShapeDtypeStruct((ROWS, WIDTH), b16),
            jax.ShapeDtypeStruct((3, 16, BLOCK, PADDED), b16),
            jax.ShapeDtypeStruct((3, 12, BLOCK, PADDED), b16),
            jax.ShapeDtypeStruct((16, BLOCK, WIDE), b16),
            jax.ShapeDtypeStruct((12, BLOCK, WIDE), b16),
            jax.ShapeDtypeStruct((BLOCK, WIDE), f32),
            jax.ShapeDtypeStruct((3, BLOCK, PADDED), f32),
            jax.ShapeDtypeStruct((8, WIDTH), f32),
        ),
        in_specs=[hbm, hbm, smem] + [vmem] * 6,
        out_specs=(hbm,) * 6 + (vmem,) * 3,
        scratch_shapes=[
            pltpu.VMEM((BLOCK, WIDE), b16),
            pltpu.VMEM((3, BLOCK, PADDED), b16),
            pltpu.VMEM((32, BLOCK, WIDE), b16),
            pltpu.VMEM((3, 32, BLOCK, PADDED), b16),
            pltpu.VMEM((WIDTH, PADDED), b16),
            pltpu.VMEM((ROWS, 3 * CHANNELS), b16),
            full,
            own16,
            pltpu.VMEM((2, 2, EDGE, WIDTH), b16),
            pltpu.VMEM((ROWS + 4 * EDGE, WIDTH), b16),
            across,
            across,
            full,
            full,
            pltpu.VMEM((3, 2, HALF, WIDTH), b16),
            pltpu.VMEM((3, 2, QUARTER, WIDTH), b16),
            pltpu.VMEM((ROWS + 2 * EDGE, WIDTH), b16),
            own32,
            pltpu.VMEM((3, ROWS + 4 * EDGE, CHANNELS), f32),
            pltpu.VMEM((2, 8 + SLOT_ROWS, CHANNELS), f32),
            pltpu.VMEM((ROWS, CHANNELS), f32),
            pltpu.VMEM((ROWS, CHANNELS), b16),
            own32,
            own16,
            own16,
            pltpu.VMEM((2, SLOT_ROWS + 8, CHANNELS), f32),
            pltpu.VMEM((16, BLOCK, PADDED), b16),
            pltpu.VMEM((3, 3, BLOCK, PADDED), b16),
            pltpu.VMEM((3, BLOCK, WIDE), b16),
            pltpu.VMEM((10, 8, WIDTH), f32),
            dma((2, Gather.SEMS)),
            dma((2, Gather.SEMS)),
            dma((2, Gather.SEMS)),
            dma((4, 2, Scatter.SEMS)),
            dma((4, 2, TpSum.SEMS)),
            dma((4, 2, TpSpread.SEMS)),
            dma((2, 6)),
            dma((2, 10)),
            dma((6,)),
        ],
        compiler_params=pltpu.CompilerParams(
            collective_id=0, has_side_effects=True, vmem_limit_bytes=63 * 2**20
        ),
        name="step",
    )(*given)


def nesterov(weight, moment, average, gradient, step_rate):
    moment_new = momentum * moment + gradient
    weight_new = weight - step_rate * (gradient + momentum * moment_new)
    average_new = average_decay * average + (1.0 - average_decay) * weight_new
    return (moment_new, weight_new, average_new)


def on_device(
    hidden,
    lengths,
    cotangent,
    in_weight,
    in_moment,
    in_average,
    out_weight,
    out_moment,
    out_average,
    gate_up_weight,
    gate_up_moment,
    gate_up_average,
    down_weight,
    down_moment,
    down_average,
    norm_gains,
    gain_moment,
    gain_average,
    conv_taps,
    taps_moment,
    taps_average,
):
    slot_count, seq_len, model_width = hidden.shape
    row_count = slot_count * seq_len
    block_output, input_low_grad, _, _, _, _, io_sum, gud_sum, small = step(
        hidden.reshape(row_count, model_width),
        cotangent.reshape(row_count, model_width),
        lengths,
        in_weight,
        out_weight.T,
        gate_up_weight,
        down_weight.T,
        norm_gains,
        conv_taps,
    )
    block_output = block_output.reshape(slot_count, seq_len, model_width)
    input_grad = input_low_grad.astype(jnp.float32).reshape(slot_count, seq_len, model_width)
    in_sum = jnp.moveaxis(io_sum[:, : 3 * CHANNELS].reshape(BLOCK, 3, CHANNELS), 1, 0)
    out_sum = io_sum[:, 3 * CHANNELS :].T
    gate_up_sum = gud_sum[:2, :, :HIDDEN]
    down_sum = gud_sum[2, :, :HIDDEN].T
    gain_total = small[:2]
    taps_total = lax.dynamic_slice_in_dim(
        small[2:5], lax.axis_index("tp") * CHANNELS, CHANNELS, axis=1
    )
    in_new = nesterov(in_weight, in_moment, in_average, in_sum, matrix_rate)
    out_new = nesterov(out_weight, out_moment, out_average, out_sum, matrix_rate)
    gate_up_new = nesterov(
        gate_up_weight, gate_up_moment, gate_up_average, gate_up_sum, matrix_rate
    )
    down_new = nesterov(down_weight, down_moment, down_average, down_sum, matrix_rate)
    gain_new = nesterov(norm_gains, gain_moment, gain_average, gain_total, small_rate)
    taps_new = nesterov(conv_taps, taps_moment, taps_average, taps_total, small_rate)
    return (
        block_output,
        input_grad,
        in_new[0],
        in_new[1],
        in_new[2],
        out_new[0],
        out_new[1],
        out_new[2],
        gate_up_new[0],
        gate_up_new[1],
        gate_up_new[2],
        down_new[0],
        down_new[1],
        down_new[2],
        gain_new[0],
        gain_new[1],
        gain_new[2],
        taps_new[0],
        taps_new[1],
        taps_new[2],
    )


def solution(mesh):
    placed = (
        P("shard", "ctx", None),
        P("shard"),
        P("shard", "ctx", None),
        P(None, ("shard", "ctx"), "tp"),
        P(None, ("shard", "ctx"), "tp"),
        P(None, ("shard", "ctx"), "tp"),
        P("tp", ("shard", "ctx")),
        P("tp", ("shard", "ctx")),
        P("tp", ("shard", "ctx")),
        P(None, ("shard", "ctx"), "tp"),
        P(None, ("shard", "ctx"), "tp"),
        P(None, ("shard", "ctx"), "tp"),
        P("tp", ("shard", "ctx")),
        P("tp", ("shard", "ctx")),
        P("tp", ("shard", "ctx")),
        P(),
        P(),
        P(),
        P(None, "tp"),
        P(None, "tp"),
        P(None, "tp"),
    )
    return jax.shard_map(
        on_device,
        mesh=mesh,
        in_specs=placed,
        out_specs=(
            P("shard", "ctx", None),
            P("shard", "ctx", None),
            P(None, ("shard", "ctx"), "tp"),
            P(None, ("shard", "ctx"), "tp"),
            P(None, ("shard", "ctx"), "tp"),
            P("tp", ("shard", "ctx")),
            P("tp", ("shard", "ctx")),
            P("tp", ("shard", "ctx")),
            P(None, ("shard", "ctx"), "tp"),
            P(None, ("shard", "ctx"), "tp"),
            P(None, ("shard", "ctx"), "tp"),
            P("tp", ("shard", "ctx")),
            P("tp", ("shard", "ctx")),
            P("tp", ("shard", "ctx")),
            P(),
            P(),
            P(),
            P(None, "tp"),
            P(None, "tp"),
            P(None, "tp"),
        ),
        check_vma=False,
    )
```

time: 267 us -> 201 us (0.75)
  Pallas kernels: 247 us -> 189 us
  other arithmetic: 14.4 us -> 8.99 us
  local copies, waits for them, and re-layouts: 4.56 us -> 1.43 us
    pallas_call x2 -> x1, Pallas kernels: 247 us -> 189 us  [step(): pl.pallas_call(kernel, out_shape=(jax.ShapeDtypeStruct((ROWS, WIDTH), b16...]
where the time goes in v3:
time: 201 us; the launch traced here: 200 us
  Pallas kernels  189 us (94%)
  other arithmetic  8.99 us (4%)
    pallas_call x1, Pallas kernels, step(): pl.pallas_call(kernel, out_shape=(jax.ShapeDtypeStruct((ROWS, WIDTH), b16...  189 us
    add x6, other arithmetic, nesterov(): average_new = average_decay * average + (1.0 - average_decay) * weight_new  5.39 us

profile of v3, /device:TPU:0, one launch (start us, length us, event | category | flops | bytes accessed | tf_op | source)
XLA Modules:
  0.0 200.2 jit_solution(10064152334573492055)
XLA Ops:
  0.7 188.9 %step.1 = (bf16[512,1536]{1,0:T(8,128)(2,1)}, bf16[512,1536]{1,0:T(8,128)(2,1)}, bf16[3,16,48,1792]{3,2,1,0:T(8,128)(2,1)}, bf16[3,12,48,1792]{3,2,1,0:T(8,128)(...) custom-call(bf16[512,1536]{1,0:T(8,128)(2,1)} %bitcast.52, ...), custom_call_target="tpu_custom_call" | custom-call | tf_op jit(solution)/shard_map/step/pallas_call | solution.py:879
  189.6 0.0 copy-start.9
  189.6 0.0 copy-start.4
  189.6 0.0 copy-start.11
  189.6 0.0 copy-start.12
  189.6 0.0 copy-start.10
  189.7 0.0 copy-start.13
  189.7 0.0 copy-start.14
  189.7 0.0 copy-start.6
  189.7 3.6 %convert.1 = f32[2,256,1536]{2,1,0:T(8,128)} convert(bf16[2,256,1536]{2,1,0:T(8,128)(2,1)} %bitcast.55) | non-fusion elementwise | flops 786432 | bytes 4718592 | tf_op jit(solution)/shard_map/reshape | solution.py:986
  193.3 0.0 copy-done.9
  193.3 0.0 copy-done.4
  193.3 0.0 copy-done.11
  193.3 0.0 copy-done.12
  193.4 0.9 multiply_add_fusion.3
  194.3 0.0 copy-done.10
  194.3 0.0 copy-done.13
  194.3 0.0 copy-done.14
  194.3 0.7 multiply_add_fusion.4
  195.0 0.0 copy-done.6
  195.0 0.0 copy-done
  195.0 0.0 copy-done.3
  195.0 0.2 copy-done.5
  195.2 1.5 multiply_add_fusion
  196.6 0.0 copy-start.17
  196.7 0.0 copy-start.20
  196.7 0.0 copy-start.21
  196.7 1.1 multiply_add_fusion.2
  197.8 0.0 copy-done.15
  197.8 0.6 multiply_add_fusion.5
  198.5 0.6 multiply_add_fusion.7
  199.1 1.1 copy.55
  (23 shorter events, 0.1 us)
Async XLA Ops:
  189.6 3.7 %copy-start.9 = (f32[48,1536]{1,0:T(8,128)S(1)}, f32[48,1536]{1,0:T(8,128)}, u32[]{:S(2)}) copy-start(f32[48,1536]{1,0:T(8,128)} %get-tuple-element.27) | copy-start | bytes 884740
  189.6 3.7 %copy-start.4 = (f32[3,48,384]{2,1,0:T(8,128)S(1)}, f32[3,48,384]{2,1,0:T(8,128)}, u32[]{:S(2)}) copy-start(f32[3,48,384]{2,1,0:T(8,128)} %in_weight.1) | copy-start | bytes 663556
  189.6 3.7 %copy-start.11 = (f32[3,48,384]{2,1,0:T(8,128)S(1)}, f32[3,48,384]{2,1,0:T(8,128)}, u32[]{:S(2)}) copy-start(f32[3,48,384]{2,1,0:T(8,128)} %param.26) | copy-start | bytes 663556
  189.6 3.7 %copy-start.12 = (f32[3,48,384]{2,1,0:T(8,128)S(1)}, f32[3,48,384]{2,1,0:T(8,128)}, u32[]{:S(2)}) copy-start(f32[3,48,384]{2,1,0:T(8,128)} %param.25) | copy-start | bytes 663556
  189.6 4.6 %copy-start.10 = (f32[384,48]{0,1:T(8,128)S(1)}, f32[384,48]{0,1:T(8,128)}, u32[]{:S(2)}) copy-start(f32[384,48]{0,1:T(8,128)} %param.27) | copy-start | bytes 221188
  189.7 4.6 %copy-start.13 = (f32[384,48]{0,1:T(8,128)S(1)}, f32[384,48]{0,1:T(8,128)}, u32[]{:S(2)}) copy-start(f32[384,48]{0,1:T(8,128)} %param.29) | copy-start | bytes 221188
  189.7 4.6 %copy-start.14 = (f32[384,48]{0,1:T(8,128)S(1)}, f32[384,48]{0,1:T(8,128)}, u32[]{:S(2)}) copy-start(f32[384,48]{0,1:T(8,128)} %param.28) | copy-start | bytes 221188
  189.7 5.3 %copy-start.6 = (f32[2,48,1728]{2,1,0:T(8,128)S(1)}, f32[2,48,1728]{2,1,0:T(8,128)}, u32[]{:S(2)}) copy-start(f32[2,48,1728]{2,1,0:T(8,128)} %param.31) | copy-start | bytes 1990660
  193.3 1.7 copy-start
  193.3 1.7 copy-start.3
  193.3 1.9 copy-start.5
  195.1 1.5 copy-start.2
  195.1 1.6 copy-start.7
  195.2 1.6 copy-start.8
  196.6 1.1 copy-start.15
  196.6 1.1 copy-start.16
  196.6 1.1 copy-start.18
  196.6 1.1 copy-start.19
  196.6 1.8 copy-start.17
  196.7 1.8 copy-start.20
  196.7 1.8 copy-start.21
  196.7 2.4 %copy-start.1 = (bf16[512,1536]{1,0:T(8,128)(2,1)S(1)}, bf16[512,1536]{1,0:T(8,128)(2,1)}, u32[]{:S(2)}) copy-start(bf16[512,1536]{1,0:T(8,128)(2,1)} %get-tuple-element.25) | copy-start | bytes 4718596

commit v4 on v3

v4 whole, which is shorter than its diff:
```python
import functools

import jax
import jax.numpy as jnp
from jax import lax
from jax.experimental import pallas as pl
from jax.experimental.pallas import tpu as pltpu
from jax.sharding import PartitionSpec as P

MESH = pl.DeviceIdType.MESH
epsilon = 1e-05
momentum = 0.9
average_decay = 0.9
matrix_rate = 0.0004
small_rate = 0.005
WIDTH = 1536
CHANNELS = 384
HIDDEN = 1728
TILE = 256
EDGE = 16
EARLY = 4
SLOTS = ((0, 512), (512, 512), (1024, 512))
WIDE = 4 * CHANNELS
PADDED = 1792
ROWS = 512
QUARTER = 128
SLOT_ROWS = 256
BLOCK = 48
HALF = QUARTER // 2


class Place:
    def __init__(self):
        self.shard = lax.axis_index("shard")
        self.ctx = lax.axis_index("ctx")
        self.tp = lax.axis_index("tp")
        self.y = self.shard * 2 + lax.div(self.ctx, 8)
        self.z = lax.rem(lax.div(self.ctx, 2), 4)
        self.core = lax.rem(self.ctx, 2)
        self.first = self.y * (1 - self.core) + self.z * self.core
        self.second = self.z * (1 - self.core) + self.y * self.core

    def turn(self, value, by):
        return lax.rem(value + by + 4, 4)

    def device(self, y, z, core):
        return (lax.div(y, 2), lax.rem(y, 2) * 8 + z * 2 + core, self.tp)

    def grid_device(self, first, second):
        y = first * (1 - self.core) + second * self.core
        z = second * (1 - self.core) + first * self.core
        return self.device(y, z, self.core)

    def block(self, first, second):
        y = first * (1 - self.core) + second * self.core
        z = second * (1 - self.core) + first * self.core
        return y * 8 + z * 2 + self.core

    def along_first(self, by):
        return self.grid_device(self.turn(self.first, by), self.second)

    def along_second(self, by):
        return self.grid_device(self.first, self.turn(self.second, by))

    def along_tp(self, by):
        return (self.shard, self.ctx, self.turn(self.tp, by))

    def along_ctx(self, by, tp=None):
        return (self.shard, lax.rem(self.ctx + by + 16, 16), self.tp if tp is None else tp)

    def sibling(self):
        return self.device(self.y, self.z, 1 - self.core)

    def greet(self):
        barrier = pltpu.get_barrier_semaphore()
        friends = [self.sibling()]
        for tp in range(4):
            friends += [self.along_ctx(1, tp), self.along_ctx(-1, tp)]
        for by in (1, 2, 3):
            friends += [self.along_first(by), self.along_second(by), self.along_tp(by)]
        for friend in friends:
            pl.semaphore_signal(barrier, inc=1, device_id=friend, device_id_type=MESH)
        pl.semaphore_wait(barrier, len(friends))


def remote(source, target, send_sem, recv_sem, device):
    return pltpu.make_async_remote_copy(
        src_ref=source,
        dst_ref=target,
        send_sem=send_sem,
        recv_sem=recv_sem,
        device_id=device,
        device_id_type=MESH,
    )


def wait_bytes(spot, sem):
    pltpu.make_async_copy(spot, spot, sem).wait()


class Gather:
    SEMS = 12

    def __init__(self, place, local, whole, sems):
        self.place, self.local, self.whole, self.sems = place, local, whole, sems
        self.half = local.shape[-1] // 2

    def part(self, block, half=None):
        spot = self.whole.at[:, block] if self.whole.ndim == 4 else self.whole.at[block]
        if half is None:
            return spot
        columns = pl.ds(half * self.half, self.half)
        return spot.at[:, :, columns] if self.whole.ndim == 4 else spot.at[:, columns]

    def send(self, source, target, at, device):
        remote(source, target, self.sems.at[0], self.sems.at[at], device).start()

    def arrived(self, blocks, at):
        few = pl.ds(0, blocks)
        wait_bytes(self.whole.at[:, few] if self.whole.ndim == 4 else self.whole.at[few], self.sems.at[at])

    def block(self, back, by):
        p = self.place
        return p.block(p.turn(p.first, -back), p.turn(p.second, -by))

    def to_second(self, source, back, by):
        spot = self.part(self.block(back, 0))
        self.send(source, spot, 3 + back, self.place.along_second(1))
        self.send(source, spot, 3 + back, self.place.along_second(-1))
        self.to_sibling(source, back, by)

    def to_sibling(self, source, back, by):
        self.send(source, self.part(self.block(back, by)), 11, self.place.sibling())

    def start(self):
        p = self.place
        spot = self.part(self.block(0, 0))
        self.send(self.local, spot, 1, p.along_first(1))
        self.send(self.local, spot, 1, p.along_first(-1))
        self.to_second(self.local, 0, 0)

    def first(self):
        p = self.place
        self.arrived(2, 1)
        for back, half, by in ((1, 0, 1), (3, 1, -1)):
            piece = self.part(self.block(back, 0), half)
            self.send(piece, piece, 2, p.along_first(by))
        for back in (1, 3):
            self.to_second(self.part(self.block(back, 0)), back, 0)

    def first_far(self):
        self.arrived(1, 2)
        self.to_second(self.part(self.block(2, 0)), 2, 0)

    def second(self, back):
        p = self.place
        self.arrived(2, 3 + back)
        for by, half, step in ((1, 0, 1), (3, 1, -1)):
            piece = self.part(self.block(back, by), half)
            self.send(piece, piece, 7 + back, p.along_second(step))
        for by in (1, 3):
            self.to_sibling(self.part(self.block(back, by)), back, by)

    def second_far(self, back):
        self.arrived(1, 7 + back)
        self.to_sibling(self.part(self.block(back, 2)), back, 2)

    def finish(self):
        self.arrived(16, 11)

    def drain(self):
        self.arrived(31, 0)


class Scatter:
    SEMS = 6

    def __init__(self, place, partial, width, recv, out, stage, sems, local_sems):
        self.place, self.width, self.out = place, width, out
        self.sib_recv, self.second_recv, self.first_recv = recv
        self.stage, self.sems, self.local_sems = stage, sems, local_sems
        columns = pl.ds(0, width)
        self.blocks = partial.reshape(16, 2, BLOCK, PADDED).at[:, :, :, columns]
        self.grid = partial.reshape(4, 4, 2, BLOCK, PADDED).at[:, :, :, :, columns]
        self.rows = partial.reshape(32, BLOCK, PADDED).at[:, :, columns]

    def mine(self, first, second):
        return lax.div(self.place.block(first, second), 2)

    def arrived(self, spot, at):
        wait_bytes(spot, self.sems.at[at])

    def move(self, source, target, at, device):
        remote(source, target, self.sems.at[0], self.sems.at[at], device).start()

    def to_sibling(self, start=0, width=None):
        p = self.place
        columns = pl.ds(start, self.width if width is None else width)
        source = self.blocks.at[:, 1 - p.core, :, columns]
        self.move(source, self.sib_recv.at[:, :, columns], 1, p.sibling())

    def fetch(self, source, count):
        if self.stage is None:
            return source
        target = self.stage.at[pl.ds(0, count), :, pl.ds(0, self.width)]
        copy = pltpu.make_async_copy(source, target, self.local_sems.at[0])
        copy.start()
        copy.wait()
        return target

    def add_to(self, at, held, parts):
        core = self.place.core
        if len(parts) == 1:
            self.blocks[at, core] = self.blocks[at, core] + held[parts[0]]
        else:
            total = self.blocks[at, core].astype(jnp.float32)
            for part in parts:
                total = total + held[part].astype(jnp.float32)
            self.blocks[at, core] = total.astype(jnp.bfloat16)

    def pair(self, half, by, target, at, step):
        p = self.place
        there = p.turn(p.second, by)
        two = pl.ds(2 * half, 2)

        @pl.when(p.core == 0)
        def _():
            self.move(self.grid.at[two, there, 0], target, at, p.along_second(step))

        @pl.when(p.core == 1)
        def _():
            self.move(self.grid.at[there, two, 1], target, at, p.along_second(step))

    def second_start(self):
        p = self.place
        self.arrived(self.sib_recv, 1)
        held = self.fetch(self.sib_recv, 16)

        @pl.loop(0, 4)
        def _(first):
            at = self.mine(first, p.turn(p.second, 2))
            self.add_to(at, held, [at])

        for half, step in ((0, 1), (1, -1)):
            self.pair(half, 2, self.second_recv.at[pl.ds(8 + 2 * half, 2)], 2, step)

        @pl.loop(0, 12)
        def _(other):
            away = lax.rem(lax.div(other, 4) + 3, 4)
            at = self.mine(lax.rem(other, 4), p.turn(p.second, away))
            self.add_to(at, held, [at])

        for half, step in ((0, 1), (1, -1)):
            spot = self.second_recv.at[pl.ds(4 * half + 2 * (1 - half), 2)]
            self.pair(1 - half, step, spot, 3, step)

    def second_relay(self):
        p = self.place
        self.arrived(self.second_recv.at[pl.ds(8, 4)], 2)
        held = self.fetch(self.second_recv.at[pl.ds(8, 4)], 4)
        for half, step in ((0, 1), (1, -1)):

            @pl.loop(0, 2)
            def _(first):
                at = self.mine(2 * half + first, p.turn(p.second, step))
                self.add_to(at, held, [2 * half + first])

            spot = self.second_recv.at[pl.ds(4 * half + 2 * half, 2)]
            self.pair(half, step, spot, 3, step)

    def first_start(self):
        p = self.place
        self.arrived(self.second_recv.at[pl.ds(0, 8)], 3)
        held = self.fetch(self.second_recv.at[pl.ds(0, 8)], 8)

        @pl.loop(0, 4)
        def _(first):
            self.add_to(self.mine(first, p.second), held, [first, 4 + first])

        for half, step in ((0, 1), (1, -1)):
            self.strip(half, 2, self.first_recv.at[2], 4, step)
        for half, step in ((0, 1), (1, -1)):
            self.strip(1 - half, step, self.first_recv.at[half], 5, step)

    def columns(self, half):
        return pl.ds(half * (self.width // 2), self.width // 2)

    def strip(self, half, by, target, at, step):
        p = self.place
        source = self.blocks.at[self.mine(p.turn(p.first, by), p.second), p.core]
        columns = self.columns(half)
        self.move(source.at[:, columns], target.at[:, columns], at, p.along_first(step))

    def first_relay(self):
        p = self.place
        self.arrived(self.first_recv.at[2], 4)
        for half, step in ((0, 1), (1, -1)):
            columns = self.columns(half)
            at = self.mine(p.turn(p.first, step), p.second)
            both = self.blocks[at, p.core, :, columns].astype(jnp.float32)
            both = both + self.first_recv[2, :, columns].astype(jnp.float32)
            self.blocks[at, p.core, :, columns] = both.astype(jnp.bfloat16)
            self.strip(half, step, self.first_recv.at[half], 5, step)

    def finish(self):
        p = self.place
        self.arrived(self.first_recv.at[pl.ds(0, 2)], 5)
        total = self.blocks[self.mine(p.first, p.second), p.core].astype(jnp.float32)
        for by in range(2):
            total = total + self.first_recv[by].astype(jnp.float32)
        self.out[...] = total

    def drain(self):
        self.arrived(self.rows.at[pl.ds(0, 31)], 0)


class TpSum:
    SEMS = 5

    def __init__(self, place, send, relay, final, sems):
        self.place, self.send, self.relay_in, self.final = place, send, relay, final
        self.sems = sems

    def rows(self, by, half):
        p = self.place
        start = p.turn(p.tp, by) * QUARTER + half * HALF
        return pl.ds(pl.multiple_of(start, HALF), HALF)

    def move(self, source, target, at, by):
        remote(source, target, self.sems.at[0], self.sems.at[at], self.place.along_tp(by)).start()

    def give(self, values, slot):
        columns = pl.ds(*SLOTS[slot])
        self.send[:, columns] = values.astype(jnp.bfloat16)
        for half, by in ((0, 1), (1, -1)):
            source = self.send.at[self.rows(2, half), columns]
            self.move(source, self.relay_in.at[half, :, columns], 2 + slot, by)
        for half, by in ((0, 1), (1, -1)):
            source = self.send.at[self.rows(by, 1 - half), columns]
            target = self.final.at[half, pl.ds((1 - half) * HALF, HALF), columns]
            self.move(source, target, 1, by)

    def relay(self, slot):
        columns = pl.ds(*SLOTS[slot])
        wait_bytes(self.relay_in.at[:, :, columns], self.sems.at[2 + slot])
        for half, by in ((0, 1), (1, -1)):
            rows = self.rows(by, half)
            both = self.send[rows, columns].astype(jnp.float32)
            both = both + self.relay_in[half, :, columns].astype(jnp.float32)
            self.send[rows, columns] = both.astype(jnp.bfloat16)
            target = self.final.at[half, pl.ds(half * HALF, HALF), columns]
            self.move(self.send.at[rows, columns], target, 1, by)

    def take(self):
        p = self.place
        wait_bytes(self.final, self.sems.at[1])
        rows = pl.ds(pl.multiple_of(p.tp * QUARTER, QUARTER), QUARTER)
        total = self.send[rows, :].astype(jnp.float32)
        for half in range(2):
            total = total + self.final[half].astype(jnp.float32)
        return total

    def drain(self):
        wait_bytes(self.send.at[pl.ds(0, 3 * QUARTER)], self.sems.at[0])


class TpSpread:
    SEMS = 3

    def __init__(self, place, source, whole, sems):
        self.place, self.source, self.whole, self.sems = place, source, whole, sems

    def spot(self, by, half):
        p = self.place
        start = p.turn(p.tp, by) * QUARTER + half * HALF
        return self.whole.at[pl.ds(pl.multiple_of(start, HALF), HALF)]

    def move(self, source, target, at, by):
        remote(source, target, self.sems.at[0], self.sems.at[at], self.place.along_tp(by)).start()

    def start(self):
        for at, half, by in ((1, 0, 1), (1, 1, -1), (2, 1, 1), (2, 0, -1)):
            self.move(self.source.at[pl.ds(half * HALF, HALF)], self.spot(0, half), at, by)

    def arrived(self, rows, at):
        wait_bytes(self.whole.at[pl.ds(0, rows)], self.sems.at[at])

    def relay(self):
        self.arrived(QUARTER, 1)
        for half, by in ((0, 1), (1, -1)):
            spot = self.spot(-by, half)
            self.move(spot, spot, 2, by)

    def finish(self):
        self.arrived(2 * QUARTER, 2)

    def drain(self):
        self.arrived(3 * QUARTER, 0)


def dot(left, right):
    return jnp.dot(left, right, preferred_element_type=jnp.float32)


def dot_t(left, right):
    return lax.dot_general(
        left, right, (((1,), (1,)), ((), ())), preferred_element_type=jnp.float32
    )


def turned(source, target):
    @pl.loop(0, WIDTH // TILE)
    def _(at):
        at = pl.multiple_of(at * TILE, TILE)
        target[pl.ds(at, TILE), :] = source[pl.ds(0, ROWS), pl.ds(at, TILE)].T


def slot_rows(slot):
    start, width = SLOTS[slot]
    return slice(start, start + width)


def own_rows_of(place):
    return pl.ds(pl.multiple_of(place.tp * QUARTER, QUARTER), QUARTER)


def norm_of(values):
    inverse = lax.rsqrt(jnp.mean(values * values, axis=-1, keepdims=True) + epsilon)
    return values * inverse, inverse


def norm_back(grad, normed, inverse, gain):
    scaled = grad * gain
    return inverse * (scaled - normed * jnp.mean(scaled * normed, axis=-1, keepdims=True))


def kernel(
    x,
    cotangent,
    lengths,
    in_weight,
    out_weight,
    gate_up_weight,
    down_weight,
    gains,
    taps,
    block_out,
    input_out,
    sib_hbm,
    second_hbm,
    io_grad,
    gud_grad,
    small,
    io_local,
    gud_local,
    io,
    weights,
    big,
    grad_proj,
    grad_low,
    x_own,
    edges,
    input_low,
    turn_a,
    turn_b,
    send_a,
    send_b,
    relays,
    finals,
    second_low,
    residual,
    projected,
    product,
    convolved,
    gated,
    grad_own,
    block_own,
    input_own,
    conv_grad,
    stage,
    first_recv,
    io_sib_recv,
    io_second_recv,
    small_recv,
    io_sems,
    down_sems,
    early_sems,
    late_sems,
    scatter_sems,
    sum_sems,
    spread_sems,
    edge_sems,
    small_sems,
    local_sems,
):
    f32, b16 = jnp.float32, jnp.bfloat16
    place = Place()
    own_rows = own_rows_of(place)
    tiles = PADDED // TILE
    mine = place.block(place.first, place.second)
    flat_io = io.reshape(WIDTH, WIDE)
    flat_weights = weights.reshape(3, WIDTH, PADDED)

    x_copy = pltpu.make_async_copy(x, send_b, local_sems.at[1])
    low_copy = pltpu.make_async_copy(cotangent, grad_low, local_sems.at[2])
    own_copy = pltpu.make_async_copy(x.at[own_rows], x_own, local_sems.at[3])
    for copy in (x_copy, low_copy, own_copy):
        copy.start()
    for member in range(3):
        io_local[:, member * CHANNELS : (member + 1) * CHANNELS] = in_weight[member].astype(b16)
    io_local[:, 3 * CHANNELS :] = out_weight[...].astype(b16)
    for member in range(2):
        gud_local[member, :, :HIDDEN] = gate_up_weight[member].astype(b16)
    gud_local[2, :, :HIDDEN] = down_weight[...].astype(b16)
    gud_local[:, :, HIDDEN:] = jnp.zeros((3, BLOCK, PADDED - HIDDEN), b16)
    io[mine] = io_local[...]
    weights[:, mine] = gud_local[...]
    place.greet()
    early, late = pl.ds(0, EARLY * TILE), pl.ds(EARLY * TILE, PADDED - EARLY * TILE)
    two = pl.ds(0, 2)
    io_gather = Gather(place, io_local, io, io_sems)
    down_gather = Gather(place, gud_local.at[2], weights.at[2], down_sems)
    early_gather = Gather(
        place, gud_local.at[two, :, early], weights.at[two, :, :, early], early_sems
    )
    late_gather = Gather(
        place, gud_local.at[two, :, late], weights.at[two, :, :, late], late_sems
    )
    mixed = TpSum(place, send_a, relays.at[0], finals.at[0], sum_sems.at[0])
    second = TpSum(place, send_b, relays.at[1], finals.at[1], sum_sems.at[1])
    branch = TpSum(place, send_a, relays.at[0], finals.at[0], sum_sems.at[2])
    first = TpSum(place, send_b, relays.at[1], finals.at[1], sum_sems.at[3])
    second_spread = TpSpread(place, second_low.at[own_rows], second_low, spread_sems.at[0])
    low_spread = TpSpread(place, second_low.at[own_rows], second_low, spread_sems.at[1])
    block_spread = TpSpread(place, block_own, block_out, spread_sems.at[2])
    input_spread = TpSpread(place, input_own, input_out, spread_sems.at[3])
    block_keep = pltpu.make_async_copy(block_own, block_out.at[own_rows], local_sems.at[4])
    input_keep = pltpu.make_async_copy(input_own, input_out.at[own_rows], local_sems.at[5])
    even = lax.rem(place.tp, 2) == 0
    edge_source = second_low.at[pl.ds(pl.multiple_of(place.tp * QUARTER, QUARTER), EDGE)]
    edge_target = second_low.at[
        pl.ds(pl.multiple_of(ROWS + lax.div(place.tp, 2) * EDGE, EDGE), EDGE)
    ]
    own_columns = pl.ds(pl.multiple_of(place.tp * CHANNELS, QUARTER), CHANNELS)

    def piece(at):
        return Scatter(
            place,
            flat_weights.at[at],
            PADDED,
            (sib_hbm.at[at], second_hbm.at[at], first_recv.at[at]),
            gud_grad.at[at],
            stage,
            scatter_sems.at[at],
            local_sems,
        )

    gate_piece, up_piece, down_piece = piece(0), piece(1), piece(2)
    io_piece = Scatter(
        place,
        big,
        WIDE,
        (io_sib_recv, io_second_recv, gud_local.at[:, :, pl.ds(0, WIDE)]),
        io_grad,
        None,
        scatter_sems.at[3],
        local_sems,
    )

    def normed_low(values):
        normed, _ = norm_of(values.astype(f32))
        return (normed * gains[0:1, :]).astype(b16)

    def send_edges():
        slots_x = x.reshape(2, SLOT_ROWS, WIDTH)
        for side, start, by in ((0, SLOT_ROWS - EDGE, 1), (1, 0, -1)):
            remote(
                slots_x.at[:, pl.ds(start, EDGE)],
                edges.at[side],
                edge_sems.at[0],
                edge_sems.at[1],
                place.along_ctx(by),
            ).start()

    def project(member):
        columns = slice(member * CHANNELS, (member + 1) * CHANNELS)
        projected[member] = dot(input_low[...], flat_io[:, columns])

    def give_mixed(slot):
        mixed.give(dot_t(gated[...], flat_io[slot_rows(slot), 3 * CHANNELS :]), slot)

    def inner_grad(at):
        columns = pl.ds(pl.multiple_of(at * TILE, TILE), TILE)
        big[0:ROWS, columns] = dot(grad_low[...], flat_weights[2, :, columns]).astype(b16)

    def gate_up(at):
        columns = pl.ds(at * TILE, TILE)
        gate = dot(second_low[0:ROWS, :], flat_weights[0, :, columns])
        up = dot(second_low[0:ROWS, :], flat_weights[1, :, columns])
        grad_inner = big[0:ROWS, columns].astype(f32)
        sigmoid = jax.nn.sigmoid(gate)
        active = gate * sigmoid
        big[0:ROWS, columns] = (active * up).astype(b16)
        big[ROWS : 2 * ROWS, columns] = (
            grad_inner * up * sigmoid * (1.0 + gate * (1.0 - sigmoid))
        ).astype(b16)
        big[2 * ROWS :, columns] = (grad_inner * active).astype(b16)

    def give_second(slot):
        rows = slot_rows(slot)
        part = dot_t(big[ROWS : 2 * ROWS, :], flat_weights[0, rows, :])
        part = part + dot_t(big[2 * ROWS :, :], flat_weights[1, rows, :])
        second.give(part, slot)

    def give_branch(slot):
        branch.give(dot_t(big[0:ROWS, :], flat_weights[2, slot_rows(slot), :]), slot)

    def give_first(slot):
        first.give(dot_t(grad_proj[...], flat_io[slot_rows(slot), : 3 * CHANNELS]), slot)

    def gradient(left, at, member):
        @pl.loop(0, tiles)
        def _(tile):
            columns = pl.ds(pl.multiple_of(tile * TILE, TILE), TILE)
            flat_weights[at, :, columns] = dot(
                left[...], big[member * ROWS : (member + 1) * ROWS, columns]
            ).astype(b16)

    def exchange(phase, start, devices):
        for at, device in enumerate(devices):
            remote(
                small, small_recv.at[start + at], small_sems.at[0, phase], small_sems.at[1, phase], device
            ).start()

    def added(phase, start, count):
        spots = small_recv.at[pl.ds(start, count)]
        for side in range(2):
            wait_bytes(spots, small_sems.at[side, phase])
        total = small[...]
        for at in range(count):
            total = total + small_recv[start + at]
        small[...] = total

    io_gather.start()
    x_copy.wait()

    @pl.loop(0, ROWS, step=64)
    def _(at):
        input_low[pl.ds(at, 64), :] = normed_low(send_b[pl.ds(at, 64), :])

    down_gather.start()
    io_gather.first()
    io_gather.first_far()
    io_gather.second(0)
    io_gather.second(1)
    low_copy.wait()
    positions = place.ctx * SLOT_ROWS + lax.broadcasted_iota(jnp.int32, (SLOT_ROWS, 1), 0)
    for slot in range(2):
        rows = slice(slot * SLOT_ROWS, (slot + 1) * SLOT_ROWS)
        kept = jnp.where(positions < lengths[slot], 1.0, 0.0)
        grad_low[rows, :] = (grad_low[rows, :].astype(f32) * kept).astype(b16)
    io_gather.second(3)
    io_gather.second(2)
    io_gather.second_far(0)
    send_edges()
    early_gather.start()
    io_gather.second_far(1)
    io_gather.second_far(3)
    io_gather.second_far(2)
    wait_bytes(edges, edge_sems.at[1])
    wait_bytes(edges, edge_sems.at[0])
    for side in range(2):
        rows = pl.ds(ROWS + side * 2 * EDGE, 2 * EDGE)
        input_low[rows, :] = normed_low(edges[side].reshape(2 * EDGE, WIDTH))
    down_gather.first()
    io_gather.finish()
    project(0)
    project(1)
    project(2)
    product[:, 8:, :] = (projected[0, :ROWS] * projected[2, :ROWS]).reshape(
        2, SLOT_ROWS, CHANNELS
    )
    before = (
        projected[0, ROWS : ROWS + 2 * EDGE] * projected[2, ROWS : ROWS + 2 * EDGE]
    ).reshape(2, EDGE, CHANNELS)
    product[:, :8, :] = jnp.where(place.ctx > 0, before[:, EDGE - 8 :, :], 0.0)
    convolved[...] = (
        taps[0:1, :] * product[:, 6 : 6 + SLOT_ROWS, :]
        + taps[1:2, :] * product[:, 7 : 7 + SLOT_ROWS, :]
        + taps[2:3, :] * product[:, 8 : 8 + SLOT_ROWS, :]
    ).reshape(ROWS, CHANNELS)
    gated[...] = (projected[1, :ROWS] * convolved[...]).astype(b16)

    give_mixed(0)
    down_gather.first_far()
    late_gather.start()
    turned(grad_low, turn_a)
    give_mixed(1)
    down_gather.second(1)
    early_gather.first()
    early_gather.second(0)
    mixed.relay(0)
    down_gather.second(3)
    give_mixed(2)
    mixed.relay(1)
    mixed.relay(2)
    down_gather.second(0)
    early_gather.second(3)
    down_gather.second(2)
    own_copy.wait()
    stream = x_own[...].astype(f32) + mixed.take()
    residual[...] = stream
    normed, _ = norm_of(stream)
    second_low[own_rows, :] = (normed * gains[1:2, :]).astype(b16)
    second_spread.start()
    early_gather.first_far()
    down_gather.second_far(3)
    down_gather.second_far(1)
    early_gather.second(1)
    late_gather.first()
    down_gather.second_far(2)
    down_gather.second_far(0)
    second_spread.relay()
    down_gather.finish()
    early_gather.second(2)
    late_gather.first_far()
    pl.loop(3, 5)(inner_grad)
    early_gather.second_far(1)
    early_gather.second_far(0)
    pl.loop(0, 3)(inner_grad)
    early_gather.second_far(3)
    late_gather.second(0)
    late_gather.second(1)
    early_gather.second_far(2)
    late_gather.second(3)
    pl.loop(5, 7)(inner_grad)
    late_gather.second(2)
    early_gather.finish()
    late_gather.second_far(0)
    second_spread.finish()
    gate_up(2)
    late_gather.second_far(1)
    gate_up(3)
    late_gather.second_far(3)
    late_gather.second_far(2)
    gate_up(0)
    gate_up(1)
    late_gather.finish()
    gate_up(4)
    gate_up(6)
    gate_up(5)
    mixed.drain()
    give_branch(0)
    for part in (io_gather, down_gather, early_gather, late_gather, second_spread):
        part.drain()
    give_second(0)
    give_second(1)
    turned(second_low, turn_b)
    give_second(2)
    gradient(turn_b, 0, 1)
    gate_piece.to_sibling()
    second.relay(1)
    second.relay(0)
    second.relay(2)
    give_branch(1)
    branch.relay(0)
    gradient(turn_b, 1, 2)
    up_piece.to_sibling()
    normed, inverse = norm_of(residual[...])
    grad_second = second.take()
    small[...] = jnp.zeros_like(small)
    small[1:2, :] = jnp.sum(grad_second * normed, axis=0, keepdims=True)
    grad_stream = grad_low[own_rows, :].astype(f32) + norm_back(
        grad_second, normed, inverse, gains[1:2, :]
    )
    grad_own[...] = grad_stream
    second_low[own_rows, :] = grad_stream.astype(b16)
    low_spread.start()
    for tp in range(4):

        @pl.when(even)
        def _():
            remote(
                edge_source, edge_target, edge_sems.at[2], edge_sems.at[3], place.along_ctx(-1, tp)
            ).start()

    gate_piece.second_start()
    up_piece.second_start()
    low_spread.relay()
    give_branch(2)
    gradient(turn_a, 2, 0)
    down_piece.to_sibling()
    branch.relay(1)
    up_piece.second_relay()
    low_spread.finish()
    wait_bytes(second_low.at[pl.ds(ROWS, 2 * EDGE)], edge_sems.at[3])

    @pl.when(even)
    def _():
        wait_bytes(second_low.at[pl.ds(0, 4 * EDGE)], edge_sems.at[2])

    grad_gated = dot(second_low[...], flat_io[:, 3 * CHANNELS :])
    conv_grad[:, :SLOT_ROWS, :] = (grad_gated[:ROWS] * projected[1, :ROWS]).reshape(
        2, SLOT_ROWS, CHANNELS
    )
    after = (grad_gated[ROWS:] * projected[1, ROWS + 2 * EDGE :]).reshape(2, EDGE, CHANNELS)
    conv_grad[:, SLOT_ROWS:, :] = jnp.where(place.ctx < 15, after[:, :8, :], 0.0)
    grad_proj[:, CHANNELS : 2 * CHANNELS] = (grad_gated[:ROWS] * convolved[...]).astype(b16)
    branch.relay(2)
    grad_product = (
        taps[2:3, :] * conv_grad[:, 0:SLOT_ROWS, :]
        + taps[1:2, :] * conv_grad[:, 1 : 1 + SLOT_ROWS, :]
        + taps[0:1, :] * conv_grad[:, 2 : 2 + SLOT_ROWS, :]
    ).reshape(ROWS, CHANNELS)
    grad_proj[:, 0:CHANNELS] = (grad_product * projected[2, :ROWS]).astype(b16)
    grad_proj[:, 2 * CHANNELS :] = (grad_product * projected[0, :ROWS]).astype(b16)
    second.drain()
    give_first(0)
    give_first(1)
    gate_piece.second_relay()
    give_first(2)
    for tap in range(3):
        small[2 + tap : 3 + tap, own_columns] = jnp.sum(
            conv_grad[:, :SLOT_ROWS, :] * product[:, 6 + tap : 6 + tap + SLOT_ROWS, :], axis=(0, 1)
        ).reshape(1, CHANNELS)
    down_piece.second_start()
    turned(input_low, turn_a)
    up_piece.first_start()
    first.relay(0)
    turned(second_low, turn_b)
    gate_piece.first_start()
    first.relay(1)
    block_own[...] = (residual[...] + branch.take()).astype(b16)
    block_keep.start()
    first.relay(2)
    block_spread.start()
    big[:, : 2 * CHANNELS] = dot(turn_a[...], grad_proj[:, : 2 * CHANNELS]).astype(b16)
    io_piece.to_sibling(0, 2 * CHANNELS)
    big[:, 2 * CHANNELS : 3 * CHANNELS] = dot(turn_a[...], grad_proj[:, 2 * CHANNELS :]).astype(b16)
    big[:, 3 * CHANNELS : 4 * CHANNELS] = dot(turn_b[...], gated[...]).astype(b16)
    io_piece.to_sibling(2 * CHANNELS, 2 * CHANNELS)
    down_piece.second_relay()
    normed, inverse = norm_of(x_own[...].astype(f32))
    grad_first = first.take()
    small[0:1, :] = jnp.sum(grad_first * normed, axis=0, keepdims=True)
    input_own[...] = (
        grad_own[...] + norm_back(grad_first, normed, inverse, gains[0:1, :])
    ).astype(b16)
    input_keep.start()
    exchange(0, 0, [place.along_tp(by) for by in (1, 2, 3)])
    input_spread.start()
    gate_piece.first_relay()
    io_piece.second_start()
    io_piece.second_relay()
    down_piece.first_start()
    up_piece.first_relay()
    input_spread.relay()
    added(0, 0, 3)
    exchange(1, 3, [place.sibling()])
    down_piece.first_relay()
    added(1, 3, 1)
    exchange(2, 4, [place.along_first(by) for by in (1, 2, 3)])
    block_spread.relay()
    io_piece.first_start()
    gate_piece.finish()
    added(2, 4, 3)
    exchange(3, 7, [place.along_second(by) for by in (1, 2, 3)])
    io_piece.first_relay()
    down_piece.finish()
    input_spread.finish()
    up_piece.finish()
    added(3, 7, 3)
    small[2:5, :CHANNELS] = small[2:5, own_columns]
    io_piece.finish()
    block_spread.finish()
    block_keep.wait()
    input_keep.wait()
    for part in (low_spread, block_spread, input_spread, first, branch):
        part.drain()
    for part in (down_piece, gate_piece, up_piece, io_piece):
        part.drain()


def step(*given):
    vmem = pl.BlockSpec(memory_space=pltpu.VMEM)
    smem = pl.BlockSpec(memory_space=pltpu.SMEM)
    hbm = pl.BlockSpec(memory_space=pl.ANY)
    f32, b16 = jnp.float32, jnp.bfloat16
    dma = pltpu.SemaphoreType.DMA
    own16 = pltpu.VMEM((QUARTER, WIDTH), b16)
    own32 = pltpu.VMEM((QUARTER, WIDTH), f32)
    full = pltpu.VMEM((ROWS, WIDTH), b16)
    across = pltpu.VMEM((WIDTH, ROWS), b16)
    return pl.pallas_call(
        kernel,
        out_shape=(
            jax.ShapeDtypeStruct((ROWS, WIDTH), b16),
            jax.ShapeDtypeStruct((ROWS, WIDTH), b16),
            jax.ShapeDtypeStruct((3, 16, BLOCK, PADDED), b16),
            jax.ShapeDtypeStruct((3, 12, BLOCK, PADDED), b16),
            jax.ShapeDtypeStruct((BLOCK, WIDE), f32),
            jax.ShapeDtypeStruct((3, BLOCK, PADDED), f32),
            jax.ShapeDtypeStruct((8, WIDTH), f32),
        ),
        in_specs=[hbm, hbm, smem] + [vmem] * 6,
        out_specs=(hbm,) * 4 + (vmem,) * 3,
        scratch_shapes=[
            pltpu.VMEM((BLOCK, WIDE), b16),
            pltpu.VMEM((3, BLOCK, PADDED), b16),
            pltpu.VMEM((32, BLOCK, WIDE), b16),
            pltpu.VMEM((3, 32, BLOCK, PADDED), b16),
            pltpu.VMEM((WIDTH, PADDED), b16),
            pltpu.VMEM((ROWS, 3 * CHANNELS), b16),
            full,
            own16,
            pltpu.VMEM((2, 2, EDGE, WIDTH), b16),
            pltpu.VMEM((ROWS + 4 * EDGE, WIDTH), b16),
            across,
            across,
            full,
            full,
            pltpu.VMEM((2, 2, HALF, WIDTH), b16),
            pltpu.VMEM((2, 2, QUARTER, WIDTH), b16),
            pltpu.VMEM((ROWS + 2 * EDGE, WIDTH), b16),
            own32,
            pltpu.VMEM((3, ROWS + 4 * EDGE, CHANNELS), f32),
            pltpu.VMEM((2, 8 + SLOT_ROWS, CHANNELS), f32),
            pltpu.VMEM((ROWS, CHANNELS), f32),
            pltpu.VMEM((ROWS, CHANNELS), b16),
            own32,
            own16,
            own16,
            pltpu.VMEM((2, SLOT_ROWS + 8, CHANNELS), f32),
            pltpu.VMEM((16, BLOCK, PADDED), b16),
            pltpu.VMEM((3, 3, BLOCK, PADDED), b16),
            pltpu.VMEM((16, BLOCK, WIDE), b16),
            pltpu.VMEM((12, BLOCK, WIDE), b16),
            pltpu.VMEM((10, 8, WIDTH), f32),
            dma((Gather.SEMS,)),
            dma((Gather.SEMS,)),
            dma((Gather.SEMS,)),
            dma((Gather.SEMS,)),
            dma((4, Scatter.SEMS)),
            dma((4, TpSum.SEMS)),
            dma((4, TpSpread.SEMS)),
            dma((4,)),
            dma((2, 4)),
            dma((6,)),
        ],
        compiler_params=pltpu.CompilerParams(
            collective_id=0, has_side_effects=True, vmem_limit_bytes=63 * 2**20
        ),
        name="step",
    )(*given)


def nesterov(weight, moment, average, gradient, step_rate):
    moment_new = momentum * moment + gradient
    weight_new = weight - step_rate * (gradient + momentum * moment_new)
    average_new = average_decay * average + (1.0 - average_decay) * weight_new
    return (moment_new, weight_new, average_new)


def update_kernel(*refs):
    block_in, input_in = refs[:2]
    old = [refs[2 + 3 * at : 5 + 3 * at] for at in range(4)]
    small_old = refs[14:20]
    io_grad, gud_grad, small = refs[20:23]
    block_out, input_out = refs[23:25]
    new = [refs[25 + 3 * at : 28 + 3 * at] for at in range(4)]
    small_new = refs[37:43]
    block_held, input_held, wide_held = refs[43:46]
    held = [refs[46 + 3 * at : 49 + 3 * at] for at in range(4)]
    in_sems, out_sems = refs[58:]

    def moved(source, target, sems, at):
        copy = pltpu.make_async_copy(source, target, sems.at[at])
        copy.start()
        return copy

    order = (2, 3, 0, 1)
    loads = {}
    input_load = moved(input_in, input_held, in_sems, 12)
    block_load = moved(block_in, block_held, in_sems, 13)
    for matrix in order:
        loads[matrix] = [
            moved(old[matrix][at], held[matrix][at], in_sems, 3 * matrix + at) for at in range(3)
        ]
    stores = []
    input_load.wait()
    for half in range(2):
        rows = pl.ds(half * SLOT_ROWS, SLOT_ROWS)
        wide_held[rows, :] = input_held[rows, :].astype(jnp.float32)
        stores.append(moved(wide_held.at[rows], input_out.at[rows], out_sems, 12 + half))
    block_load.wait()
    stores.append(moved(block_held, block_out, out_sems, 14))
    for matrix in order:
        for copy in loads[matrix]:
            copy.wait()
        weight, moment, average = held[matrix]
        if matrix == 0:
            parts = [(at, io_grad[:, at * CHANNELS : (at + 1) * CHANNELS]) for at in range(3)]
        elif matrix == 1:
            parts = [(slice(None), io_grad[:, 3 * CHANNELS :])]
        elif matrix == 2:
            parts = [(at, gud_grad[at, :, :HIDDEN]) for at in range(2)]
        else:
            parts = [(slice(None), gud_grad[2, :, :HIDDEN])]
        for at, gradient in parts:
            moment[at], weight[at], average[at] = nesterov(
                weight[at], moment[at], average[at], gradient, matrix_rate
            )
        for at, source in enumerate((moment, weight, average)):
            stores.append(moved(source, new[matrix][at], out_sems, 3 * matrix + at))
    for group, rows, columns in ((0, slice(0, 2), slice(None)), (3, slice(2, 5), slice(0, CHANNELS))):
        weight, moment, average = small_old[group : group + 3]
        results = nesterov(weight[...], moment[...], average[...], small[rows, columns], small_rate)
        for at in range(3):
            small_new[group + at][...] = results[at]
    for copy in stores:
        copy.wait()


def update(block, input_low, matrices, smalls, io_grad, gud_grad, small):
    vmem = pl.BlockSpec(memory_space=pltpu.VMEM)
    hbm = pl.BlockSpec(memory_space=pl.ANY)
    f32 = jnp.float32
    like = lambda a: jax.ShapeDtypeStruct(a.shape, a.dtype)
    return pl.pallas_call(
        update_kernel,
        out_shape=(
            like(block),
            jax.ShapeDtypeStruct((ROWS, WIDTH), f32),
            *[like(a) for a in matrices],
            *[like(a) for a in smalls],
        ),
        in_specs=[hbm] * 14 + [vmem] * 9,
        out_specs=(hbm,) * 14 + (vmem,) * 6,
        scratch_shapes=[
            pltpu.VMEM((ROWS, WIDTH), jnp.bfloat16),
            pltpu.VMEM((ROWS, WIDTH), jnp.bfloat16),
            pltpu.VMEM((ROWS, WIDTH), f32),
            *[pltpu.VMEM(a.shape, f32) for a in matrices],
            pltpu.SemaphoreType.DMA((14,)),
            pltpu.SemaphoreType.DMA((15,)),
        ],
        compiler_params=pltpu.CompilerParams(vmem_limit_bytes=62 * 2**20),
        name="update",
    )(block, input_low, *matrices, *smalls, io_grad, gud_grad, small)


def on_device(
    hidden,
    lengths,
    cotangent,
    in_weight,
    in_moment,
    in_average,
    out_weight,
    out_moment,
    out_average,
    gate_up_weight,
    gate_up_moment,
    gate_up_average,
    down_weight,
    down_moment,
    down_average,
    norm_gains,
    gain_moment,
    gain_average,
    conv_taps,
    taps_moment,
    taps_average,
):
    slot_count, seq_len, model_width = hidden.shape
    row_count = slot_count * seq_len
    block_output, input_low_grad, _, _, io_sum, gud_sum, small = step(
        hidden.reshape(row_count, model_width),
        cotangent.reshape(row_count, model_width),
        lengths,
        in_weight,
        out_weight.T,
        gate_up_weight,
        down_weight.T,
        norm_gains,
        conv_taps,
    )
    matrices = (
        (in_weight, in_moment, in_average),
        (out_weight.T, out_moment.T, out_average.T),
        (gate_up_weight, gate_up_moment, gate_up_average),
        (down_weight.T, down_moment.T, down_average.T),
    )
    smalls = (norm_gains, gain_moment, gain_average, conv_taps, taps_moment, taps_average)
    block_output, input_grad, *new = update(
        block_output,
        input_low_grad,
        [a for group in matrices for a in group],
        smalls,
        io_sum,
        gud_sum,
        small,
    )
    return (
        block_output.reshape(slot_count, seq_len, model_width),
        input_grad.reshape(slot_count, seq_len, model_width),
        *new[0:3],
        *[a.T for a in new[3:6]],
        *new[6:9],
        *[a.T for a in new[9:12]],
        *new[12:18],
    )


def solution(mesh):
    placed = (
        P("shard", "ctx", None),
        P("shard"),
        P("shard", "ctx", None),
        P(None, ("shard", "ctx"), "tp"),
        P(None, ("shard", "ctx"), "tp"),
        P(None, ("shard", "ctx"), "tp"),
        P("tp", ("shard", "ctx")),
        P("tp", ("shard", "ctx")),
        P("tp", ("shard", "ctx")),
        P(None, ("shard", "ctx"), "tp"),
        P(None, ("shard", "ctx"), "tp"),
        P(None, ("shard", "ctx"), "tp"),
        P("tp", ("shard", "ctx")),
        P("tp", ("shard", "ctx")),
        P("tp", ("shard", "ctx")),
        P(),
        P(),
        P(),
        P(None, "tp"),
        P(None, "tp"),
        P(None, "tp"),
    )
    return jax.shard_map(
        on_device,
        mesh=mesh,
        in_specs=placed,
        out_specs=(
            P("shard", "ctx", None),
            P("shard", "ctx", None),
            P(None, ("shard", "ctx"), "tp"),
            P(None, ("shard", "ctx"), "tp"),
            P(None, ("shard", "ctx"), "tp"),
            P("tp", ("shard", "ctx")),
            P("tp", ("shard", "ctx")),
            P("tp", ("shard", "ctx")),
            P(None, ("shard", "ctx"), "tp"),
            P(None, ("shard", "ctx"), "tp"),
            P(None, ("shard", "ctx"), "tp"),
            P("tp", ("shard", "ctx")),
            P("tp", ("shard", "ctx")),
            P("tp", ("shard", "ctx")),
            P(),
            P(),
            P(),
            P(None, "tp"),
            P(None, "tp"),
            P(None, "tp"),
        ),
        check_vma=False,
    )
```

time: 201 us -> 172 us (0.86)
  Pallas kernels: 189 us -> 171 us
  other arithmetic: 8.99 us -> 0 us
    pallas_call x1, Pallas kernels: 189 us -> 163 us  [step(): pl.pallas_call(kernel, out_shape=(jax.ShapeDtypeStruct((ROWS, WIDTH), b16...]
    pallas_call x0 -> x1, Pallas kernels: none -> 7.55 us  [update(): pl.pallas_call(update_kernel, out_shape=(like(block), jax.ShapeDtypeStruc...]
    add x6 -> x0, other arithmetic: 5.39 us -> none  [nesterov(): average_new = average_decay * average + (1.0 - average_decay) * weight_new]
    reshape x1 -> x0, other arithmetic: 3.6 us -> none  [on_device(): input_low_grad.astype(jnp.float32).reshape(slot_count, seq_len, model_width)]
where the time goes in v4:
time: 172 us
  Pallas kernels  171 us (99%)
    pallas_call x1, Pallas kernels, step(): pl.pallas_call(kernel, out_shape=(jax.ShapeDtypeStruct((ROWS, WIDTH), b16...  163 us
    pallas_call x1, Pallas kernels, update(): pl.pallas_call(update_kernel, out_shape=(like(block), jax.ShapeDtypeStruc...  7.55 us

profile of v4, /device:TPU:0, one launch (start us, length us, event | category | flops | bytes accessed | tf_op | source)
XLA Modules:
  0.0 171.9 jit_solution(4809966341319912892)
XLA Ops:
  0.7 163.5 %step.1 = (bf16[512,1536]{1,0:T(8,128)(2,1)}, bf16[512,1536]{1,0:T(8,128)(2,1)}, bf16[3,16,48,1792]{3,2,1,0:T(8,128)(2,1)}, bf16[3,12,48,1792]{3,2,1,0:T(8,128)(...) custom-call(bf16[512,1536]{1,0:T(8,128)(2,1)} %bitcast.16, bf16[512,1536]{1,0:T(8,128)(2,1)} %bitcast.17, ...), custom_call_target="tpu_custom_call" | custom-call | tf_op jit(solution)/shard_map/step/pallas_call | solution.py:894
  164.1 7.6 %update.1 = (bf16[512,1536]{1,0:T(8,128)(2,1)}, f32[512,1536]{1,0:T(8,128)}, f32[3,48,384]{2,1,0:T(8,128)}, f32[3,48,384]{2,1,0:T(8,128)}, f32[3,48,384]{2,1,0:T...) custom-call(bf16[512,1536]{1,0:T(8,128)(2,1)} %get-tuple-element.45., ...), custom_call_target="tpu_custom_call" | custom-call | tf_op jit(solution)/shard_map/update/pallas_call | solution.py:1029

commit v5 on v4

--- a/solution.py
+++ b/solution.py
@@ -80,7 +80,7 @@
             friends += [self.along_first(by), self.along_second(by), self.along_tp(by)]
         for friend in friends:
             pl.semaphore_signal(barrier, inc=1, device_id=friend, device_id_type=MESH)
-        pl.semaphore_wait(barrier, len(friends))
+        return len(friends)
 
 
 def remote(source, target, send_sem, recv_sem, device):
@@ -308,10 +308,16 @@
         total = self.blocks[self.mine(p.first, p.second), p.core].astype(jnp.float32)
         for by in range(2):
             total = total + self.first_recv[by].astype(jnp.float32)
-        self.out[...] = total
+        wide, out, members, columns, sem = self.out
+        for member in range(members):
+            wide[member] = total[:, member * columns : (member + 1) * columns]
+        copy = pltpu.make_async_copy(wide, out, sem)
+        copy.start()
+        self.store = copy
 
     def drain(self):
         self.arrived(self.rows.at[pl.ds(0, 31)], 0)
+        self.store.wait()
 
 
 class TpSum:
@@ -451,6 +457,8 @@
     io_grad,
     gud_grad,
     small,
+    io_wide,
+    gud_wide,
     io_local,
     gud_local,
     io,
@@ -460,6 +468,8 @@
     grad_low,
     x_own,
     edges,
+    edge_send,
+    edge_recv,
     input_low,
     turn_a,
     turn_b,
@@ -501,21 +511,33 @@
     flat_io = io.reshape(WIDTH, WIDE)
     flat_weights = weights.reshape(3, WIDTH, PADDED)
 
+    loads = [
+        pltpu.make_async_copy(source, target, local_sems.at[6 + at])
+        for at, (source, target) in enumerate(
+            (
+                (in_weight, io_wide.at[pl.ds(0, 3)]),
+                (out_weight, io_wide.at[3]),
+                (gate_up_weight, gud_wide.at[pl.ds(0, 2)]),
+                (down_weight, gud_wide.at[2]),
+            )
+        )
+    ]
     x_copy = pltpu.make_async_copy(x, send_b, local_sems.at[1])
     low_copy = pltpu.make_async_copy(cotangent, grad_low, local_sems.at[2])
     own_copy = pltpu.make_async_copy(x.at[own_rows], x_own, local_sems.at[3])
-    for copy in (x_copy, low_copy, own_copy):
+    for copy in (*loads, x_copy, low_copy, own_copy):
         copy.start()
-    for member in range(3):
-        io_local[:, member * CHANNELS : (member + 1) * CHANNELS] = in_weight[member].astype(b16)
-    io_local[:, 3 * CHANNELS :] = out_weight[...].astype(b16)
-    for member in range(2):
-        gud_local[member, :, :HIDDEN] = gate_up_weight[member].astype(b16)
-    gud_local[2, :, :HIDDEN] = down_weight[...].astype(b16)
+    friends = place.greet()
+    for copy in loads:
+        copy.wait()
+    for member in range(4):
+        io_local[:, member * CHANNELS : (member + 1) * CHANNELS] = io_wide[member].astype(b16)
+        if member < 3:
+            gud_local[member, :, :HIDDEN] = gud_wide[member].astype(b16)
     gud_local[:, :, HIDDEN:] = jnp.zeros((3, BLOCK, PADDED - HIDDEN), b16)
     io[mine] = io_local[...]
     weights[:, mine] = gud_local[...]
-    place.greet()
+    pl.semaphore_wait(pltpu.get_barrier_semaphore(), friends)
     early, late = pl.ds(0, EARLY * TILE), pl.ds(EARLY * TILE, PADDED - EARLY * TILE)
     two = pl.ds(0, 2)
     io_gather = Gather(place, io_local, io, io_sems)
@@ -537,11 +559,6 @@
     block_keep = pltpu.make_async_copy(block_own, block_out.at[own_rows], local_sems.at[4])
     input_keep = pltpu.make_async_copy(input_own, input_out.at[own_rows], local_sems.at[5])
     even = lax.rem(place.tp, 2) == 0
-    edge_source = second_low.at[pl.ds(pl.multiple_of(place.tp * QUARTER, QUARTER), EDGE)]
-    edge_target = second_low.at[
-        pl.ds(pl.multiple_of(ROWS + lax.div(place.tp, 2) * EDGE, EDGE), EDGE)
-    ]
-    own_columns = pl.ds(pl.multiple_of(place.tp * CHANNELS, QUARTER), CHANNELS)
 
     def piece(at):
         return Scatter(
@@ -549,7 +566,13 @@
             flat_weights.at[at],
             PADDED,
             (sib_hbm.at[at], second_hbm.at[at], first_recv.at[at]),
-            gud_grad.at[at],
+            (
+                gud_wide.at[pl.ds(at, 1)],
+                gud_grad.at[pl.ds(at, 1)],
+                1,
+                HIDDEN,
+                local_sems.at[6 + at],
+            ),
             stage,
             scatter_sems.at[at],
             local_sems,
@@ -561,7 +584,7 @@
         big,
         WIDE,
         (io_sib_recv, io_second_recv, gud_local.at[:, :, pl.ds(0, WIDE)]),
-        io_grad,
+        (io_wide, io_grad, 4, CHANNELS, local_sems.at[9]),
         None,
         scatter_sems.at[3],
         local_sems,
@@ -598,11 +621,11 @@
         gate = dot(second_low[0:ROWS, :], flat_weights[0, :, columns])
         up = dot(second_low[0:ROWS, :], flat_weights[1, :, columns])
         grad_inner = big[0:ROWS, columns].astype(f32)
-        sigmoid = jax.nn.sigmoid(gate)
+        sigmoid = 0.5 * jnp.tanh(0.5 * gate) + 0.5
         active = gate * sigmoid
         big[0:ROWS, columns] = (active * up).astype(b16)
         big[ROWS : 2 * ROWS, columns] = (
-            grad_inner * up * sigmoid * (1.0 + gate * (1.0 - sigmoid))
+            grad_inner * up * (sigmoid + active * (1.0 - sigmoid))
         ).astype(b16)
         big[2 * ROWS :, columns] = (grad_inner * active).astype(b16)
 
@@ -618,53 +641,58 @@
     def give_first(slot):
         first.give(dot_t(grad_proj[...], flat_io[slot_rows(slot), : 3 * CHANNELS]), slot)
 
-    def gradient(left, at, member):
-        @pl.loop(0, tiles)
+    def gradient(left, at, member, start, stop):
+        @pl.loop(start, stop)
         def _(tile):
             columns = pl.ds(pl.multiple_of(tile * TILE, TILE), TILE)
             flat_weights[at, :, columns] = dot(
                 left[...], big[member * ROWS : (member + 1) * ROWS, columns]
             ).astype(b16)
 
-    def exchange(phase, start, devices):
+    def keep_gain(start, values):
+        total = jnp.sum(values, axis=0, keepdims=True)
+        for at in range(4):
+            small[start + at : start + at + 1, :] = total[:, at * CHANNELS : (at + 1) * CHANNELS]
+
+    def exchange(phase, start, devices, rows=16):
+        few = pl.ds(0, rows)
         for at, device in enumerate(devices):
             remote(
-                small, small_recv.at[start + at], small_sems.at[0, phase], small_sems.at[1, phase], device
+                small.at[few],
+                small_recv.at[start + at, few],
+                small_sems.at[0, phase],
+                small_sems.at[1, phase],
+                device,
             ).start()
 
-    def added(phase, start, count):
-        spots = small_recv.at[pl.ds(start, count)]
+    def added(phase, start, count, rows=16):
+        spots = small_recv.at[pl.ds(start, count), pl.ds(0, rows)]
         for side in range(2):
             wait_bytes(spots, small_sems.at[side, phase])
-        total = small[...]
+        total = small[0:rows, :]
         for at in range(count):
-            total = total + small_recv[start + at]
-        small[...] = total
+            total = total + small_recv[start + at, 0:rows, :]
+        small[0:rows, :] = total
 
     io_gather.start()
+    down_gather.start()
+    io_gather.first()
+    io_gather.first_far()
     x_copy.wait()
 
     @pl.loop(0, ROWS, step=64)
     def _(at):
         input_low[pl.ds(at, 64), :] = normed_low(send_b[pl.ds(at, 64), :])
 
-    down_gather.start()
-    io_gather.first()
-    io_gather.first_far()
+    io_gather.second(1)
+    io_gather.second(3)
     io_gather.second(0)
-    io_gather.second(1)
-    low_copy.wait()
-    positions = place.ctx * SLOT_ROWS + lax.broadcasted_iota(jnp.int32, (SLOT_ROWS, 1), 0)
-    for slot in range(2):
-        rows = slice(slot * SLOT_ROWS, (slot + 1) * SLOT_ROWS)
-        kept = jnp.where(positions < lengths[slot], 1.0, 0.0)
-        grad_low[rows, :] = (grad_low[rows, :].astype(f32) * kept).astype(b16)
-    io_gather.second(3)
     io_gather.second(2)
+    io_gather.second_far(1)
+    send_edges()
+    down_gather.first()
     io_gather.second_far(0)
-    send_edges()
     early_gather.start()
-    io_gather.second_far(1)
     io_gather.second_far(3)
     io_gather.second_far(2)
     wait_bytes(edges, edge_sems.at[1])
@@ -672,11 +700,10 @@
     for side in range(2):
         rows = pl.ds(ROWS + side * 2 * EDGE, 2 * EDGE)
         input_low[rows, :] = normed_low(edges[side].reshape(2 * EDGE, WIDTH))
-    down_gather.first()
     io_gather.finish()
-    project(0)
     project(1)
     project(2)
+    project(0)
     product[:, 8:, :] = (projected[0, :ROWS] * projected[2, :ROWS]).reshape(
         2, SLOT_ROWS, CHANNELS
     )
@@ -692,112 +719,145 @@
     gated[...] = (projected[1, :ROWS] * convolved[...]).astype(b16)
 
     give_mixed(0)
+    give_mixed(1)
     down_gather.first_far()
-    late_gather.start()
-    turned(grad_low, turn_a)
-    give_mixed(1)
     down_gather.second(1)
+    down_gather.second(0)
     early_gather.first()
-    early_gather.second(0)
+    give_mixed(2)
+    down_gather.second(2)
     mixed.relay(0)
+    down_gather.second_far(0)
+    early_gather.first_far()
     down_gather.second(3)
-    give_mixed(2)
     mixed.relay(1)
     mixed.relay(2)
-    down_gather.second(0)
-    early_gather.second(3)
-    down_gather.second(2)
+    late_gather.start()
     own_copy.wait()
     stream = x_own[...].astype(f32) + mixed.take()
     residual[...] = stream
     normed, _ = norm_of(stream)
     second_low[own_rows, :] = (normed * gains[1:2, :]).astype(b16)
     second_spread.start()
-    early_gather.first_far()
+    early_gather.second(0)
+    early_gather.second(1)
+    early_gather.second(3)
+    early_gather.second(2)
+    low_copy.wait()
+    positions = place.ctx * SLOT_ROWS + lax.broadcasted_iota(jnp.int32, (SLOT_ROWS, 1), 0)
+    for slot in range(2):
+        rows = slice(slot * SLOT_ROWS, (slot + 1) * SLOT_ROWS)
+        kept = jnp.where(positions < lengths[slot], 1.0, 0.0)
+        grad_low[rows, :] = (grad_low[rows, :].astype(f32) * kept).astype(b16)
     down_gather.second_far(3)
+    down_gather.second_far(2)
     down_gather.second_far(1)
-    early_gather.second(1)
     late_gather.first()
-    down_gather.second_far(2)
-    down_gather.second_far(0)
     second_spread.relay()
     down_gather.finish()
-    early_gather.second(2)
     late_gather.first_far()
-    pl.loop(3, 5)(inner_grad)
+    pl.loop(0, 3)(inner_grad)
+    pl.loop(5, 7)(inner_grad)
+    early_gather.second_far(0)
+    late_gather.second(1)
     early_gather.second_far(1)
-    early_gather.second_far(0)
-    pl.loop(0, 3)(inner_grad)
     early_gather.second_far(3)
-    late_gather.second(0)
-    late_gather.second(1)
     early_gather.second_far(2)
     late_gather.second(3)
-    pl.loop(5, 7)(inner_grad)
+    late_gather.second(0)
+    pl.loop(3, 5)(inner_grad)
+    early_gather.finish()
     late_gather.second(2)
-    early_gather.finish()
-    late_gather.second_far(0)
     second_spread.finish()
     gate_up(2)
     late_gather.second_far(1)
+    gate_up(1)
+    late_gather.second_far(3)
+    gate_up(0)
+    late_gather.second_far(0)
+    late_gather.second_far(2)
     gate_up(3)
-    late_gather.second_far(3)
-    late_gather.second_far(2)
-    gate_up(0)
-    gate_up(1)
     late_gather.finish()
     gate_up(4)
+    gate_up(5)
     gate_up(6)
-    gate_up(5)
     mixed.drain()
     give_branch(0)
     for part in (io_gather, down_gather, early_gather, late_gather, second_spread):
         part.drain()
     give_second(0)
     give_second(1)
+    give_second(2)
     turned(second_low, turn_b)
-    give_second(2)
-    gradient(turn_b, 0, 1)
-    gate_piece.to_sibling()
+    gradient(turn_b, 1, 2, 0, 4)
+    up_piece.to_sibling(0, 4 * TILE)
+    gradient(turn_b, 1, 2, 4, 7)
+    up_piece.to_sibling(4 * TILE, 3 * TILE)
+    second.relay(0)
     second.relay(1)
-    second.relay(0)
+    gradient(turn_b, 0, 1, 0, 4)
+    gate_piece.to_sibling(0, 4 * TILE)
     second.relay(2)
+    turned(grad_low, turn_a)
     give_branch(1)
+    up_piece.second_start()
     branch.relay(0)
-    gradient(turn_b, 1, 2)
-    up_piece.to_sibling()
     normed, inverse = norm_of(residual[...])
     grad_second = second.take()
     small[...] = jnp.zeros_like(small)
-    small[1:2, :] = jnp.sum(grad_second * normed, axis=0, keepdims=True)
+    keep_gain(4, grad_second * normed)
     grad_stream = grad_low[own_rows, :].astype(f32) + norm_back(
         grad_second, normed, inverse, gains[1:2, :]
     )
     grad_own[...] = grad_stream
     second_low[own_rows, :] = grad_stream.astype(b16)
     low_spread.start()
+    pieces = [
+        grad_stream[row : row + 1, at * TILE : (at + 1) * TILE] for row in range(2) for at in range(6)
+    ]
+    pieces.append(jnp.zeros((EDGE - 12, TILE), f32))
+    edge_send[...] = jnp.concatenate(pieces, axis=0).astype(b16)
     for tp in range(4):
 
         @pl.when(even)
         def _():
             remote(
-                edge_source, edge_target, edge_sems.at[2], edge_sems.at[3], place.along_ctx(-1, tp)
+                edge_send,
+                edge_recv.at[lax.div(place.tp, 2)],
+                edge_sems.at[2],
+                edge_sems.at[3],
+                place.along_ctx(-1, tp),
             ).start()
 
+    gradient(turn_b, 0, 1, 4, 7)
+    gate_piece.to_sibling(4 * TILE, 3 * TILE)
     gate_piece.second_start()
-    up_piece.second_start()
     low_spread.relay()
+    up_piece.second_relay()
     give_branch(2)
-    gradient(turn_a, 2, 0)
-    down_piece.to_sibling()
     branch.relay(1)
-    up_piece.second_relay()
+    gradient(turn_a, 2, 0, 0, 4)
+    down_piece.to_sibling(0, 4 * TILE)
+    gradient(turn_a, 2, 0, 4, 7)
+    down_piece.to_sibling(4 * TILE, 3 * TILE)
+    gate_piece.second_relay()
     low_spread.finish()
-    wait_bytes(second_low.at[pl.ds(ROWS, 2 * EDGE)], edge_sems.at[3])
+    wait_bytes(edge_recv, edge_sems.at[3])
 
     @pl.when(even)
     def _():
-        wait_bytes(second_low.at[pl.ds(0, 4 * EDGE)], edge_sems.at[2])
+        wait_bytes(second_low.at[pl.ds(0, 4 * EDGE), pl.ds(0, TILE)], edge_sems.at[2])
+
+    for slot in range(2):
+        packed = edge_recv[slot].astype(f32)
+        rows = [
+            jnp.concatenate([packed[6 * row + at : 6 * row + at + 1, :] for at in range(6)], axis=1)
+            for row in range(2)
+        ]
+        rows.append(jnp.zeros((EDGE - 2, WIDTH), f32))
+        second_low[ROWS + slot * EDGE : ROWS + (slot + 1) * EDGE, :] = jnp.concatenate(
+            rows, axis=0
+        ).astype(b16)
 
     grad_gated = dot(second_low[...], flat_io[:, 3 * CHANNELS :])
     conv_grad[:, :SLOT_ROWS, :] = (grad_gated[:ROWS] * projected[1, :ROWS]).reshape(
@@ -817,60 +877,58 @@
     second.drain()
     give_first(0)
     give_first(1)
-    gate_piece.second_relay()
     give_first(2)
+    down_piece.second_start()
+    turned(second_low, turn_b)
+    block_own[...] = (residual[...] + branch.take()).astype(b16)
+    block_keep.start()
     for tap in range(3):
-        small[2 + tap : 3 + tap, own_columns] = jnp.sum(
+        small[8 + tap : 9 + tap, :] = jnp.sum(
             conv_grad[:, :SLOT_ROWS, :] * product[:, 6 + tap : 6 + tap + SLOT_ROWS, :], axis=(0, 1)
         ).reshape(1, CHANNELS)
-    down_piece.second_start()
+    first.relay(1)
     turned(input_low, turn_a)
-    up_piece.first_start()
     first.relay(0)
-    turned(second_low, turn_b)
     gate_piece.first_start()
-    first.relay(1)
-    block_own[...] = (residual[...] + branch.take()).astype(b16)
-    block_keep.start()
     first.relay(2)
-    block_spread.start()
     big[:, : 2 * CHANNELS] = dot(turn_a[...], grad_proj[:, : 2 * CHANNELS]).astype(b16)
     io_piece.to_sibling(0, 2 * CHANNELS)
+    block_spread.start()
+    down_piece.second_relay()
     big[:, 2 * CHANNELS : 3 * CHANNELS] = dot(turn_a[...], grad_proj[:, 2 * CHANNELS :]).astype(b16)
     big[:, 3 * CHANNELS : 4 * CHANNELS] = dot(turn_b[...], gated[...]).astype(b16)
     io_piece.to_sibling(2 * CHANNELS, 2 * CHANNELS)
-    down_piece.second_relay()
+    gate_piece.first_relay()
     normed, inverse = norm_of(x_own[...].astype(f32))
     grad_first = first.take()
-    small[0:1, :] = jnp.sum(grad_first * normed, axis=0, keepdims=True)
+    keep_gain(0, grad_first * normed)
     input_own[...] = (
         grad_own[...] + norm_back(grad_first, normed, inverse, gains[0:1, :])
     ).astype(b16)
     input_keep.start()
-    exchange(0, 0, [place.along_tp(by) for by in (1, 2, 3)])
+    exchange(0, 0, [place.along_tp(by) for by in (1, 2, 3)], 8)
     input_spread.start()
-    gate_piece.first_relay()
     io_piece.second_start()
     io_piece.second_relay()
+    added(0, 0, 3, 8)
+    exchange(1, 3, [place.sibling()])
     down_piece.first_start()
-    up_piece.first_relay()
-    input_spread.relay()
-    added(0, 0, 3)
-    exchange(1, 3, [place.sibling()])
-    down_piece.first_relay()
     added(1, 3, 1)
     exchange(2, 4, [place.along_first(by) for by in (1, 2, 3)])
+    up_piece.first_start()
+    input_spread.relay()
     block_spread.relay()
     io_piece.first_start()
-    gate_piece.finish()
+    down_piece.first_relay()
     added(2, 4, 3)
     exchange(3, 7, [place.along_second(by) for by in (1, 2, 3)])
+    up_piece.first_relay()
     io_piece.first_relay()
+    input_spread.finish()
+    added(3, 7, 3)
+    up_piece.finish()
+    gate_piece.finish()
     down_piece.finish()
-    input_spread.finish()
-    up_piece.finish()
-    added(3, 7, 3)
-    small[2:5, :CHANNELS] = small[2:5, own_columns]
     io_piece.finish()
     block_spread.finish()
     block_keep.wait()
@@ -898,13 +956,15 @@
             jax.ShapeDtypeStruct((ROWS, WIDTH), b16),
             jax.ShapeDtypeStruct((3, 16, BLOCK, PADDED), b16),
             jax.ShapeDtypeStruct((3, 12, BLOCK, PADDED), b16),
-            jax.ShapeDtypeStruct((BLOCK, WIDE), f32),
-            jax.ShapeDtypeStruct((3, BLOCK, PADDED), f32),
-            jax.ShapeDtypeStruct((8, WIDTH), f32),
+            jax.ShapeDtypeStruct((4, BLOCK, CHANNELS), f32),
+            jax.ShapeDtypeStruct((3, BLOCK, HIDDEN), f32),
+            jax.ShapeDtypeStruct((16, CHANNELS), f32),
         ),
-        in_specs=[hbm, hbm, smem] + [vmem] * 6,
-        out_specs=(hbm,) * 4 + (vmem,) * 3,
+        in_specs=[hbm, hbm, smem] + [hbm] * 4 + [vmem] * 2,
+        out_specs=(hbm,) * 6 + (vmem,),
         scratch_shapes=[
+            pltpu.VMEM((4, BLOCK, CHANNELS), f32),
+            pltpu.VMEM((3, BLOCK, HIDDEN), f32),
             pltpu.VMEM((BLOCK, WIDE), b16),
             pltpu.VMEM((3, BLOCK, PADDED), b16),
             pltpu.VMEM((32, BLOCK, WIDE), b16),
@@ -914,6 +974,8 @@
             full,
             own16,
             pltpu.VMEM((2, 2, EDGE, WIDTH), b16),
+            pltpu.VMEM((EDGE, TILE), b16),
+            pltpu.VMEM((2, EDGE, TILE), b16),
             pltpu.VMEM((ROWS + 4 * EDGE, WIDTH), b16),
             across,
             across,
@@ -935,7 +997,7 @@
             pltpu.VMEM((3, 3, BLOCK, PADDED), b16),
             pltpu.VMEM((16, BLOCK, WIDE), b16),
             pltpu.VMEM((12, BLOCK, WIDE), b16),
-            pltpu.VMEM((10, 8, WIDTH), f32),
+            pltpu.VMEM((10, 16, CHANNELS), f32),
             dma((Gather.SEMS,)),
             dma((Gather.SEMS,)),
             dma((Gather.SEMS,)),
@@ -945,7 +1007,7 @@
             dma((4, TpSpread.SEMS)),
             dma((4,)),
             dma((2, 4)),
-            dma((6,)),
+            dma((10,)),
         ],
         compiler_params=pltpu.CompilerParams(
             collective_id=0, has_side_effects=True, vmem_limit_bytes=63 * 2**20
@@ -963,90 +1025,105 @@
 
 def update_kernel(*refs):
     block_in, input_in = refs[:2]
-    old = [refs[2 + 3 * at : 5 + 3 * at] for at in range(4)]
-    small_old = refs[14:20]
-    io_grad, gud_grad, small = refs[20:23]
+    old = [refs[2 + 3 * at : 5 + 3 * at] for at in range(6)]
+    io_grad, gud_grad, small_grad = refs[20:23]
     block_out, input_out = refs[23:25]
-    new = [refs[25 + 3 * at : 28 + 3 * at] for at in range(4)]
-    small_new = refs[37:43]
-    block_held, input_held, wide_held = refs[43:46]
-    held = [refs[46 + 3 * at : 49 + 3 * at] for at in range(4)]
-    in_sems, out_sems = refs[58:]
+    new = [refs[25 + 3 * at : 28 + 3 * at] for at in range(6)]
+    block_held, input_held, wide_held, io_held, gud_held, small_held = refs[43:49]
+    held = [refs[49 + 3 * at : 52 + 3 * at] for at in range(6)]
+    in_sems, out_sems = refs[67:]
 
     def moved(source, target, sems, at):
         copy = pltpu.make_async_copy(source, target, sems.at[at])
         copy.start()
         return copy
 
-    order = (2, 3, 0, 1)
+    order = (2, 3, 0, 1, 4, 5)
+    input_load = moved(input_in, input_held, in_sems, 18)
+    gud_load = moved(gud_grad, gud_held, in_sems, 19)
     loads = {}
-    input_load = moved(input_in, input_held, in_sems, 12)
-    block_load = moved(block_in, block_held, in_sems, 13)
     for matrix in order:
         loads[matrix] = [
             moved(old[matrix][at], held[matrix][at], in_sems, 3 * matrix + at) for at in range(3)
         ]
+        if matrix == 2:
+            io_load = moved(io_grad, io_held, in_sems, 20)
+            small_load = moved(small_grad, small_held, in_sems, 21)
+    block_load = moved(block_in, block_held, in_sems, 22)
     stores = []
     input_load.wait()
     for half in range(2):
         rows = pl.ds(half * SLOT_ROWS, SLOT_ROWS)
         wide_held[rows, :] = input_held[rows, :].astype(jnp.float32)
-        stores.append(moved(wide_held.at[rows], input_out.at[rows], out_sems, 12 + half))
-    block_load.wait()
-    stores.append(moved(block_held, block_out, out_sems, 14))
+        stores.append(moved(wide_held.at[rows], input_out.at[rows], out_sems, 18 + half))
     for matrix in order:
         for copy in loads[matrix]:
             copy.wait()
         weight, moment, average = held[matrix]
+        every, rate = slice(None), matrix_rate
         if matrix == 0:
-            parts = [(at, io_grad[:, at * CHANNELS : (at + 1) * CHANNELS]) for at in range(3)]
+            io_load.wait()
+            parts = [(at, io_held[at]) for at in range(3)]
         elif matrix == 1:
-            parts = [(slice(None), io_grad[:, 3 * CHANNELS :])]
+            parts = [(every, io_held[3])]
         elif matrix == 2:
-            parts = [(at, gud_grad[at, :, :HIDDEN]) for at in range(2)]
+            gud_load.wait()
+            parts = [(at, gud_held[at]) for at in range(2)]
+        elif matrix == 3:
+            parts = [(every, gud_held[2])]
+        elif matrix == 4:
+            small_load.wait()
+            rate = small_rate
+            parts = [
+                (
+                    (slice(row, row + 1), slice(at * CHANNELS, (at + 1) * CHANNELS)),
+                    small_held[4 * row + at : 4 * row + at + 1, :],
+                )
+                for row in range(2)
+                for at in range(4)
+            ]
         else:
-            parts = [(slice(None), gud_grad[2, :, :HIDDEN])]
+            parts, rate = [(every, small_held[8:11, :])], small_rate
         for at, gradient in parts:
             moment[at], weight[at], average[at] = nesterov(
-                weight[at], moment[at], average[at], gradient, matrix_rate
+                weight[at], moment[at], average[at], gradient, rate
             )
         for at, source in enumerate((moment, weight, average)):
             stores.append(moved(source, new[matrix][at], out_sems, 3 * matrix + at))
-    for group, rows, columns in ((0, slice(0, 2), slice(None)), (3, slice(2, 5), slice(0, CHANNELS))):
-        weight, moment, average = small_old[group : group + 3]
-        results = nesterov(weight[...], moment[...], average[...], small[rows, columns], small_rate)
-        for at in range(3):
-            small_new[group + at][...] = results[at]
+    block_load.wait()
+    stores.append(moved(block_held, block_out, out_sems, 20))
     for copy in stores:
         copy.wait()
 
 
-def update(block, input_low, matrices, smalls, io_grad, gud_grad, small):
-    vmem = pl.BlockSpec(memory_space=pltpu.VMEM)
+def update(block, input_low, arrays, io_grad, gud_grad, small):
     hbm = pl.BlockSpec(memory_space=pl.ANY)
     f32 = jnp.float32
     like = lambda a: jax.ShapeDtypeStruct(a.shape, a.dtype)
+    held = lambda a: pltpu.VMEM(a.shape, a.dtype)
     return pl.pallas_call(
         update_kernel,
         out_shape=(
             like(block),
             jax.ShapeDtypeStruct((ROWS, WIDTH), f32),
-            *[like(a) for a in matrices],
-            *[like(a) for a in smalls],
+            *[like(a) for a in arrays],
         ),
-        in_specs=[hbm] * 14 + [vmem] * 9,
-        out_specs=(hbm,) * 14 + (vmem,) * 6,
+        in_specs=[hbm] * 23,
+        out_specs=(hbm,) * 20,
         scratch_shapes=[
-            pltpu.VMEM((ROWS, WIDTH), jnp.bfloat16),
-            pltpu.VMEM((ROWS, WIDTH), jnp.bfloat16),
+            held(block),
+            held(input_low),
             pltpu.VMEM((ROWS, WIDTH), f32),
-            *[pltpu.VMEM(a.shape, f32) for a in matrices],
-            pltpu.SemaphoreType.DMA((14,)),
-            pltpu.SemaphoreType.DMA((15,)),
+            held(io_grad),
+            held(gud_grad),
+            held(small),
+            *[held(a) for a in arrays],
+            pltpu.SemaphoreType.DMA((23,)),
+            pltpu.SemaphoreType.DMA((21,)),
         ],
         compiler_params=pltpu.CompilerParams(vmem_limit_bytes=62 * 2**20),
         name="update",
-    )(block, input_low, *matrices, *smalls, io_grad, gud_grad, small)
+    )(block, input_low, *arrays, io_grad, gud_grad, small)
 
 
 def on_device(
@@ -1095,8 +1172,7 @@
     block_output, input_grad, *new = update(
         block_output,
         input_low_grad,
-        [a for group in matrices for a in group],
-        smalls,
+        [a for group in matrices for a in group] + list(smalls),
         io_sum,
         gud_sum,
         small,

time: 172 us -> 164 us (0.953)
  Pallas kernels: 171 us -> 162 us
    pallas_call x1, Pallas kernels: 163 us -> 155 us  [step(): pl.pallas_call(kernel, out_shape=(jax.ShapeDtypeStruct((ROWS, WIDTH), b16...]
where the time goes in v5:
time: 164 us; the launch traced here: 163 us
  Pallas kernels  162 us (99%)
    pallas_call x1, Pallas kernels, step(): pl.pallas_call(kernel, out_shape=(jax.ShapeDtypeStruct((ROWS, WIDTH), b16...  155 us
    pallas_call x1, Pallas kernels, update(): pl.pallas_call(update_kernel, out_shape=(like(block), jax.ShapeDtypeStruc...  7.58 us

profile of v5, /device:TPU:0, one launch (start us, length us, event | category | flops | bytes accessed | tf_op | source)
XLA Modules:
  0.0 163.2 jit_solution(7827664220367738119)
XLA Ops:
  0.7 154.8 %step.1 = (bf16[512,1536]{1,0:T(8,128)(2,1)}, bf16[512,1536]{1,0:T(8,128)(2,1)}, bf16[3,16,48,1792]{3,2,1,0:T(8,128)(2,1)}, bf16[3,12,48,1792]{3,2,1,0:T(8,128)(...) custom-call(bf16[512,1536]{1,0:T(8,128)(2,1)} %bitcast.16, bf16[512,1536]{1,0:T(8,128)(2,1)} %bitcast.17, ...), custom_call_target="tpu_custom_call" | custom-call | tf_op jit(solution)/shard_map/step/pallas_call | solution.py:952
  155.5 7.6 %update.1 = (bf16[512,1536]{1,0:T(8,128)(2,1)}, f32[512,1536]{1,0:T(8,128)}, f32[3,48,384]{2,1,0:T(8,128)}, f32[3,48,384]{2,1,0:T(8,128)}, f32[3,48,384]{2,1,0:T...) custom-call(bf16[512,1536]{1,0:T(8,128)(2,1)} %get-tuple-element.45., ...), custom_call_target="tpu_custom_call" | custom-call | tf_op jit(solution)/shard_map/update/pallas_call | solution.py:1104

commit v6 on v5

--- a/solution.py
+++ b/solution.py
@@ -30,15 +30,16 @@
 
 
 class Place:
-    def __init__(self):
+    def __init__(self, flip=False):
         self.shard = lax.axis_index("shard")
         self.ctx = lax.axis_index("ctx")
         self.tp = lax.axis_index("tp")
         self.y = self.shard * 2 + lax.div(self.ctx, 8)
         self.z = lax.rem(lax.div(self.ctx, 2), 4)
         self.core = lax.rem(self.ctx, 2)
-        self.first = self.y * (1 - self.core) + self.z * self.core
-        self.second = self.z * (1 - self.core) + self.y * self.core
+        self.way = 1 - self.core if flip else self.core
+        self.first = self.y * (1 - self.way) + self.z * self.way
+        self.second = self.z * (1 - self.way) + self.y * self.way
 
     def turn(self, value, by):
         return lax.rem(value + by + 4, 4)
@@ -47,13 +48,13 @@
         return (lax.div(y, 2), lax.rem(y, 2) * 8 + z * 2 + core, self.tp)
 
     def grid_device(self, first, second):
-        y = first * (1 - self.core) + second * self.core
-        z = second * (1 - self.core) + first * self.core
+        y = first * (1 - self.way) + second * self.way
+        z = second * (1 - self.way) + first * self.way
         return self.device(y, z, self.core)
 
     def block(self, first, second):
-        y = first * (1 - self.core) + second * self.core
-        z = second * (1 - self.core) + first * self.core
+        y = first * (1 - self.way) + second * self.way
+        z = second * (1 - self.way) + first * self.way
         return y * 8 + z * 2 + self.core
 
     def along_first(self, by):
@@ -170,6 +171,36 @@
 
     def drain(self):
         self.arrived(31, 0)
+
+
+class Both:
+    def __init__(self, *parts):
+        self.parts = parts
+
+    def each(self, name, *given):
+        for part in self.parts:
+            getattr(part, name)(*given)
+
+    def start(self):
+        self.each("start")
+
+    def first(self):
+        self.each("first")
+
+    def first_far(self):
+        self.each("first_far")
+
+    def second(self, back):
+        self.each("second", back)
+
+    def second_far(self, back):
+        self.each("second_far", back)
+
+    def finish(self):
+        self.each("finish")
+
+    def drain(self):
+        self.each("drain")
 
 
 class Scatter:
@@ -528,25 +559,30 @@
     for copy in (*loads, x_copy, low_copy, own_copy):
         copy.start()
     friends = place.greet()
-    for copy in loads:
+    for copy in loads[:2]:
         copy.wait()
     for member in range(4):
         io_local[:, member * CHANNELS : (member + 1) * CHANNELS] = io_wide[member].astype(b16)
-        if member < 3:
-            gud_local[member, :, :HIDDEN] = gud_wide[member].astype(b16)
-    gud_local[:, :, HIDDEN:] = jnp.zeros((3, BLOCK, PADDED - HIDDEN), b16)
     io[mine] = io_local[...]
-    weights[:, mine] = gud_local[...]
     pl.semaphore_wait(pltpu.get_barrier_semaphore(), friends)
-    early, late = pl.ds(0, EARLY * TILE), pl.ds(EARLY * TILE, PADDED - EARLY * TILE)
+    other_place = Place(flip=True)
     two = pl.ds(0, 2)
     io_gather = Gather(place, io_local, io, io_sems)
     down_gather = Gather(place, gud_local.at[2], weights.at[2], down_sems)
-    early_gather = Gather(
-        place, gud_local.at[two, :, early], weights.at[two, :, :, early], early_sems
-    )
-    late_gather = Gather(
-        place, gud_local.at[two, :, late], weights.at[two, :, :, late], late_sems
+
+    def columns_gather(way, start, width, sems):
+        columns = pl.ds(start, width)
+        return Gather(
+            way, gud_local.at[two, :, columns], weights.at[two, :, :, columns], sems
+        )
+
+    early_gather = Both(
+        columns_gather(place, 0, 512, early_sems.at[0]),
+        columns_gather(other_place, 512, 512, early_sems.at[1]),
+    )
+    late_gather = Both(
+        columns_gather(place, 1024, 256, late_sems.at[0]),
+        columns_gather(other_place, 1280, 512, late_sems.at[1]),
     )
     mixed = TpSum(place, send_a, relays.at[0], finals.at[0], sum_sems.at[0])
     second = TpSum(place, send_b, relays.at[1], finals.at[1], sum_sems.at[1])
@@ -606,8 +642,11 @@
             ).start()
 
     def project(member):
-        columns = slice(member * CHANNELS, (member + 1) * CHANNELS)
-        projected[member] = dot(input_low[...], flat_io[:, columns])
+        if member == 0:
+            columns = slice(0, 3 * CHANNELS)
+            whole = dot(input_low[...], flat_io[:, columns])
+            for at in range(3):
+                projected[at] = whole[:, at * CHANNELS : (at + 1) * CHANNELS]
 
     def give_mixed(slot):
         mixed.give(dot_t(gated[...], flat_io[slot_rows(slot), 3 * CHANNELS :]), slot)
@@ -618,16 +657,20 @@
 
     def gate_up(at):
         columns = pl.ds(at * TILE, TILE)
-        gate = dot(second_low[0:ROWS, :], flat_weights[0, :, columns])
-        up = dot(second_low[0:ROWS, :], flat_weights[1, :, columns])
-        grad_inner = big[0:ROWS, columns].astype(f32)
-        sigmoid = 0.5 * jnp.tanh(0.5 * gate) + 0.5
-        active = gate * sigmoid
-        big[0:ROWS, columns] = (active * up).astype(b16)
-        big[ROWS : 2 * ROWS, columns] = (
-            grad_inner * up * (sigmoid + active * (1.0 - sigmoid))
-        ).astype(b16)
-        big[2 * ROWS :, columns] = (grad_inner * active).astype(b16)
+        parts = [slice(0, SLOT_ROWS), slice(SLOT_ROWS, ROWS)]
+        gates = [dot(second_low[rows, :], flat_weights[0, :, columns]) for rows in parts]
+        ups = [dot(second_low[rows, :], flat_weights[1, :, columns]) for rows in parts]
+        for half, rows in enumerate(parts):
+            gate, up = gates[half], ups[half]
+            grad_inner = big[rows, columns].astype(f32)
+            sigmoid = 0.5 * jnp.tanh(0.5 * gate) + 0.5
+            active = gate * sigmoid
+            big[rows, columns] = (active * up).astype(b16)
+            start = ROWS + rows.start
+            big[start : start + SLOT_ROWS, columns] = (
+                grad_inner * up * (sigmoid + active * (1.0 - sigmoid))
+            ).astype(b16)
+            big[start + ROWS : start + ROWS + SLOT_ROWS, columns] = (grad_inner * active).astype(b16)
 
     def give_second(slot):
         rows = slot_rows(slot)
@@ -675,35 +718,50 @@
         small[0:rows, :] = total
 
     io_gather.start()
-    down_gather.start()
-    io_gather.first()
-    io_gather.first_far()
     x_copy.wait()
 
     @pl.loop(0, ROWS, step=64)
     def _(at):
         input_low[pl.ds(at, 64), :] = normed_low(send_b[pl.ds(at, 64), :])
 
+    for copy in loads[2:]:
+        copy.wait()
+    for member in range(3):
+        gud_local[member, :, :HIDDEN] = gud_wide[member].astype(b16)
+    gud_local[:, :, HIDDEN:] = jnp.zeros((3, BLOCK, PADDED - HIDDEN), b16)
+    weights[:, mine] = gud_local[...]
+    down_gather.start()
+    io_gather.first()
+    send_edges()
+    io_gather.first_far()
+    io_gather.second(0)
     io_gather.second(1)
+    low_copy.wait()
+    positions = place.ctx * SLOT_ROWS + lax.broadcasted_iota(jnp.int32, (SLOT_ROWS, 1), 0)
+    for slot in range(2):
+        rows = slice(slot * SLOT_ROWS, (slot + 1) * SLOT_ROWS)
+        kept = jnp.where(positions < lengths[slot], 1.0, 0.0)
+        grad_low[rows, :] = (grad_low[rows, :].astype(f32) * kept).astype(b16)
     io_gather.second(3)
-    io_gather.second(0)
-    io_gather.second(2)
-    io_gather.second_far(1)
-    send_edges()
-    down_gather.first()
-    io_gather.second_far(0)
-    early_gather.start()
-    io_gather.second_far(3)
-    io_gather.second_far(2)
     wait_bytes(edges, edge_sems.at[1])
     wait_bytes(edges, edge_sems.at[0])
     for side in range(2):
         rows = pl.ds(ROWS + side * 2 * EDGE, 2 * EDGE)
         input_low[rows, :] = normed_low(edges[side].reshape(2 * EDGE, WIDTH))
+    turned(grad_low, turn_a)
+    io_gather.second(2)
+    io_gather.second_far(0)
+    down_gather.first()
+    early_gather.start()
+    io_gather.second_far(1)
+    down_gather.second(0)
+    io_gather.second_far(3)
+    late_gather.start()
+    io_gather.second_far(2)
     io_gather.finish()
+    project(0)
     project(1)
     project(2)
-    project(0)
     product[:, 8:, :] = (projected[0, :ROWS] * projected[2, :ROWS]).reshape(
         2, SLOT_ROWS, CHANNELS
     )
@@ -720,88 +778,81 @@
 
     give_mixed(0)
     give_mixed(1)
+    give_mixed(2)
     down_gather.first_far()
+    mixed.relay(1)
+    down_gather.second_far(0)
     down_gather.second(1)
-    down_gather.second(0)
+    down_gather.second(3)
+    late_gather.first()
+    mixed.relay(0)
+    late_gather.second(0)
+    mixed.relay(2)
+    down_gather.second(2)
     early_gather.first()
-    give_mixed(2)
-    down_gather.second(2)
-    mixed.relay(0)
-    down_gather.second_far(0)
-    early_gather.first_far()
-    down_gather.second(3)
-    mixed.relay(1)
-    mixed.relay(2)
-    late_gather.start()
+    down_gather.second_far(1)
     own_copy.wait()
     stream = x_own[...].astype(f32) + mixed.take()
     residual[...] = stream
     normed, _ = norm_of(stream)
     second_low[own_rows, :] = (normed * gains[1:2, :]).astype(b16)
     second_spread.start()
+    down_gather.second_far(3)
+    down_gather.second_far(2)
+    late_gather.first_far()
+    late_gather.second(3)
+    late_gather.second(1)
+    down_gather.finish()
+    pl.loop(3, 5)(inner_grad)
+    early_gather.second(3)
+    pl.loop(5, 7)(inner_grad)
+    late_gather.second_far(0)
+    second_spread.relay()
+    early_gather.first_far()
+    late_gather.second(2)
+    late_gather.second_far(3)
+    pl.loop(0, 3)(inner_grad)
+    late_gather.second_far(1)
     early_gather.second(0)
     early_gather.second(1)
-    early_gather.second(3)
     early_gather.second(2)
-    low_copy.wait()
-    positions = place.ctx * SLOT_ROWS + lax.broadcasted_iota(jnp.int32, (SLOT_ROWS, 1), 0)
-    for slot in range(2):
-        rows = slice(slot * SLOT_ROWS, (slot + 1) * SLOT_ROWS)
-        kept = jnp.where(positions < lengths[slot], 1.0, 0.0)
-        grad_low[rows, :] = (grad_low[rows, :].astype(f32) * kept).astype(b16)
-    down_gather.second_far(3)
-    down_gather.second_far(2)
-    down_gather.second_far(1)
-    late_gather.first()
-    second_spread.relay()
-    down_gather.finish()
-    late_gather.first_far()
-    pl.loop(0, 3)(inner_grad)
-    pl.loop(5, 7)(inner_grad)
+    late_gather.second_far(2)
+    early_gather.second_far(3)
     early_gather.second_far(0)
-    late_gather.second(1)
-    early_gather.second_far(1)
-    early_gather.second_far(3)
-    early_gather.second_far(2)
-    late_gather.second(3)
-    late_gather.second(0)
-    pl.loop(3, 5)(inner_grad)
-    early_gather.finish()
-    late_gather.second(2)
     second_spread.finish()
-    gate_up(2)
-    late_gather.second_far(1)
-    gate_up(1)
-    late_gather.second_far(3)
-    gate_up(0)
-    late_gather.second_far(0)
-    late_gather.second_far(2)
-    gate_up(3)
     late_gather.finish()
     gate_up(4)
+    early_gather.second_far(1)
+    gate_up(6)
+    early_gather.second_far(2)
     gate_up(5)
-    gate_up(6)
+    early_gather.finish()
+    gate_up(3)
+    gate_up(1)
+    gate_up(2)
+    gate_up(0)
     mixed.drain()
     give_branch(0)
     for part in (io_gather, down_gather, early_gather, late_gather, second_spread):
         part.drain()
     give_second(0)
+    turned(second_low, turn_b)
     give_second(1)
     give_second(2)
-    turned(second_low, turn_b)
     gradient(turn_b, 1, 2, 0, 4)
     up_piece.to_sibling(0, 4 * TILE)
     gradient(turn_b, 1, 2, 4, 7)
     up_piece.to_sibling(4 * TILE, 3 * TILE)
+    second.relay(1)
     second.relay(0)
-    second.relay(1)
     gradient(turn_b, 0, 1, 0, 4)
     gate_piece.to_sibling(0, 4 * TILE)
     second.relay(2)
-    turned(grad_low, turn_a)
     give_branch(1)
+    give_branch(2)
     up_piece.second_start()
-    branch.relay(0)
+    gradient(turn_b, 0, 1, 4, 7)
+    gate_piece.to_sibling(4 * TILE, 3 * TILE)
     normed, inverse = norm_of(residual[...])
     grad_second = second.take()
     small[...] = jnp.zeros_like(small)
@@ -829,18 +880,18 @@
                 place.along_ctx(-1, tp),
             ).start()
 
-    gradient(turn_b, 0, 1, 4, 7)
-    gate_piece.to_sibling(4 * TILE, 3 * TILE)
-    gate_piece.second_start()
-    low_spread.relay()
-    up_piece.second_relay()
-    give_branch(2)
-    branch.relay(1)
     gradient(turn_a, 2, 0, 0, 4)
     down_piece.to_sibling(0, 4 * TILE)
+    gate_piece.second_start()
     gradient(turn_a, 2, 0, 4, 7)
     down_piece.to_sibling(4 * TILE, 3 * TILE)
-    gate_piece.second_relay()
+    low_spread.relay()
+    turned(input_low, turn_a)
+    branch.relay(0)
+    up_piece.second_relay()
+    branch.relay(2)
+    branch.relay(1)
+    down_piece.second_start()
     low_spread.finish()
     wait_bytes(edge_recv, edge_sems.at[3])
 
@@ -866,7 +917,6 @@
     after = (grad_gated[ROWS:] * projected[1, ROWS + 2 * EDGE :]).reshape(2, EDGE, CHANNELS)
     conv_grad[:, SLOT_ROWS:, :] = jnp.where(place.ctx < 15, after[:, :8, :], 0.0)
     grad_proj[:, CHANNELS : 2 * CHANNELS] = (grad_gated[:ROWS] * convolved[...]).astype(b16)
-    branch.relay(2)
     grad_product = (
         taps[2:3, :] * conv_grad[:, 0:SLOT_ROWS, :]
         + taps[1:2, :] * conv_grad[:, 1 : 1 + SLOT_ROWS, :]
@@ -876,29 +926,30 @@
     grad_proj[:, 2 * CHANNELS :] = (grad_product * projected[0, :ROWS]).astype(b16)
     second.drain()
     give_first(0)
+    gate_piece.second_relay()
     give_first(1)
-    give_first(2)
-    down_piece.second_start()
-    turned(second_low, turn_b)
-    block_own[...] = (residual[...] + branch.take()).astype(b16)
-    block_keep.start()
     for tap in range(3):
         small[8 + tap : 9 + tap, :] = jnp.sum(
             conv_grad[:, :SLOT_ROWS, :] * product[:, 6 + tap : 6 + tap + SLOT_ROWS, :], axis=(0, 1)
         ).reshape(1, CHANNELS)
+    up_piece.first_start()
+    block_own[...] = (residual[...] + branch.take()).astype(b16)
+    block_keep.start()
+    give_first(2)
     first.relay(1)
-    turned(input_low, turn_a)
+    down_piece.second_relay()
+    turned(second_low, turn_b)
     first.relay(0)
-    gate_piece.first_start()
     first.relay(2)
+    block_spread.start()
     big[:, : 2 * CHANNELS] = dot(turn_a[...], grad_proj[:, : 2 * CHANNELS]).astype(b16)
     io_piece.to_sibling(0, 2 * CHANNELS)
-    block_spread.start()
-    down_piece.second_relay()
     big[:, 2 * CHANNELS : 3 * CHANNELS] = dot(turn_a[...], grad_proj[:, 2 * CHANNELS :]).astype(b16)
     big[:, 3 * CHANNELS : 4 * CHANNELS] = dot(turn_b[...], gated[...]).astype(b16)
     io_piece.to_sibling(2 * CHANNELS, 2 * CHANNELS)
-    gate_piece.first_relay()
+    up_piece.first_relay()
+    io_piece.second_start()
+    up_piece.finish()
     normed, inverse = norm_of(x_own[...].astype(f32))
     grad_first = first.take()
     keep_gain(0, grad_first * normed)
@@ -907,30 +958,28 @@
     ).astype(b16)
     input_keep.start()
     exchange(0, 0, [place.along_tp(by) for by in (1, 2, 3)], 8)
+    block_spread.relay()
     input_spread.start()
-    io_piece.second_start()
     io_piece.second_relay()
     added(0, 0, 3, 8)
     exchange(1, 3, [place.sibling()])
+    gate_piece.first_start()
     down_piece.first_start()
+    gate_piece.first_relay()
+    block_spread.finish()
     added(1, 3, 1)
     exchange(2, 4, [place.along_first(by) for by in (1, 2, 3)])
-    up_piece.first_start()
-    input_spread.relay()
-    block_spread.relay()
     io_piece.first_start()
     down_piece.first_relay()
+    input_spread.relay()
     added(2, 4, 3)
     exchange(3, 7, [place.along_second(by) for by in (1, 2, 3)])
-    up_piece.first_relay()
     io_piece.first_relay()
+    added(3, 7, 3)
+    down_piece.finish()
+    gate_piece.finish()
+    io_piece.finish()
     input_spread.finish()
-    added(3, 7, 3)
-    up_piece.finish()
-    gate_piece.finish()
-    down_piece.finish()
-    io_piece.finish()
-    block_spread.finish()
     block_keep.wait()
     input_keep.wait()
     for part in (low_spread, block_spread, input_spread, first, branch):
@@ -1000,8 +1049,8 @@
             pltpu.VMEM((10, 16, CHANNELS), f32),
             dma((Gather.SEMS,)),
             dma((Gather.SEMS,)),
-            dma((Gather.SEMS,)),
-            dma((Gather.SEMS,)),
+            dma((2, Gather.SEMS)),
+            dma((2, Gather.SEMS)),
             dma((4, Scatter.SEMS)),
             dma((4, TpSum.SEMS)),
             dma((4, TpSpread.SEMS)),

time: 164 us -> 163 us (level)
  no operation moved by 1% of the time
where the time goes in v6:
time: 163 us
  Pallas kernels  162 us (99%)
    pallas_call x1, Pallas kernels, step(): pl.pallas_call(kernel, out_shape=(jax.ShapeDtypeStruct((ROWS, WIDTH), b16...  154 us
    pallas_call x1, Pallas kernels, update(): pl.pallas_call(update_kernel, out_shape=(like(block), jax.ShapeDtypeStruc...  7.58 us

profile of v6, /device:TPU:0, one launch (start us, length us, event | category | flops | bytes accessed | tf_op | source)
XLA Modules:
  0.0 162.6 jit_solution(702649245080620165)
XLA Ops:
  0.7 154.2 %step.1 = (bf16[512,1536]{1,0:T(8,128)(2,1)}, bf16[512,1536]{1,0:T(8,128)(2,1)}, bf16[3,16,48,1792]{3,2,1,0:T(8,128)(2,1)}, bf16[3,12,48,1792]{3,2,1,0:T(8,128)(...) custom-call(bf16[512,1536]{1,0:T(8,128)(2,1)} %bitcast.16, bf16[512,1536]{1,0:T(8,128)(2,1)} %bitcast.17, ...), custom_call_target="tpu_custom_call" | custom-call | tf_op jit(solution)/shard_map/step/pallas_call | solution.py:1001
  154.8 7.6 %update.1 = (bf16[512,1536]{1,0:T(8,128)(2,1)}, f32[512,1536]{1,0:T(8,128)}, f32[3,48,384]{2,1,0:T(8,128)}, f32[3,48,384]{2,1,0:T(8,128)}, f32[3,48,384]{2,1,0:T...) custom-call(bf16[512,1536]{1,0:T(8,128)(2,1)} %get-tuple-element.45., ...), custom_call_target="tpu_custom_call" | custom-call | tf_op jit(solution)/shard_map/update/pallas_call | solution.py:1153

commit v7 on v6

--- a/solution.py
+++ b/solution.py
@@ -102,8 +102,9 @@
 class Gather:
     SEMS = 12
 
-    def __init__(self, place, local, whole, sems):
+    def __init__(self, place, local, whole, sems, joint=None):
         self.place, self.local, self.whole, self.sems = place, local, whole, sems
+        self.joint = joint
         self.half = local.shape[-1] // 2
 
     def part(self, block, half=None):
@@ -117,8 +118,10 @@
         remote(source, target, self.sems.at[0], self.sems.at[at], device).start()
 
     def arrived(self, blocks, at):
+        spot = self.whole if self.joint is None else self.joint
         few = pl.ds(0, blocks)
-        wait_bytes(self.whole.at[:, few] if self.whole.ndim == 4 else self.whole.at[few], self.sems.at[at])
+        if spot is not False:
+            wait_bytes(spot.at[:, few] if spot.ndim == 4 else spot.at[few], self.sems.at[at])
 
     def block(self, back, by):
         p = self.place
@@ -570,20 +573,17 @@
     io_gather = Gather(place, io_local, io, io_sems)
     down_gather = Gather(place, gud_local.at[2], weights.at[2], down_sems)
 
-    def columns_gather(way, start, width, sems):
-        columns = pl.ds(start, width)
-        return Gather(
-            way, gud_local.at[two, :, columns], weights.at[two, :, :, columns], sems
-        )
-
-    early_gather = Both(
-        columns_gather(place, 0, 512, early_sems.at[0]),
-        columns_gather(other_place, 512, 512, early_sems.at[1]),
-    )
-    late_gather = Both(
-        columns_gather(place, 1024, 256, late_sems.at[0]),
-        columns_gather(other_place, 1280, 512, late_sems.at[1]),
-    )
+    def columns_pair(start, widths, sems):
+        joint, parts = weights.at[two, :, :, pl.ds(start, sum(widths))], []
+        for way, width in zip((place, other_place), widths):
+            columns = pl.ds(start, width)
+            local, whole = gud_local.at[two, :, columns], weights.at[two, :, :, columns]
+            parts.append(Gather(way, local, whole, sems, False if parts else joint))
+            start += width
+        return Both(*parts)
+
+    early_gather = columns_pair(0, (512, 512), early_sems)
+    late_gather = columns_pair(1024, (256, 512), late_sems)
     mixed = TpSum(place, send_a, relays.at[0], finals.at[0], sum_sems.at[0])
     second = TpSum(place, send_b, relays.at[1], finals.at[1], sum_sems.at[1])
     branch = TpSum(place, send_a, relays.at[0], finals.at[0], sum_sems.at[2])
@@ -1049,8 +1049,8 @@
             pltpu.VMEM((10, 16, CHANNELS), f32),
             dma((Gather.SEMS,)),
             dma((Gather.SEMS,)),
-            dma((2, Gather.SEMS)),
-            dma((2, Gather.SEMS)),
+            dma((Gather.SEMS,)),
+            dma((Gather.SEMS,)),
             dma((4, Scatter.SEMS)),
             dma((4, TpSum.SEMS)),
             dma((4, TpSpread.SEMS)),
@@ -1088,7 +1088,13 @@
         return copy
 
     order = (2, 3, 0, 1, 4, 5)
-    input_load = moved(input_in, input_held, in_sems, 18)
+    quarters = [pl.ds(at * QUARTER, QUARTER) for at in range(4)]
+    input_loads = [
+        moved(input_in.at[rows], input_held.at[rows], in_sems, (18, 22, 23, 24)[at])
+        for at, rows in enumerate(quarters)
+    ]
+    block_load = moved(block_in, block_held, in_sems, 25)
+    stores = []
     gud_load = moved(gud_grad, gud_held, in_sems, 19)
     loads = {}
     for matrix in order:
@@ -1098,13 +1104,12 @@
         if matrix == 2:
             io_load = moved(io_grad, io_held, in_sems, 20)
             small_load = moved(small_grad, small_held, in_sems, 21)
-    block_load = moved(block_in, block_held, in_sems, 22)
-    stores = []
-    input_load.wait()
-    for half in range(2):
-        rows = pl.ds(half * SLOT_ROWS, SLOT_ROWS)
+    for at, rows in enumerate(quarters):
+        input_loads[at].wait()
         wide_held[rows, :] = input_held[rows, :].astype(jnp.float32)
-        stores.append(moved(wide_held.at[rows], input_out.at[rows], out_sems, 18 + half))
+        stores.append(moved(wide_held.at[rows], input_out.at[rows], out_sems, (18, 19, 21, 22)[at]))
+    block_load.wait()
+    stores.append(moved(block_held, block_out, out_sems, 20))
     for matrix in order:
         for copy in loads[matrix]:
             copy.wait()
@@ -1139,8 +1144,6 @@
             )
         for at, source in enumerate((moment, weight, average)):
             stores.append(moved(source, new[matrix][at], out_sems, 3 * matrix + at))
-    block_load.wait()
-    stores.append(moved(block_held, block_out, out_sems, 20))
     for copy in stores:
         copy.wait()
 
@@ -1167,8 +1170,8 @@
             held(gud_grad),
             held(small),
             *[held(a) for a in arrays],
+            pltpu.SemaphoreType.DMA((26,)),
             pltpu.SemaphoreType.DMA((23,)),
-            pltpu.SemaphoreType.DMA((21,)),
         ],
         compiler_params=pltpu.CompilerParams(vmem_limit_bytes=62 * 2**20),
         name="update",

time: 163 us -> 162 us (level)
  no operation moved by 1% of the time
where the time goes in v7:
time: 162 us
  Pallas kernels  161 us (99%)
    pallas_call x1, Pallas kernels, step(): pl.pallas_call(kernel, out_shape=(jax.ShapeDtypeStruct((ROWS, WIDTH), b16...  154 us
    pallas_call x1, Pallas kernels, update(): pl.pallas_call(update_kernel, out_shape=(like(block), jax.ShapeDtypeStruc...  7.05 us

profile of v7, /device:TPU:0, one launch (start us, length us, event | category | flops | bytes accessed | tf_op | source)
XLA Modules:
  0.0 162.0 jit_solution(17390721593202965982)
XLA Ops:
  0.7 154.1 %step.1 = (bf16[512,1536]{1,0:T(8,128)(2,1)}, bf16[512,1536]{1,0:T(8,128)(2,1)}, bf16[3,16,48,1792]{3,2,1,0:T(8,128)(2,1)}, bf16[3,12,48,1792]{3,2,1,0:T(8,128)(...) custom-call(bf16[512,1536]{1,0:T(8,128)(2,1)} %bitcast.16, bf16[512,1536]{1,0:T(8,128)(2,1)} %bitcast.17, ...), custom_call_target="tpu_custom_call" | custom-call | tf_op jit(solution)/shard_map/step/pallas_call | solution.py:1001
  154.8 7.1 %update.1 = (bf16[512,1536]{1,0:T(8,128)(2,1)}, f32[512,1536]{1,0:T(8,128)}, f32[3,48,384]{2,1,0:T(8,128)}, f32[3,48,384]{2,1,0:T(8,128)}, f32[3,48,384]{2,1,0:T...) custom-call(bf16[512,1536]{1,0:T(8,128)(2,1)} %get-tuple-element.45., ...), custom_call_target="tpu_custom_call" | custom-call | tf_op jit(solution)/shard_map/update/pallas_call | solution.py:1156
